TPU v7x, 32 devices: a whole 2x2x4 slice. The times are simulated.
32 devices in a mesh: dp: 32 (over z, y, x, core).
Axes of the slice: x: 2, y: 2, z: 4, core: 2. Of those that a mesh axis runs over, the one named last changes fastest.
Arguments:
- history: bfloat16 [9, 8192, 2048], P(None, 'dp'), may hold values from -6 to 6
- d_out: bfloat16 [8192, 2048], P('dp'), may hold values from -6 to 6
- group_ids: int32 [32], P('dp'), may hold values from 0 to 7
- group_weight: float32 [8], replicated, may hold values from 0.5 to 2
- attn_in: float32 [2048, 6144], P('dp'), may hold values from -0.22097087 to 0.22097087
- attn_out: float32 [2048, 2048], P('dp'), may hold values from -0.8838835 to 0.8838835
- ffn_up: float32 [2048, 8192], P('dp'), may hold values from -0.22097087 to 0.22097087
- ffn_down: float32 [8192, 2048], P('dp'), may hold values from -0.110485435 to 0.110485435
- mixer_in: float32 [2048, 36], P('dp'), may hold values from -0.22097087 to 0.22097087
- mixer_out: float32 [36, 36], replicated, may hold values from -1 to 1
- norm_gain: float32 [3, 2048], P(None, 'dp'), may hold values from 0.5 to 1.5
- norm_bias: float32 [2, 2048], P(None, 'dp'), may hold values from -1.5 to 1.5
- first_attn_in: float32 [2048, 6144], P('dp'), may hold values from -1.9086836 to 1.9086836
- second_attn_in: float32 [2048, 6144], P('dp'), may hold values from 0.022235554 to 0.088942215
- first_attn_out: float32 [2048, 2048], P('dp'), may hold values from -1.9086836 to 1.9086836
- second_attn_out: float32 [2048, 2048], P('dp'), may hold values from 0.022235554 to 0.088942215
- first_ffn_up: float32 [2048, 8192], P('dp'), may hold values from -1.9086836 to 1.9086836
- second_ffn_up: float32 [2048, 8192], P('dp'), may hold values from 0.022235554 to 0.088942215
- first_ffn_down: float32 [8192, 2048], P('dp'), may hold values from -1.9086836 to 1.9086836
- second_ffn_down: float32 [8192, 2048], P('dp'), may hold values from 0.022235554 to 0.088942215
- first_mixer_in: float32 [2048, 36], P('dp'), may hold values from -86.37716 to 86.37716
- second_mixer_in: float32 [2048, 36], P('dp'), may hold values from 45.538414 to 182.15366
- first_mixer_out: float32 [36, 36], replicated, may hold values from -40 to 40
- second_mixer_out: float32 [36, 36], replicated, may hold values from 45.538414 to 182.15366
- first_norm_gain: float32 [3, 2048], P(None, 'dp'), may hold values from -1.75 to 1.75
- second_norm_gain: float32 [3, 2048], P(None, 'dp'), may hold values from 0.088942215 to 0.35576886
- first_norm_bias: float32 [2, 2048], P(None, 'dp'), may hold values from -1.75 to 1.75
- second_norm_bias: float32 [2, 2048], P(None, 'dp'), may hold values from 0.088942215 to 0.35576886
Outputs:
- out_state: bfloat16 [8192, 2048], P('dp')
- grad_history: bfloat16 [9, 8192, 2048], P(None, 'dp')
- global_norm: float32 [], replicated
- lamb_stats: float32 [6, 3], replicated
- next_attn_in: float32 [2048, 6144], P('dp')
- copy_attn_in: bfloat16 [2048, 6144], P('dp')
- next_first_attn_in: float32 [2048, 6144], P('dp')
- next_second_attn_in: float32 [2048, 6144], P('dp')
- next_attn_out: float32 [2048, 2048], P('dp')
- copy_attn_out: bfloat16 [2048, 2048], P('dp')
- next_first_attn_out: float32 [2048, 2048], P('dp')
- next_second_attn_out: float32 [2048, 2048], P('dp')
- next_ffn_up: float32 [2048, 8192], P('dp')
- copy_ffn_up: bfloat16 [2048, 8192], P('dp')
- next_first_ffn_up: float32 [2048, 8192], P('dp')
- next_second_ffn_up: float32 [2048, 8192], P('dp')
- next_ffn_down: float32 [8192, 2048], P('dp')
- copy_ffn_down: bfloat16 [8192, 2048], P('dp')
- next_first_ffn_down: float32 [8192, 2048], P('dp')
- next_second_ffn_down: float32 [8192, 2048], P('dp')
- next_mixer_in: float32 [2048, 36], P('dp')
- copy_mixer_in: bfloat16 [2048, 36], P('dp')
- next_first_mixer_in: float32 [2048, 36], P('dp')
- next_second_mixer_in: float32 [2048, 36], P('dp')
- next_mixer_out: float32 [36, 36], replicated
- copy_mixer_out: bfloat16 [36, 36], replicated
- next_first_mixer_out: float32 [36, 36], replicated
- next_second_mixer_out: float32 [36, 36], replicated
- next_norm_gain: float32 [3, 2048], P(None, 'dp')
- copy_norm_gain: bfloat16 [3, 2048], P(None, 'dp')
- next_first_norm_gain: float32 [3, 2048], P(None, 'dp')
- next_second_norm_gain: float32 [3, 2048], P(None, 'dp')
- next_norm_bias: float32 [2, 2048], P(None, 'dp')
- copy_norm_bias: bfloat16 [2, 2048], P(None, 'dp')
- next_first_norm_bias: float32 [2, 2048], P(None, 'dp')
- next_second_norm_bias: float32 [2, 2048], P(None, 'dp')
All inputs are finite; a program needn't handle non-finite values.
Results may differ from a plain program's by a relative error of at most 0.019.
The roundings to bfloat16 on the way count: a program that leaves them out, or rounds other values in their place, can miss the bound.
Values may be sent and summed in bfloat16 or wider, within the bound.
No kernel may reach another device: no remote copies, remote signals or barrier semaphores. Data moves between devices by JAX's collectives and lax.ppermute only.
A program may use at most 512 MiB of HBM per device.

v0:
```python
import math

import jax
import jax.numpy as jnp
from jax import lax
from jax.sharding import PartitionSpec as P

HD = 128
ROT = 32
PARAMS = 50416912


EPS_NORM = 1e-05
EPS_ADAM = 1e-06
DECAY_WEIGHT = 0.01
RATE_MATRIX = 0.3
RATE_VECTOR = 0.25
BETA = 0.5
NEGATIVE = -1e30


def layer_norm(values):
    centre = jnp.mean(values, axis=-1, keepdims=True)
    centred = values - centre
    spread = jnp.mean(centred * centred, axis=-1, keepdims=True)
    return centred * lax.rsqrt(spread + EPS_NORM)


def scaled_norm(values, gain_row):
    return layer_norm(values) * gain_row


def shifted_norm(values, gain_row, shift_row):
    return layer_norm(values) * gain_row + shift_row


def rotate(values, cosine, sine_table, turn_sign):
    half_width = cosine.shape[-1]
    first_half = values[..., :half_width]
    second = values[..., half_width : 2 * half_width]
    return jnp.concatenate(
        [
            first_half * cosine - turn_sign * second * sine_table,
            second * cosine + turn_sign * first_half * sine_table,
            values[..., 2 * half_width :],
        ],
        axis=-1,
    )


def phases(seq_len):
    half_width = ROT // 2
    frequency = 10000.0 ** (-(2.0 * jnp.arange(half_width, dtype=jnp.float32)) / ROT)
    phase_grid = jnp.arange(seq_len, dtype=jnp.float32)[:, None] * frequency[None, :]
    return (jnp.cos(phase_grid)[:, None, :], jnp.sin(phase_grid)[:, None, :])


def gelu_exact(values):
    return jax.nn.gelu(values, approximate=False)


def mix_history(coef, history):
    total_mix = jnp.zeros((coef.shape[1],) + history.shape[1:], jnp.float32)
    for member in range(history.shape[0]):
        total_mix = (
            total_mix
            + jnp.transpose(coef[:, :, member])[:, :, None]
            * history[member].astype(jnp.float32)[None]
        )
    return total_mix


def block_scores(query_rows, key_rot, offset, block_rows):
    seq_len = key_rot.shape[0]
    scale = 1.0 / math.sqrt(key_rot.shape[2])
    scores = (
        jnp.einsum("qhd,khd->hqk", query_rows, key_rot, preferred_element_type=jnp.float32) * scale
    )
    allowed = (offset + jnp.arange(block_rows))[:, None] >= jnp.arange(seq_len)[None, :]
    return jnp.where(allowed[None], scores, NEGATIVE)


def attention_forward(query_rot, key_rot, value, block_rows):
    seq_len = query_rot.shape[0]
    block_count = seq_len // block_rows

    def one_block(offset):
        scores = block_scores(query_rot, key_rot, offset, block_rows)
        row_max = jnp.max(scores, axis=-1, keepdims=True)
        exponent = jnp.exp(scores - row_max)
        row_total = jnp.sum(exponent, axis=-1, keepdims=True)
        probability = (exponent / row_total).astype(jnp.bfloat16)
        block_out = jnp.einsum(
            "hqk,khd->qhd", probability, value, preferred_element_type=jnp.float32
        )
        return (block_out, row_max + jnp.log(row_total))

    outputs, logsum = lax.map(one_block, jnp.arange(block_count) * block_rows)
    return (outputs.reshape(seq_len, -1), logsum)


def attention_backward(query_rot, key_rot, value, logsum, grad_heads, block_rows):
    seq_len = query_rot.shape[0]
    block_count = seq_len // block_rows
    scale = 1.0 / math.sqrt(key_rot.shape[2])

    def one_block(running, inputs):
        grad_keys, grad_values = running
        offset, block_logsum = inputs
        scores = block_scores(query_rot, key_rot, offset, block_rows)
        probability = jnp.exp(scores - block_logsum)
        grad_probs = jnp.einsum(
            "qhd,khd->hqk", grad_heads, value, preferred_element_type=jnp.float32
        )
        centre = jnp.sum(probability * grad_probs, axis=-1, keepdims=True)
        grad_scores = (probability * (grad_probs - centre)).astype(jnp.bfloat16)
        grad_query_rows = (
            jnp.einsum("hqk,khd->qhd", grad_scores, key_rot, preferred_element_type=jnp.float32)
            * scale
        )
        grad_keys = (
            grad_keys
            + jnp.einsum("hqk,qhd->khd", grad_scores, query_rot, preferred_element_type=jnp.float32)
            * scale
        )
        grad_values = grad_values + jnp.einsum(
            "hqk,qhd->khd",
            probability.astype(jnp.bfloat16),
            grad_heads,
            preferred_element_type=jnp.float32,
        )
        return ((grad_keys, grad_values), grad_query_rows)

    initial = jnp.zeros(key_rot.shape, jnp.float32)
    (grad_keys, grad_values), grad_query = lax.scan(
        one_block, (initial, initial), (jnp.arange(block_count) * block_rows, logsum)
    )
    return (grad_query.reshape(key_rot.shape), grad_keys, grad_values)


def local(
    history,
    d_out,
    group_ids,
    group_weight,
    attn_in,
    attn_out,
    ffn_up,
    ffn_down,
    mixer_in,
    mixer_out,
    norm_gain,
    norm_bias,
    first_attn_in,
    second_attn_in,
    first_attn_out,
    second_attn_out,
    first_ffn_up,
    second_ffn_up,
    first_ffn_down,
    second_ffn_down,
    first_mixer_in,
    second_mixer_in,
    first_mixer_out,
    second_mixer_out,
    first_norm_gain,
    second_norm_gain,
    first_norm_bias,
    second_norm_bias,
):
    low_shards = (
        attn_in.astype(jnp.bfloat16),
        attn_out.astype(jnp.bfloat16),
        ffn_up.astype(jnp.bfloat16),
        ffn_down.astype(jnp.bfloat16),
        mixer_in.astype(jnp.bfloat16),
        norm_gain.astype(jnp.bfloat16),
        norm_bias.astype(jnp.bfloat16),
    )
    gathered = (
        lax.all_gather(low_shards[0], "dp", axis=0, tiled=True),
        lax.all_gather(low_shards[1], "dp", axis=0, tiled=True),
        lax.all_gather(low_shards[2], "dp", axis=0, tiled=True),
        lax.all_gather(low_shards[3], "dp", axis=0, tiled=True),
        lax.all_gather(low_shards[4], "dp", axis=0, tiled=True),
        lax.all_gather(low_shards[5], "dp", axis=1, tiled=True),
        lax.all_gather(low_shards[6], "dp", axis=1, tiled=True),
    )
    w_attn_in, w_attn_out, w_ffn_up, w_ffn_down, w_mixer_in, gain_low, bias_low = gathered
    mixer_low = mixer_out.astype(jnp.bfloat16)
    gain_table = gain_low.astype(jnp.float32)
    bias_table = bias_low.astype(jnp.float32)
    hist_len, seq_len, width = history.shape
    heads = width // HD
    block_rows = min(seq_len, 512)
    current = history[hist_len - 1].astype(jnp.float32)
    mix_normed = scaled_norm(current, gain_table[0]).astype(jnp.bfloat16)
    mix_pre = jnp.dot(mix_normed, w_mixer_in, preferred_element_type=jnp.float32)
    mix_hidden = gelu_exact(mix_pre).astype(jnp.bfloat16)
    coef = jnp.dot(mix_hidden, mixer_low, preferred_element_type=jnp.float32).reshape(
        seq_len, -1, hist_len
    )
    streams = mix_history(coef, history)
    normed = shifted_norm(streams[:3], gain_table[1], bias_table[0]).astype(jnp.bfloat16)
    projected = jnp.einsum(
        "asd,dae->ase",
        normed,
        w_attn_in.reshape(width, 3, width),
        preferred_element_type=jnp.float32,
    )
    cosine, sine_table = phases(seq_len)
    query_rot = rotate(projected[0].reshape(seq_len, heads, HD), cosine, sine_table, 1.0).astype(
        jnp.bfloat16
    )
    key_rot = rotate(projected[1].reshape(seq_len, heads, HD), cosine, sine_table, 1.0).astype(
        jnp.bfloat16
    )
    value = projected[2].reshape(seq_len, heads, HD).astype(jnp.bfloat16)
    attended, logsum = attention_forward(query_rot, key_rot, value, block_rows)
    attended = attended.astype(jnp.bfloat16)
    residual = streams[3] + jnp.dot(attended, w_attn_out, preferred_element_type=jnp.float32)
    ffn_normed = shifted_norm(residual, gain_table[2], bias_table[1]).astype(jnp.bfloat16)
    up_proj = jnp.dot(ffn_normed, w_ffn_up, preferred_element_type=jnp.float32)
    activated = gelu_exact(up_proj).astype(jnp.bfloat16)
    out_state = (
        residual + jnp.dot(activated, w_ffn_down, preferred_element_type=jnp.float32)
    ).astype(jnp.bfloat16)
    regathered = (
        lax.all_gather(low_shards[0], "dp", axis=0, tiled=True),
        lax.all_gather(low_shards[1], "dp", axis=0, tiled=True),
        lax.all_gather(low_shards[2], "dp", axis=0, tiled=True),
        lax.all_gather(low_shards[3], "dp", axis=0, tiled=True),
        lax.all_gather(low_shards[4], "dp", axis=0, tiled=True),
        lax.all_gather(low_shards[5], "dp", axis=1, tiled=True),
        lax.all_gather(low_shards[6], "dp", axis=1, tiled=True),
    )
    w_attn_in, w_attn_out, w_ffn_up, w_ffn_down, w_mixer_in, gain_low, bias_low = regathered
    gain_table = gain_low.astype(jnp.float32)
    bias_table = bias_low.astype(jnp.float32)
    group_count = group_weight.shape[0]
    seq_weight = jnp.sum(
        jnp.where(jnp.arange(group_count, dtype=jnp.int32) == group_ids[0], group_weight, 0.0)
    )
    grad_out = (d_out.astype(jnp.float32) * seq_weight).astype(jnp.bfloat16)
    grad_ffn_down = jnp.einsum("sf,sd->fd", activated, grad_out, preferred_element_type=jnp.float32)
    grad_activated = jnp.einsum(
        "sd,fd->sf", grad_out, w_ffn_down, preferred_element_type=jnp.float32
    )
    _, gelu_back = jax.vjp(gelu_exact, up_proj)
    grad_up = gelu_back(grad_activated)[0].astype(jnp.bfloat16)
    grad_ffn_up = jnp.einsum("sd,sf->df", ffn_normed, grad_up, preferred_element_type=jnp.float32)
    grad_ffn_normed = jnp.einsum("sf,df->sd", grad_up, w_ffn_up, preferred_element_type=jnp.float32)
    _, ffn_norm_back = jax.vjp(shifted_norm, residual, gain_table[2], bias_table[1])
    grad_ffn_x, grad_gain_ffn, grad_bias_ffn = ffn_norm_back(grad_ffn_normed)
    grad_residual = (grad_out.astype(jnp.float32) + grad_ffn_x).astype(jnp.bfloat16)
    grad_attn_out = jnp.einsum(
        "sd,se->de", attended, grad_residual, preferred_element_type=jnp.float32
    )
    grad_attended = jnp.einsum(
        "se,de->sd", grad_residual, w_attn_out, preferred_element_type=jnp.float32
    ).astype(jnp.bfloat16)
    grad_query_rot, grad_key_rot, grad_value = attention_backward(
        query_rot, key_rot, value, logsum, grad_attended.reshape(seq_len, heads, HD), block_rows
    )
    grad_query = rotate(grad_query_rot, cosine, sine_table, -1.0).astype(jnp.bfloat16)
    grad_key = rotate(grad_key_rot, cosine, sine_table, -1.0).astype(jnp.bfloat16)
    grad_proj = jnp.stack(
        [
            grad_query.reshape(seq_len, width),
            grad_key.reshape(seq_len, width),
            grad_value.astype(jnp.bfloat16).reshape(seq_len, width),
        ]
    )
    grad_attn_in = jnp.einsum(
        "asd,ase->dae", normed, grad_proj, preferred_element_type=jnp.float32
    ).reshape(width, 3 * width)
    grad_normed = jnp.einsum(
        "ase,dae->asd",
        grad_proj,
        w_attn_in.reshape(width, 3, width),
        preferred_element_type=jnp.float32,
    )
    _, attn_norm_back = jax.vjp(shifted_norm, streams[:3], gain_table[1], bias_table[0])
    grad_streams, grad_gain_attn, grad_bias_attn = attn_norm_back(grad_normed)
    grad_mixed = jnp.concatenate([grad_streams, grad_residual.astype(jnp.float32)[None]], axis=0)
    coef_columns = []
    hist_grads = []
    for member in range(hist_len):
        history_rows = history[member].astype(jnp.float32)
        coef_columns.append(jnp.sum(grad_mixed * history_rows[None], axis=-1))
        hist_grads.append(
            jnp.sum(jnp.transpose(coef[:, :, member])[:, :, None] * grad_mixed, axis=0)
        )
    grad_coef = (
        jnp.transpose(jnp.stack(coef_columns, axis=-1), (1, 0, 2))
        .reshape(seq_len, -1)
        .astype(jnp.bfloat16)
    )
    grad_mixer_out = jnp.einsum(
        "sh,sc->hc", mix_hidden, grad_coef, preferred_element_type=jnp.float32
    )
    grad_mix_hidden = jnp.einsum(
        "sc,hc->sh", grad_coef, mixer_low, preferred_element_type=jnp.float32
    )
    _, mix_gelu_back = jax.vjp(gelu_exact, mix_pre)
    grad_mix_pre = mix_gelu_back(grad_mix_hidden)[0].astype(jnp.bfloat16)
    grad_mixer_in = jnp.einsum(
        "sd,sh->dh", mix_normed, grad_mix_pre, preferred_element_type=jnp.float32
    )
    grad_mix_normed = jnp.einsum(
        "sh,dh->sd", grad_mix_pre, w_mixer_in, preferred_element_type=jnp.float32
    )
    _, mix_norm_back = jax.vjp(scaled_norm, current, gain_table[0])
    grad_current, grad_gain_mix = mix_norm_back(grad_mix_normed)
    hist_grads[hist_len - 1] = hist_grads[hist_len - 1] + grad_current
    grad_history = jnp.stack(hist_grads).astype(jnp.bfloat16)
    shard_grads = (
        lax.psum_scatter(grad_attn_in, "dp", scatter_dimension=0, tiled=True),
        lax.psum_scatter(grad_attn_out, "dp", scatter_dimension=0, tiled=True),
        lax.psum_scatter(grad_ffn_up, "dp", scatter_dimension=0, tiled=True),
        lax.psum_scatter(grad_ffn_down, "dp", scatter_dimension=0, tiled=True),
        lax.psum_scatter(grad_mixer_in, "dp", scatter_dimension=0, tiled=True),
        lax.psum_scatter(
            jnp.stack([grad_gain_mix, grad_gain_attn, grad_gain_ffn]),
            "dp",
            scatter_dimension=1,
            tiled=True,
        ),
        lax.psum_scatter(
            jnp.stack([grad_bias_attn, grad_bias_ffn]), "dp", scatter_dimension=1, tiled=True
        ),
    )
    mixer_grad = lax.psum(grad_mixer_out, "dp")
    grads = (
        shard_grads[0],
        shard_grads[1],
        shard_grads[2],
        shard_grads[3],
        shard_grads[4],
        mixer_grad,
        shard_grads[5],
        shard_grads[6],
    )
    weights = (attn_in, attn_out, ffn_up, ffn_down, mixer_in, mixer_out, norm_gain, norm_bias)
    firsts = (
        first_attn_in,
        first_attn_out,
        first_ffn_up,
        first_ffn_down,
        first_mixer_in,
        first_mixer_out,
        first_norm_gain,
        first_norm_bias,
    )
    seconds = (
        second_attn_in,
        second_attn_out,
        second_ffn_up,
        second_ffn_down,
        second_mixer_in,
        second_mixer_out,
        second_norm_gain,
        second_norm_bias,
    )
    devices = lax.axis_size("dp")

    def portion(member, amount):
        return amount / devices if member == 5 else amount

    local_squares = sum(
        (portion(member, jnp.sum(grads[member] * grads[member])) for member in range(8))
    )
    local_weight_sq = jnp.stack(
        [portion(member, jnp.sum(weights[member] * weights[member])) for member in range(6)]
    )
    squares, weight_sq = lax.psum((local_squares, local_weight_sq), "dp")
    global_norm = jnp.sqrt(squares)
    clip = 0.3 * math.sqrt(PARAMS) / (global_norm + 1e-06)
    pending = []
    local_update_sq = []
    for member in range(8):
        scaled = grads[member] * clip
        first_new = BETA * firsts[member] + (1.0 - BETA) * scaled
        second_new = BETA * seconds[member] + (1.0 - BETA) * scaled * scaled
        step_value = first_new / (jnp.sqrt(second_new) + EPS_ADAM)
        if member < 6:
            step_value = step_value + DECAY_WEIGHT * weights[member]
            local_update_sq.append(portion(member, jnp.sum(step_value * step_value)))
        pending.append((first_new, second_new, step_value))
    update_sq = lax.psum(jnp.stack(local_update_sq), "dp")
    weight_norm = jnp.sqrt(weight_sq)
    update_norm = jnp.sqrt(update_sq)
    trust = weight_norm / (update_norm + 1e-06)
    lamb_stats = jnp.stack([weight_norm, update_norm, trust], axis=1)
    results = []
    for member in range(8):
        first_new, second_new, step_value = pending[member]
        if member < 6:
            updated = weights[member] - RATE_MATRIX * trust[member] * step_value
        else:
            updated = weights[member] - RATE_VECTOR * step_value
        results.append((updated, updated.astype(jnp.bfloat16), first_new, second_new))
    return (
        out_state,
        grad_history,
        global_norm,
        lamb_stats,
        results[0][0],
        results[0][1],
        results[0][2],
        results[0][3],
        results[1][0],
        results[1][1],
        results[1][2],
        results[1][3],
        results[2][0],
        results[2][1],
        results[2][2],
        results[2][3],
        results[3][0],
        results[3][1],
        results[3][2],
        results[3][3],
        results[4][0],
        results[4][1],
        results[4][2],
        results[4][3],
        results[5][0],
        results[5][1],
        results[5][2],
        results[5][3],
        results[6][0],
        results[6][1],
        results[6][2],
        results[6][3],
        results[7][0],
        results[7][1],
        results[7][2],
        results[7][3],
    )


def solution(mesh):
    placed = (
        P(None, "dp", None),
        P("dp", None),
        P("dp"),
        P(),
        P("dp", None),
        P("dp", None),
        P("dp", None),
        P("dp", None),
        P("dp", None),
        P(),
        P(None, "dp"),
        P(None, "dp"),
        P("dp", None),
        P("dp", None),
        P("dp", None),
        P("dp", None),
        P("dp", None),
        P("dp", None),
        P("dp", None),
        P("dp", None),
        P("dp", None),
        P("dp", None),
        P(),
        P(),
        P(None, "dp"),
        P(None, "dp"),
        P(None, "dp"),
        P(None, "dp"),
    )
    return jax.shard_map(
        local,
        mesh=mesh,
        in_specs=placed,
        out_specs=(
            P("dp", None),
            P(None, "dp", None),
            P(),
            P(),
            P("dp", None),
            P("dp", None),
            P("dp", None),
            P("dp", None),
            P("dp", None),
            P("dp", None),
            P("dp", None),
            P("dp", None),
            P("dp", None),
            P("dp", None),
            P("dp", None),
            P("dp", None),
            P("dp", None),
            P("dp", None),
            P("dp", None),
            P("dp", None),
            P("dp", None),
            P("dp", None),
            P("dp", None),
            P("dp", None),
            P(),
            P(),
            P(),
            P(),
            P(None, "dp"),
            P(None, "dp"),
            P(None, "dp"),
            P(None, "dp"),
            P(None, "dp"),
            P(None, "dp"),
            P(None, "dp"),
            P(None, "dp"),
        ),
        check_vma=False,
    )
```

profile of v0, /device:TPU:0, one launch (start us, length us, event | category | flops | bytes accessed | tf_op | source)
XLA Modules:
  0.0 3390.4 jit_solution(6495081831972836644)
XLA Ops:
  16.4 43.4 %all-gather.2 = bf16[32,64,2]{1,2,0:T(2,128)(2,1)S(1)} all-gather(bf16[1,64,2]{1,2,0:T(2,128)(2,1)S(1)} %convert_bitcast_fusion.3), channel_id=1, replica_groups=mesh['dp'=32] {'dp'}, dimensions={0}, use_global_device_ids=true | all-gather | bytes 8448 | tf_op jit(solution)/shard_map/all_gather | solution.py:187
  59.9 36.8 %all-gather = bf16[32,64,3]{1,2,0:T(4,128)(2,1)S(1)} all-gather(bf16[1,64,3]{1,2,0:T(4,128)(2,1)S(1)} %convert_bitcast_fusion.2), channel_id=1, replica_groups=mesh['dp'=32] {'dp'}, dimensions={0}, use_global_device_ids=true | all-gather | bytes 12672 | tf_op jit(solution)/shard_map/all_gather | solution.py:186
  96.8 40.9 %all-gather.1 = bf16[32,64,36]{1,2,0:T(8,128)(2,1)S(1)} all-gather(bf16[1,64,36]{1,2,0:T(8,128)(2,1)S(1)} %convert_bitcast_fusion.1), channel_id=1, replica_groups=mesh['dp'=32] {'dp'}, dimensions={0}, use_global_device_ids=true | all-gather | bytes 152064 | tf_op jit(solution)/shard_map/all_gather | solution.py:185
  172.3 32.9 copy.183
  258.7 189.8 %all-gather.12.cloned.1.call-done = bf16[2048,8192]{1,0:T(8,128)(2,1)} async-done(((bf16[64,8192]{1,0:T(8,128)(2,1)}), bf16[2048,8192]{1,0:T(8,128)(2,1)}) %all-gather.12.cloned.1.call-update) | async-done | bytes 33554448 | tf_op jit(solution)/shard_map/all_gather | solution.py:183
  448.5 17.9 fusion.59
  466.4 178.3 %all-gather.14.cloned.1.call-done = bf16[8192,2048]{1,0:T(8,128)(2,1)} async-done(((bf16[256,2048]{1,0:T(8,128)(2,1)}), bf16[8192,2048]{1,0:T(8,128)(2,1)}) %all-gather.14.cloned.1.call-update) | async-done | bytes 33554448 | tf_op jit(solution)/shard_map/all_gather | solution.py:184
  644.7 33.4 add_convert_fusion
  678.1 18.0 multiply_reduce_fusion.26
  775.8 19.8 multiply_reduce_fusion.1
  817.3 22.7 fusion.20
  840.1 48.9 %copy.211 = f32[2048,6144]{1,0:T(8,128)} copy(f32[2048,6144]{0,1:T(8,128)} %bitcast.242) | data formatting | bytes 100663296 | tf_op jit(solution)/shard_map/reshape | solution.py:276
  890.6 25.6 fusion.58
  917.4 34.6 %fusion.28 = f32[8192,2048]{1,0:T(8,128)} fusion(bf16[256,2048]{1,0:T(8,128)(2,1)S(1)} %copy-done.75, f32[]{:T(128)} %fusion.53, f32[256,8192]{1,0:T(8,128)} %fusion.59), kind=kOutput, calls=%fused_computation.149 | convolution fusion | flops 8727822336 | bytes 76546048 | tf_op jit(solution)/shard_map/sf,sd->fd/dot_general | solution.py:245
  952.9 38.8 %psum.28 = f32[36,36]{1,0:T(8,128)S(1)} all-reduce(f32[36,36]{1,0:T(8,128)S(1)} %fusion.89), channel_id=1, replica_groups=mesh['dp'=32] {'dp'}, use_global_device_ids=true, to_apply=%region_44.45 | all-reduce | flops 1296 | bytes 10368 | tf_op jit(solution)/shard_map/psum | solution.py:333
  1005.4 31.1 fusion.8
  1038.2 25.7 reduce-scatter.24.cloned.1.call-done
  1065.4 132.1 %reduce-scatter.22.cloned.1.call-done = f32[64,36]{1,0:T(8,128)} async-done(((f32[2048,36]{1,0:T(8,128)}), f32[64,36]{1,0:T(8,128)}) %reduce-scatter.22.cloned.1.call-update) | async-done | bytes 9232
  1198.9 179.8 %reduce-scatter.16.cloned.1.call-done = f32[64,2048]{1,0:T(8,128)} async-done(((f32[2048,2048]{1,0:T(8,128)}), f32[64,2048]{1,0:T(8,128)}) %reduce-scatter.16.cloned.1.call-update) | async-done | bytes 524304 | tf_op jit(solution)/shard_map/reduce_scatter | solution.py:319
  1380.5 438.9 %reduce-scatter.14.cloned.1.call-done = f32[64,6144]{1,0:T(8,128)} async-done(((f32[2048,6144]{1,0:T(8,128)}), f32[64,6144]{1,0:T(8,128)}) %reduce-scatter.14.cloned.1.call-update) | async-done | bytes 1572880 | tf_op jit(solution)/shard_map/reduce_scatter | solution.py:318
  1823.3 700.1 %reduce-scatter.18.cloned.1.call-done = f32[64,8192]{1,0:T(8,128)} async-done(((f32[2048,8192]{1,0:T(8,128)}), f32[64,8192]{1,0:T(8,128)}) %reduce-scatter.18.cloned.1.call-update) | async-done | bytes 2097168 | tf_op jit(solution)/shard_map/reduce_scatter | solution.py:320
  2526.8 709.3 %reduce-scatter.20.cloned.1.call-done = f32[256,2048]{1,0:T(8,128)} async-done(((f32[8192,2048]{1,0:T(8,128)}), f32[256,2048]{1,0:T(8,128)}) %reduce-scatter.20.cloned.1.call-update) | async-done | bytes 2097168 | tf_op jit(solution)/shard_map/reduce_scatter | solution.py:321
  3241.5 47.2 %psum.29 = f32[]{:T(128)} all-reduce(f32[]{:T(128)S(6)} %add.322), channel_id=1, replica_groups=mesh['dp'=32] {'dp'}, use_global_device_ids=true, to_apply=%region_55.56 | all-reduce | flops 1 | bytes 8 | tf_op jit(solution)/shard_map/psum | solution.py:376
  3321.3 39.8 %all-reduce = (f32[6]{0:T(128)S(1)}, f32[6]{0:T(128)S(1)}) all-reduce(f32[6]{0:T(128)S(1)} %stack.191, f32[6]{0:T(128)S(1)} %stack.183), channel_id=1, replica_groups=mesh['dp'=32] {'dp'}, use_global_device_ids=true, to_apply=%region_69.70 | all-reduce | flops 12 | bytes 96 | tf_op jit(solution)/shard_map/psum | solution.py:390
  (488 shorter events, 274.9 us)
Async XLA Ops:
  7.3 165.1 %all-gather.8.cloned.1.call-start = ((), (), s32[]{:S(2)}) async-start(), calls=%async_computation.7 | async-start | bytes 25952256 | tf_op jit(solution)/shard_map/all_gather | solution.py:181
  9.8 241.8 %all-gather.10.cloned.1.call-start = ((), (), s32[]{:S(2)}) async-start(), calls=%async_computation.8 | async-start | bytes 8650752 | tf_op jit(solution)/shard_map/all_gather | solution.py:182
  11.7 436.8 %all-gather.12.cloned.1.call-start = ((), (), s32[]{:S(2)}) async-start(), calls=%async_computation.9 | async-start | bytes 34603008 | tf_op jit(solution)/shard_map/all_gather | solution.py:183
  14.4 630.3 %all-gather.14.cloned.1.call-start = ((), (), s32[]{:S(2)}) async-start(), calls=%async_computation.10 | async-start | bytes 34603008 | tf_op jit(solution)/shard_map/all_gather | solution.py:184
  15.6 1021.0 %reduce-scatter.26.cloned.1.call-start = ((), (), s32[]{:S(2)}) async-start(), calls=%async_computation.17 | async-start | bytes 1081344
  141.3 554.9 %copy-start.78 = (f32[1,2048]{1,0:T(1,128)}, f32[1,2048]{1,0:T(1,128)S(1)}, u32[]{:S(2)}) copy-start(f32[1,2048]{1,0:T(1,128)S(1)} %get-tuple-element.202) | copy-start | bytes 24580
  258.3 437.8 %copy-start.4 = (f32[256,2048]{1,0:T(8,128)}, f32[256,2048]{1,0:T(8,128)S(1)}, u32[]{:S(2)}) copy-start(f32[256,2048]{1,0:T(8,128)S(1)} %get-tuple-element.223) | copy-start | bytes 6291460
  258.3 437.8 %copy-start.99 = (f32[256]{0:T(256)}, f32[256]{0:T(256)S(1)}, u32[]{:S(2)}) copy-start(f32[256]{0:T(256)S(1)} %broadcast_multiply_fusion.2) | copy-start | bytes 3076
  258.7 437.5 %copy-start.109 = (f32[256]{0:T(256)}, f32[256]{0:T(256)S(1)}, u32[]{:S(2)}) copy-start(f32[256]{0:T(256)S(1)} %fusion.52) | copy-start | bytes 3076
  797.2 266.8 %reduce-scatter.24.cloned.1.call-start = ((), (), s32[]{:S(2)}) async-start(), calls=%async_computation.16 | async-start | bytes 1081344
  804.8 392.7 %reduce-scatter.22.cloned.1.call-start = ((), (), s32[]{:S(2)}) async-start(), calls=%async_computation.15 | async-start | bytes 1081344
  806.3 572.4 %reduce-scatter.16.cloned.1.call-start = ((), (), s32[]{:S(2)}) async-start(), calls=%async_computation.12 | async-start | bytes 17301504 | tf_op jit(solution)/shard_map/reduce_scatter | solution.py:319
  815.8 1003.6 %reduce-scatter.14.cloned.1.call-start = ((), (), s32[]{:S(2)}) async-start(), calls=%async_computation.11 | async-start | bytes 51904512 | tf_op jit(solution)/shard_map/reduce_scatter | solution.py:318
  889.0 1634.4 %reduce-scatter.18.cloned.1.call-start = ((), (), s32[]{:S(2)}) async-start(), calls=%async_computation.13 | async-start | bytes 69206016 | tf_op jit(solution)/shard_map/reduce_scatter | solution.py:320
  916.2 2319.9 %reduce-scatter.20.cloned.1.call-start = ((), (), s32[]{:S(2)}) async-start(), calls=%async_computation.14 | async-start | bytes 69206016 | tf_op jit(solution)/shard_map/reduce_scatter | solution.py:321
  1036.5 2204.9 %copy-start.147 = (f32[256]{0:T(256)S(1)}, f32[256]{0:T(256)}, u32[]{:S(2)}) copy-start(f32[256]{0:T(256)} %get-tuple-element.84) | copy-start | bytes 3076
  1036.5 2252.9 %copy-start.92 = (f32[36,36]{1,0:T(8,128)S(1)}, f32[36,36]{1,0:T(8,128)}, u32[]{:S(2)}) copy-start(f32[36,36]{1,0:T(8,128)} %param.37) | copy-start | bytes 15556
  1036.5 2252.9 %copy-start.134 = (f32[36,36]{1,0:T(8,128)S(1)}, f32[36,36]{1,0:T(8,128)}, u32[]{:S(2)}) copy-start(f32[36,36]{1,0:T(8,128)} %param.51) | copy-start | bytes 15556
  1036.5 2252.9 %copy-start.135 = (f32[36,36]{1,0:T(8,128)S(1)}, f32[36,36]{1,0:T(8,128)}, u32[]{:S(2)}) copy-start(f32[36,36]{1,0:T(8,128)} %param.50) | copy-start | bytes 15556
  1036.5 2254.9 %copy-start.94 = (f32[64,36]{0,1:T(8,128)S(1)}, f32[64,36]{0,1:T(8,128)}, u32[]{:S(2)}) copy-start(f32[64,36]{0,1:T(8,128)} %param.36) | copy-start | bytes 27652
  1036.5 2254.9 %copy-start.136 = (f32[64,36]{0,1:T(8,128)S(1)}, f32[64,36]{0,1:T(8,128)}, u32[]{:S(2)}) copy-start(f32[64,36]{0,1:T(8,128)} %param.49) | copy-start | bytes 27652
  1036.6 2254.9 %copy-start.137 = (f32[64,36]{0,1:T(8,128)S(1)}, f32[64,36]{0,1:T(8,128)}, u32[]{:S(2)}) copy-start(f32[64,36]{0,1:T(8,128)} %param.48) | copy-start | bytes 27652
  1036.6 2259.1 %copy-start.29 = (f32[64,6144]{1,0:T(8,128)S(1)}, f32[64,6144]{1,0:T(8,128)}, u32[]{:S(2)}) copy-start(f32[64,6144]{1,0:T(8,128)} %param.32) | copy-start | bytes 4718596
  1819.4 1476.3 %copy-start.50 = (f32[64,6144]{1,0:T(8,128)S(1)}, f32[64,6144]{1,0:T(8,128)}, u32[]{:S(2)}) copy-start(f32[64,6144]{1,0:T(8,128)} %reduce-scatter.14.cloned.1.call-done) | copy-start | bytes 4718596
  (144 other events, 2841.3 us)
Sparse Core Ops, SparseCore 0:
  11.5 160.7 all-gather.7
  175.8 75.8 all-gather.9
  255.1 193.3 all-gather.11
  451.8 192.9 all-gather.13
  797.3 132.9 reduce-scatter.25
  933.0 130.8 reduce-scatter.23
  1066.7 130.7 reduce-scatter.21
  1199.9 178.7 reduce-scatter.15
  1386.3 433.1 reduce-scatter.13
  1821.8 701.5 reduce-scatter.17
  2525.9 710.1 reduce-scatter.19
where the time goes:
time: 3400 us; the launch traced here: 3390 us
  waiting for transfers between devices  2580 us (76%)
  matrix products  255 us (8%)
  blocking collectives  247 us (7%)
  local copies, waits for them, and re-layouts  149 us (4%)
  other arithmetic  132 us (4%)
    reduce_scatter x1, waiting for transfers between devices, local(): lax.psum_scatter(grad_ffn_down, 'dp', scatter_dimension=0, tiled=True)  709 us
    reduce_scatter x1, waiting for transfers between devices, local(): lax.psum_scatter(grad_ffn_up, 'dp', scatter_dimension=0, tiled=True)  700 us
    reduce_scatter x1, waiting for transfers between devices, local(): lax.psum_scatter(grad_attn_in, 'dp', scatter_dimension=0, tiled=True)  439 us
    all_gather x1, waiting for transfers between devices, local(): lax.all_gather(low_shards[2], 'dp', axis=0, tiled=True)  190 us
    reduce_scatter x1, waiting for transfers between devices, local(): lax.psum_scatter(grad_attn_out, 'dp', scatter_dimension=0, tiled=True)  180 us
    all_gather x1, waiting for transfers between devices, local(): lax.all_gather(low_shards[3], 'dp', axis=0, tiled=True)  178 us
    unnamed x14, waiting for transfers between devices  158 us
  transfers between devices with their start and end apart: 11, of which 10 were waited for; matrix products, arithmetic and copies ran while one was open for 9% of the time, Pallas kernels for 0%

commit v1 on v0

v1 whole, which is shorter than its diff:
```python
import functools
import math

import jax
import jax.numpy as jnp
from jax import lax
from jax.experimental import pallas as pl
from jax.experimental.pallas import tpu as pltpu
from jax.sharding import PartitionSpec as P

HD = 128
ROT = 32
PARAMS = 50416912

EPS_NORM = 1e-05
EPS_ADAM = 1e-06
DECAY_WEIGHT = 0.01
RATE_MATRIX = 0.3
RATE_VECTOR = 0.25
BETA = 0.5
NEGATIVE = -1e30

BF = jnp.bfloat16
F32 = jnp.float32


def layer_norm(values):
    centre = jnp.mean(values, axis=-1, keepdims=True)
    centred = values - centre
    spread = jnp.mean(centred * centred, axis=-1, keepdims=True)
    return centred * lax.rsqrt(spread + EPS_NORM)


def scaled_norm(values, gain_row):
    return layer_norm(values) * gain_row


def shifted_norm(values, gain_row, shift_row):
    return layer_norm(values) * gain_row + shift_row


def gelu_exact(values):
    return jax.nn.gelu(values, approximate=False)


def dot(left, right):
    return jnp.dot(left, right, preferred_element_type=F32)


def dot_tn(left, right):
    return lax.dot_general(left, right, (((0,), (0,)), ((), ())), preferred_element_type=F32)


def dot_nt(left, right):
    return lax.dot_general(left, right, (((1,), (1,)), ((), ())), preferred_element_type=F32)


def mix_history(coef, history):
    total_mix = jnp.zeros((coef.shape[1],) + history.shape[1:], F32)
    for member in range(history.shape[0]):
        total_mix = (
            total_mix
            + jnp.transpose(coef[:, :, member])[:, :, None] * history[member].astype(F32)[None]
        )
    return total_mix


def rotary_tables(seq_len):
    half_width = ROT // 2
    frequency = 10000.0 ** (-(2.0 * jnp.arange(half_width, dtype=F32)) / ROT)
    angles = jnp.arange(seq_len, dtype=F32)[:, None] * frequency[None, :]
    cosine, sine = jnp.cos(angles), jnp.sin(angles)
    rest = HD - ROT
    cos_table = jnp.concatenate([cosine, cosine, jnp.ones((seq_len, rest), F32)], axis=1)
    sin_table = jnp.concatenate([-sine, sine, jnp.zeros((seq_len, rest), F32)], axis=1)
    return cos_table, sin_table


def turn(values, cos_table, sin_table):
    half_width = ROT // 2
    lane = lax.broadcasted_iota(jnp.int32, values.shape, 1)
    partner = jnp.where(
        lane < half_width,
        pltpu.roll(values, HD - half_width, axis=1),
        pltpu.roll(values, half_width, axis=1),
    )
    return values * cos_table + partner * sin_table


def head_scores(query, key):
    seq_len = query.shape[0]
    scores = dot_nt(query, key) * (1.0 / math.sqrt(HD))
    row = lax.broadcasted_iota(jnp.int32, (seq_len, seq_len), 0)
    column = lax.broadcasted_iota(jnp.int32, (seq_len, seq_len), 1)
    scores = jnp.where(row >= column, scores, NEGATIVE)
    exponent = jnp.exp(scores - jnp.max(scores, axis=-1, keepdims=True))
    return exponent / jnp.sum(exponent, axis=-1, keepdims=True)


def attention_forward_kernel(q_ref, k_ref, v_ref, cos_ref, sin_ref, o_ref, qr_ref, kr_ref):
    cos_table, sin_table = cos_ref[...], sin_ref[...]
    query = turn(q_ref[...], cos_table, sin_table).astype(BF)
    key = turn(k_ref[...], cos_table, sin_table).astype(BF)
    qr_ref[...] = query
    kr_ref[...] = key
    probs = head_scores(query, key).astype(BF)
    o_ref[...] = dot(probs, v_ref[...]).astype(BF)


def attention_backward_kernel(
    q_ref, k_ref, v_ref, g_ref, cos_ref, sin_ref, dq_ref, dk_ref, dv_ref
):
    scale = 1.0 / math.sqrt(HD)
    cos_table, sin_table = cos_ref[...], -sin_ref[...]
    query, key, grad = q_ref[...], k_ref[...], g_ref[...]
    probs = head_scores(query, key)
    grad_probs = dot_nt(grad, v_ref[...])
    centre = jnp.sum(probs * grad_probs, axis=-1, keepdims=True)
    grad_scores = (probs * (grad_probs - centre)).astype(BF)
    dq_ref[...] = turn(dot(grad_scores, key) * scale, cos_table, sin_table).astype(BF)
    dk_ref[...] = turn(dot_tn(grad_scores, query) * scale, cos_table, sin_table).astype(BF)
    dv_ref[...] = dot_tn(probs.astype(BF), grad).astype(BF)


def attention_call(kernel, seq_len, blocks, tables, out_types):
    rows, width = blocks[0].shape
    head_block = pl.BlockSpec((seq_len, HD), lambda s, h: (s, h))
    table_block = pl.BlockSpec((seq_len, HD), lambda s, h: (0, 0))
    return pl.pallas_call(
        kernel,
        grid=(rows // seq_len, width // HD),
        in_specs=[head_block] * len(blocks) + [table_block] * 2,
        out_specs=[head_block] * len(out_types),
        out_shape=[jax.ShapeDtypeStruct((rows, width), kind) for kind in out_types],
        compiler_params=pltpu.CompilerParams(vmem_limit_bytes=32 * 1024 * 1024),
        cost_estimate=pl.CostEstimate(
            flops=rows * width * seq_len * 10,
            bytes_accessed=rows * width * 16,
            transcendentals=rows * width * seq_len // HD,
        ),
    )(*blocks, *tables)


class Links:
    def __init__(self, devices):
        self.devices = devices
        self.planes = devices // 8
        index = lax.axis_index("dp")
        self.index = index
        self.core = index & 1
        self.x = (index >> 1) & 1
        self.y = (index >> 2) & 1
        self.z = index >> 3
        self.rank = index & 3

    def swap(self, value, bit):
        return lax.ppermute(value, "dp", [(j, j ^ bit) for j in range(self.devices)])

    def swap_core(self, value):
        return self.swap(value, 1)

    def swap_x(self, value):
        return self.swap(value, 2)

    def swap_y(self, value):
        return self.swap(value, 4)

    def z_groups(self):
        return [[j + 8 * k for k in range(self.planes)] for j in range(8)]

    def z_gather(self, value):
        return lax.all_gather(value, "dp", axis=0, tiled=True, axis_index_groups=self.z_groups())

    def z_reduce(self, value):
        return lax.psum_scatter(
            value, "dp", scatter_dimension=0, tiled=True, axis_index_groups=self.z_groups()
        )

    def total(self, value):
        bit = 1
        while bit < self.devices:
            value = value + self.swap(value, bit)
            bit *= 2
        return value


    def to_absolute(self, parts):
        own, across_x, across_core, across_both = parts
        low_x = self.x == 0
        core_own = (jnp.where(low_x, own, across_x), jnp.where(low_x, across_x, own))
        core_other = (
            jnp.where(low_x, across_core, across_both),
            jnp.where(low_x, across_both, across_core),
        )
        low_core = self.core == 0
        ordered = []
        for mine, other in zip(core_own, core_other):
            ordered.append(jnp.where(low_core, mine, other))
            ordered.append(jnp.where(low_core, other, mine))
        return ordered

    def to_relative(self, parts):
        low_x, low_core = self.x == 0, self.core == 0
        near = [jnp.where(low_x, parts[c], parts[2 + c]) for c in (0, 1)]
        far = [jnp.where(low_x, parts[2 + c], parts[c]) for c in (0, 1)]
        return [
            jnp.where(low_core, near[0], near[1]),
            jnp.where(low_core, far[0], far[1]),
            jnp.where(low_core, near[1], near[0]),
            jnp.where(low_core, far[1], far[0]),
        ]

    def group_gather(self, value):
        across_x = self.swap_x(value)
        across = self.swap_core(jnp.stack([value, across_x]))
        return [value, across_x, across[0], across[1]]

    def group_exchange(self, parts):
        own, for_x, for_core, for_both = parts
        from_x = self.swap_x(jnp.stack([for_x, for_both]))
        from_core = self.swap_core(jnp.stack([for_core, from_x[1]]))
        return [own, from_x[0], from_core[0], from_core[1]]

    def group_reduce(self, parts, kind=BF):
        own, for_x, for_core, for_both = parts
        low = lambda part: part.astype(kind)
        from_core = self.swap_core(jnp.stack([low(for_core), low(for_both)]))
        own = own.astype(F32) + from_core[0].astype(F32)
        for_x = for_x.astype(F32) + from_core[1].astype(F32)
        return own + self.swap_x(low(for_x)).astype(F32)

    def split_y(self, values, axis=-1):
        width = values.shape[-1]
        block = width // (2 * self.planes)
        shape = values.shape[:-1]
        halves = jnp.moveaxis(values.reshape(shape + (self.planes, 2, block)), -2, 0)
        halves = halves.reshape((2,) + shape + (width // 2,))
        low_y = self.y == 0
        return jnp.where(low_y, halves[0], halves[1]), jnp.where(low_y, halves[1], halves[0])

    def join_y(self, own, other):
        width = 2 * own.shape[-1]
        block = width // (2 * self.planes)
        shape = own.shape[:-1]
        low_y = self.y == 0
        first = jnp.where(low_y, own, other).reshape(shape + (self.planes, 1, block))
        second = jnp.where(low_y, other, own).reshape(shape + (self.planes, 1, block))
        return jnp.concatenate([first, second], axis=-2).reshape(shape + (width,))


def program(
    devices,
    history,
    d_out,
    group_ids,
    group_weight,
    attn_in,
    attn_out,
    ffn_up,
    ffn_down,
    mixer_in,
    mixer_out,
    norm_gain,
    norm_bias,
    first_attn_in,
    second_attn_in,
    first_attn_out,
    second_attn_out,
    first_ffn_up,
    second_ffn_up,
    first_ffn_down,
    second_ffn_down,
    first_mixer_in,
    second_mixer_in,
    first_mixer_out,
    second_mixer_out,
    first_norm_gain,
    second_norm_gain,
    first_norm_bias,
    second_norm_bias,
):
    links = Links(devices)
    planes = links.planes
    hist_len, seq_len, width = history.shape
    quarter = width // 4
    rows = width // devices
    hidden = ffn_down.shape[0] * devices
    units = hidden // devices

    low_attn = attn_in.astype(BF).reshape(rows, 3, 4, quarter)
    low_out = attn_out.astype(BF).reshape(rows, 1, 4, quarter)
    by_rank = jnp.concatenate([low_attn, low_out], axis=1)
    by_rank = [by_rank[:, :, r].reshape(rows, width) for r in range(4)]
    attn_block = jnp.concatenate(
        links.to_absolute(links.group_exchange(links.to_relative(by_rank))), axis=0
    )

    low_up = ffn_up.astype(BF).reshape(rows, planes * 2, 4, units)
    by_rank = [low_up[:, :, r].reshape(rows, hidden // 4) for r in range(4)]
    up_block = jnp.concatenate(
        links.to_absolute(links.group_exchange(links.to_relative(by_rank))), axis=0
    )
    low_down = ffn_down.astype(BF)
    other_down = links.swap_y(low_down)
    low_y = links.y == 0
    down_block = jnp.concatenate(
        [jnp.where(low_y, low_down, other_down), jnp.where(low_y, other_down, low_down)], axis=0
    )

    attn_own = links.z_gather(attn_block)
    attn_other = links.swap_y(attn_own)
    up_own = links.z_gather(up_block)
    up_other = links.swap_y(up_own)
    w_down = links.z_gather(down_block)

    out_quarter = jnp.concatenate([attn_own[:, 3 * quarter :], attn_other[:, 3 * quarter :]])
    w_out = links.group_gather(out_quarter)

    hidden_mix = mixer_in.shape[1]
    pack = jnp.concatenate([mixer_in.T, norm_gain, norm_bias], axis=0).astype(BF)
    for bit, high in ((1, links.core), (2, links.x), (4, links.y)):
        other = links.swap(pack, bit)
        pack = jnp.concatenate(
            [jnp.where(high == 0, pack, other), jnp.where(high == 0, other, pack)], axis=1
        )
    pieces = [pack]
    for shift in range(1, planes):
        pieces.append(
            lax.ppermute(pack, "dp", [(j, (j + 8 * shift) % devices) for j in range(devices)])
        )
    backwards = jnp.stack([pieces[-k % planes] for k in range(planes)] * 2)
    ordered = lax.dynamic_slice_in_dim(backwards, planes - links.z, planes, axis=0)
    pack = jnp.transpose(ordered, (1, 0, 2)).reshape(pack.shape[0], width)
    w_mixer_in = pack[:hidden_mix]
    gain_table = pack[hidden_mix : hidden_mix + 3].astype(F32)
    bias_table = pack[hidden_mix + 3 :].astype(F32)
    mixer_low = mixer_out.astype(BF)

    current = history[hist_len - 1].astype(F32)
    mix_normed = scaled_norm(current, gain_table[0]).astype(BF)
    mix_pre = dot_nt(mix_normed, w_mixer_in)
    mix_hidden = gelu_exact(mix_pre).astype(BF)
    coef = dot(mix_hidden, mixer_low).reshape(seq_len, -1, hist_len)
    streams = mix_history(coef, history)
    normed = shifted_norm(streams[:3], gain_table[1], bias_table[0]).astype(BF)

    tables = rotary_tables(seq_len)
    normed_own, normed_other, projected = [], [], []
    for a in range(3):
        gathered = jnp.concatenate(links.group_gather(normed[a]), axis=0)
        own, other = links.split_y(gathered)
        normed_own.append(own)
        normed_other.append(other)
        columns = slice(a * quarter, (a + 1) * quarter)
        projected.append(dot(own, attn_own[:, columns]) + dot(other, attn_other[:, columns]))
    value = projected[2].astype(BF)
    attended, query_rot, key_rot = attention_call(
        attention_forward_kernel,
        seq_len,
        (projected[0], projected[1], value),
        tables,
        (BF, BF, BF),
    )
    attended = links.group_exchange(list(attended.reshape(4, seq_len, quarter)))
    attended = jnp.concatenate(links.to_absolute(attended), axis=-1)
    attended = jnp.concatenate(links.split_y(attended), axis=-1)
    out_parts = [dot(attended, part) for part in w_out]
    residual = streams[3] + jnp.concatenate(links.to_absolute(out_parts), axis=-1)

    ffn_normed = shifted_norm(residual, gain_table[2], bias_table[1]).astype(BF)
    gathered = jnp.concatenate(links.group_gather(ffn_normed), axis=0)
    ffn_own, ffn_other = links.split_y(gathered)
    up_proj = dot(ffn_own, up_own) + dot(ffn_other, up_other)
    activated = gelu_exact(up_proj).astype(BF)
    down_parts = dot(activated, w_down).astype(BF).reshape(4, seq_len, width)
    out_state = (residual + links.group_reduce(list(down_parts))).astype(BF)

    group_count = group_weight.shape[0]
    seq_weight = jnp.sum(
        jnp.where(jnp.arange(group_count, dtype=jnp.int32) == group_ids[0], group_weight, 0.0)
    )
    grad_out = (d_out.astype(F32) * seq_weight).astype(BF)
    grad_out_four = jnp.concatenate(links.group_gather(grad_out), axis=0)

    grad_down = dot_tn(activated, grad_out_four).astype(BF)
    grad_down = links.z_reduce(grad_down).reshape(2, units, width)
    down_mine = jnp.where(low_y, grad_down[0], grad_down[1])
    down_theirs = jnp.where(low_y, grad_down[1], grad_down[0])
    shard_down = down_mine.astype(F32) + links.swap_y(down_theirs).astype(F32)

    grad_activated = dot_nt(grad_out_four, w_down)
    _, gelu_back = jax.vjp(gelu_exact, up_proj)
    grad_up = gelu_back(grad_activated)[0].astype(BF)

    def reduce_rows(own, other):
        both = own.astype(F32) + links.swap_y(other.astype(BF)).astype(F32)
        block = links.z_reduce(both.astype(BF))
        parts = list(block.reshape(4, rows, block.shape[1]))
        parts = links.to_absolute(links.group_exchange(links.to_relative(parts)))
        return jnp.stack(parts, axis=1).astype(F32)

    grad_ffn_up = reduce_rows(
        dot_tn(ffn_own, grad_up).astype(BF), dot_tn(ffn_other, grad_up).astype(BF)
    )
    shard_up = jnp.transpose(
        grad_ffn_up.reshape(rows, 4, planes * 2, units), (0, 2, 1, 3)
    ).reshape(rows, hidden)

    back_own = dot_nt(grad_up, up_own).astype(BF).reshape(4, seq_len, width // 2)
    back_other = dot_nt(grad_up, up_other).astype(BF).reshape(4, seq_len, width // 2)
    both = jnp.stack([back_own, back_other], axis=1)
    grad_ffn_normed = links.group_reduce(list(both))
    grad_ffn_normed = links.join_y(grad_ffn_normed[0], grad_ffn_normed[1])
    _, ffn_norm_back = jax.vjp(shifted_norm, residual, gain_table[2], bias_table[1])
    grad_ffn_x, grad_gain_ffn, grad_bias_ffn = ffn_norm_back(grad_ffn_normed)
    grad_residual = (grad_out.astype(F32) + grad_ffn_x).astype(BF)

    residual_parts = links.to_relative(
        [grad_residual[:, r * quarter : (r + 1) * quarter] for r in range(4)]
    )
    grad_attended = dot_nt(residual_parts[0], w_out[0])
    for part, weight in zip(residual_parts[1:], w_out[1:]):
        grad_attended = grad_attended + dot_nt(part, weight)
    grad_attended = grad_attended.astype(BF)
    grad_heads = links.join_y(grad_attended[:, : width // 2], grad_attended[:, width // 2 :])
    grad_heads = links.group_exchange(
        links.to_relative([grad_heads[:, r * quarter : (r + 1) * quarter] for r in range(4)])
    )
    grad_heads = jnp.concatenate(grad_heads, axis=0)
    grad_proj = attention_call(
        attention_backward_kernel,
        seq_len,
        (query_rot, key_rot, value, grad_heads),
        tables,
        (BF, BF, BF),
    )

    out_grads = [dot_tn(attended, part).astype(BF) for part in residual_parts]
    out_grad = links.group_reduce(out_grads)
    grad_attn_out = reduce_rows(out_grad[: width // 2], out_grad[width // 2 :])
    shard_out = grad_attn_out.reshape(rows, width)

    in_own = [dot_tn(normed_own[a], grad_proj[a]).astype(BF) for a in range(3)]
    in_other = [dot_tn(normed_other[a], grad_proj[a]).astype(BF) for a in range(3)]
    grad_attn_in = reduce_rows(jnp.concatenate(in_own, axis=1), jnp.concatenate(in_other, axis=1))
    shard_in = jnp.transpose(
        grad_attn_in.reshape(rows, 4, 3, quarter), (0, 2, 1, 3)
    ).reshape(rows, 3 * width)

    grad_normed = []
    for a in range(3):
        columns = slice(a * quarter, (a + 1) * quarter)
        back_own = dot_nt(grad_proj[a], attn_own[:, columns]).astype(BF)
        back_other = dot_nt(grad_proj[a], attn_other[:, columns]).astype(BF)
        both = jnp.stack(
            [
                back_own.reshape(4, seq_len, width // 2),
                back_other.reshape(4, seq_len, width // 2),
            ],
            axis=1,
        )
        both = links.group_reduce(list(both))
        grad_normed.append(links.join_y(both[0], both[1]))
    grad_normed = jnp.stack(grad_normed)
    _, attn_norm_back = jax.vjp(shifted_norm, streams[:3], gain_table[1], bias_table[0])
    grad_streams, grad_gain_attn, grad_bias_attn = attn_norm_back(grad_normed)

    grad_mixed = jnp.concatenate([grad_streams, grad_residual.astype(F32)[None]], axis=0)
    coef_columns = []
    hist_grads = []
    for member in range(hist_len):
        history_rows = history[member].astype(F32)
        coef_columns.append(jnp.sum(grad_mixed * history_rows[None], axis=-1))
        hist_grads.append(
            jnp.sum(jnp.transpose(coef[:, :, member])[:, :, None] * grad_mixed, axis=0)
        )
    grad_coef = (
        jnp.transpose(jnp.stack(coef_columns, axis=-1), (1, 0, 2)).reshape(seq_len, -1).astype(BF)
    )
    grad_mixer_out = dot_tn(mix_hidden, grad_coef)
    grad_mix_hidden = dot_nt(grad_coef, mixer_low)
    _, mix_gelu_back = jax.vjp(gelu_exact, mix_pre)
    grad_mix_pre = mix_gelu_back(grad_mix_hidden)[0].astype(BF)
    grad_mixer_in = dot_tn(grad_mix_pre, mix_normed)
    grad_mix_normed = dot(grad_mix_pre, w_mixer_in)
    _, mix_norm_back = jax.vjp(scaled_norm, current, gain_table[0])
    grad_current, grad_gain_mix = mix_norm_back(grad_mix_normed)
    hist_grads[hist_len - 1] = hist_grads[hist_len - 1] + grad_current
    grad_history = jnp.stack(hist_grads).astype(BF)

    small = jnp.concatenate(
        [
            grad_mixer_in,
            grad_gain_mix[None],
            grad_gain_attn[None],
            grad_gain_ffn[None],
            grad_bias_attn[None],
            grad_bias_ffn[None],
        ],
        axis=0,
    )
    small = small + links.swap_core(small)
    small = small + links.swap_x(small)
    small_own, small_other = links.split_y(small)
    small = small_own + links.swap_y(small_other)
    blocks = small.reshape(small.shape[0], planes, 4 * rows)
    small = lax.dynamic_index_in_dim(blocks, links.z, axis=1, keepdims=False)
    for shift in range(1, planes):
        sent = lax.dynamic_index_in_dim(
            blocks, (links.z + shift) % planes, axis=1, keepdims=False
        )
        small = small + lax.ppermute(
            sent, "dp", [(j, (j + 8 * shift) % devices) for j in range(devices)]
        )
    small = lax.dynamic_slice_in_dim(small, links.rank * rows, rows, axis=1)
    mixer_grad = links.total(grad_mixer_out)
    grads = (
        shard_in,
        shard_out,
        shard_up,
        shard_down,
        small[:hidden_mix].T,
        mixer_grad,
        small[hidden_mix : hidden_mix + 3],
        small[hidden_mix + 3 :],
    )

    weights = (attn_in, attn_out, ffn_up, ffn_down, mixer_in, mixer_out, norm_gain, norm_bias)
    firsts = (
        first_attn_in,
        first_attn_out,
        first_ffn_up,
        first_ffn_down,
        first_mixer_in,
        first_mixer_out,
        first_norm_gain,
        first_norm_bias,
    )
    seconds = (
        second_attn_in,
        second_attn_out,
        second_ffn_up,
        second_ffn_down,
        second_mixer_in,
        second_mixer_out,
        second_norm_gain,
        second_norm_bias,
    )

    def portion(member, amount):
        return amount / devices if member == 5 else amount

    local_squares = sum(
        (portion(member, jnp.sum(grads[member] * grads[member])) for member in range(8))
    )
    local_weight_sq = [
        portion(member, jnp.sum(weights[member] * weights[member])) for member in range(6)
    ]
    sums = links.total(jnp.stack([local_squares] + local_weight_sq))
    squares, weight_sq = sums[0], sums[1:]
    global_norm = jnp.sqrt(squares)
    clip = 0.3 * math.sqrt(PARAMS) / (global_norm + 1e-06)
    pending = []
    local_update_sq = []
    for member in range(8):
        scaled = grads[member] * clip
        first_new = BETA * firsts[member] + (1.0 - BETA) * scaled
        second_new = BETA * seconds[member] + (1.0 - BETA) * scaled * scaled
        step_value = first_new / (jnp.sqrt(second_new) + EPS_ADAM)
        if member < 6:
            step_value = step_value + DECAY_WEIGHT * weights[member]
            local_update_sq.append(portion(member, jnp.sum(step_value * step_value)))
        pending.append((first_new, second_new, step_value))
    update_sq = links.total(jnp.stack(local_update_sq))
    weight_norm = jnp.sqrt(weight_sq)
    update_norm = jnp.sqrt(update_sq)
    trust = weight_norm / (update_norm + 1e-06)
    lamb_stats = jnp.stack([weight_norm, update_norm, trust], axis=1)
    results = []
    for member in range(8):
        first_new, second_new, step_value = pending[member]
        if member < 6:
            updated = weights[member] - RATE_MATRIX * trust[member] * step_value
        else:
            updated = weights[member] - RATE_VECTOR * step_value
        results += [updated, updated.astype(BF), first_new, second_new]
    return (out_state, grad_history, global_norm, lamb_stats, *results)


def solution(mesh):
    rows, columns, whole = P("dp", None), P(None, "dp"), P()
    middle = P(None, "dp", None)
    matrices = (rows,) * 5 + (whole,) + (columns,) * 2
    moments = tuple(spec for spec in matrices for _ in range(2))
    results = tuple(spec for spec in matrices for _ in range(4))
    return jax.shard_map(
        functools.partial(program, mesh.shape["dp"]),
        mesh=mesh,
        in_specs=(middle, rows, P("dp"), whole) + matrices + moments,
        out_specs=(rows, middle, whole, whole) + results,
        check_vma=False,
    )
```

time: 3400 us -> 1250 us (0.37)
  waiting for transfers between devices: 2580 us -> 438 us
  blocking collectives: 247 us -> 0 us
  other arithmetic: 132 us -> 275 us
  local copies, waits for them, and re-layouts: 149 us -> 244 us
  matrix products: 255 us -> 167 us
  starting transfers between devices: 0.46 us -> 55.5 us
    reduce_scatter x4, waiting for transfers between devices: 2030 us -> 0.03 us  [z_reduce(): lax.psum_scatter(value, 'dp', scatter_dimension=0, tiled=True, axis_index...]
    ppermute x0 -> x72, waiting for transfers between devices: none -> 438 us  [the longest x66 426 us: swap(): lax.ppermute(value, 'dp', [(j, j ^ bit) for j in range(self.devices)])]
    all_gather x4 -> x3, waiting for transfers between devices: 391 us -> 0.01 us  [z_gather(): lax.all_gather(value, 'dp', axis=0, tiled=True, axis_index_groups=self.z_...]
    unnamed x14 -> x7, waiting for transfers between devices: 158 us -> 0.11 us
    psum x3 -> x0, blocking collectives: 126 us -> none  [the longest x1 47.2 us: local(): squares, weight_sq = lax.psum((local_squares, local_weight_sq), 'dp')]
    all_gather x3 -> x0, blocking collectives: 121 us -> none  [the longest x1 43.4 us: local(): lax.all_gather(low_shards[6], 'dp', axis=1, tiled=True)]
    dot_general x23 -> x45, matrix products: 253 us -> 167 us  [the longest x15 63.2 us: dot_nt(): lax.dot_general(left, right, (((1,), (1,)), ((), ())), preferred_element_...]
    concatenate x2 -> x40, local copies, waits for them, and re-layouts: 3.57 us -> 72.9 us  [the longest x24 38.1 us: program(): gathered = jnp.concatenate(links.group_gather(normed[a]), axis=0)]
  transfers between devices with their start and end apart: 11 -> 79, of which waited for: 10 -> 40; matrix products, arithmetic and copies ran while one was open for 9% -> 43% of each run, Pallas kernels for 0% -> 2%
where the time goes in v1:
time: 1250 us; the launch traced here: 1240 us
  waiting for transfers between devices  438 us (35%)
  other arithmetic  275 us (22%)
  local copies, waits for them, and re-layouts  244 us (20%)
  matrix products  167 us (13%)
  starting transfers between devices  55.5 us (4%)
  between operations  30.7 us (2%)
  Pallas kernels  25.5 us (2%)
    ppermute x66, waiting for transfers between devices, swap(): lax.ppermute(value, 'dp', [(j, j ^ bit) for j in range(self.devices)])  426 us
    dot_general x15, matrix products, dot_nt(): lax.dot_general(left, right, (((1,), (1,)), ((), ())), preferred_element_...  63.2 us
    dot_general x15, matrix products, dot(): return jnp.dot(left, right, preferred_element_type=F32)  60 us
    unnamed x549, local copies, waits for them, and re-layouts  58.3 us
    ppermute x66, starting transfers between devices, swap(): lax.ppermute(value, 'dp', [(j, j ^ bit) for j in range(self.devices)])  45.5 us
    dot_general x15, matrix products, dot_tn(): lax.dot_general(left, right, (((0,), (0,)), ((), ())), preferred_element_...  43.6 us
    concatenate x24, local copies, waits for them, and re-layouts, program(): gathered = jnp.concatenate(links.group_gather(normed[a]), axis=0)  38.1 us
    reduce_sum x2, other arithmetic, program(): coef_columns.append(jnp.sum(grad_mixed * history_rows[None], axis=-1))  29.1 us
  transfers between devices with their start and end apart: 79, of which 40 were waited for; matrix products, arithmetic and copies ran while one was open for 43% of the time, Pallas kernels for 2%

profile of v1, /device:TPU:0, one launch (start us, length us, event | category | flops | bytes accessed | tf_op | source)
XLA Modules:
  0.0 1236.2 jit_solution(4164970198114505209)
XLA Ops:
  21.5 8.7 bitcast_convert_fusion.8
  65.1 9.4 multiply_add_fusion
  95.1 13.1 %collective-permute-done.6 = bf16[256,2048]{1,0:T(8,128)(2,1)} collective-permute-done((bf16[256,2048]{1,0:T(8,128)(2,1)}, bf16[256,2048]{1,0:T(8,128)(2,1)}, u32[]{:S(2)}, u32[]{:S(2)}) %collective-permute-start.6) | collective-permute-done | bytes 1048608 | tf_op jit(solution)/shard_map/ppermute | solution.py:157
  120.3 21.5 %collective-permute-done.11 = bf16[256,2048]{1,0:T(8,128)(2,1)} collective-permute-done((bf16[256,2048]{1,0:T(8,128)(2,1)}, bf16[256,2048]{1,0:T(8,128)(2,1)}, u32[]{:S(2)}, u32[]{:S(2)}) %collective-permute-start.11) | collective-permute-done | bytes 1048608 | tf_op jit(solution)/shard_map/ppermute | solution.py:157
  213.2 26.4 %collective-permute-done.10 = bf16[1024,2048]{1,0:T(8,128)(2,1)} collective-permute-done((bf16[1024,2048]{1,0:T(8,128)(2,1)}, bf16[1024,2048]{1,0:T(8,128)(2,1)}, u32[]{:S(2)}, u32[]{:S(2)}) %collective-permute-start.10) | collective-permute-done | bytes 4194336 | tf_op jit(solution)/shard_map/ppermute | solution.py:157
  255.0 32.7 %collective-permute-done.17 = bf16[2048,512]{1,0:T(8,128)(2,1)S(1)} collective-permute-done((bf16[2048,512]{1,0:T(8,128)(2,1)S(1)}, bf16[2048,512]{1,0:T(8,128)(2,1)S(1)}, u32[]{:S(2)}, u32[]{:S(2)}) %collective-permute-start.17) | collective-permute-done | bytes 2097184 | tf_op jit(solution)/shard_map/ppermute | solution.py:157
  298.4 12.0 shard_map.547
  315.1 10.3 collective-permute-done.15
  354.6 19.0 %collective-permute-done.19 = bf16[256,2048]{1,0:T(8,128)(2,1)S(1)} collective-permute-done((bf16[256,2048]{1,0:T(8,128)(2,1)S(1)}, bf16[256,2048]{1,0:T(8,128)(2,1)S(1)}, u32[]{:S(2)}, u32[]{:S(2)}) %collective-permute-start.19) | collective-permute-done | bytes 1048608 | tf_op jit(solution)/shard_map/ppermute | solution.py:157
  423.9 44.7 %collective-permute-done.23 = bf16[1024,2048]{1,0:T(8,128)(2,1)} collective-permute-done((bf16[1024,2048]{1,0:T(8,128)(2,1)}, bf16[1024,2048]{1,0:T(8,128)(2,1)}, u32[]{:S(2)}, u32[]{:S(2)}) %collective-permute-start.23) | collective-permute-done | bytes 4194336 | tf_op jit(solution)/shard_map/ppermute | solution.py:157
  468.6 25.9 %multiply_convert_fusion = (bf16[1024,2048]{1,0:T(8,128)(2,1)}, f32[1024,2048]{1,0:T(8,128)}, f32[1024,2048]{1,0:T(8,128)}) fusion(f32[1024,2048]{1,0:T(8,128)S(1)} %fusion.158, bf16[1024,1024]{0,1:T(8,128)(2,1)S(1)} %bitcast.707, bf16[1024,2048]{1,0:T(8,128)(2,1)} %collective-permute-done.23), kind=kOutput, calls=%fused_computation.24 | convolution fusion | flops 4433379328 | bytes 35651584 | tf_op jit(solution)/shard_map/dot_general | solution.py:47
  494.6 20.6 %add_convert_fusion.1 = bf16[1024,2048]{1,0:T(8,128)(2,1)} fusion(f32[1024,2048]{1,0:T(8,128)} %get-tuple-element.136, f32[1024,2048]{1,0:T(8,128)} %get-tuple-element.323, bf16[2048,2048]{1,0:T(8,128)(2,1)} %all-gather.8.cloned.1.call-done, bf16[256,2048]{1,0:T(8,128)(2,1)} %get-tuple-element.198, bf16[256,2048]{1,0:T(8,128)(2,1)S(1)} %copy-done.145, ...), kind=kOutput, calls=%fused_computation.23 | convolution fusion | flops 8636071936 | bytes 33554432 | tf_op jit(solution)/shard_map/dot_general | solution.py:55
  535.3 9.5 convolution_convert_fusion.1
  571.1 13.4 %collective-permute-done.30 = bf16[2,256,1024]{2,1,0:T(8,128)(2,1)S(1)} collective-permute-done((bf16[2,256,1024]{2,1,0:T(8,128)(2,1)S(1)}, bf16[2,256,1024]{2,1,0:T(8,128)(2,1)S(1)}, u32[]{:S(2)}, u32[]{:S(2)}) %collective-permute-start.30) | collective-permute-done | bytes 1048608 | tf_op jit(solution)/shard_map/ppermute | solution.py:157
  622.3 36.8 %collective-permute-done.47 = bf16[1024,2048]{1,0:T(8,128)(2,1)} collective-permute-done((bf16[1024,2048]{1,0:T(8,128)(2,1)}, bf16[1024,2048]{1,0:T(8,128)(2,1)}, u32[]{:S(2)}, u32[]{:S(2)}) %collective-permute-start.47) | collective-permute-done | bytes 4194336 | tf_op jit(solution)/shard_map/ppermute | solution.py:157
  691.6 12.9 %collective-permute-done.31 = bf16[2,256,512]{2,1,0:T(8,128)(2,1)S(1)} collective-permute-done((bf16[2,256,512]{2,1,0:T(8,128)(2,1)S(1)}, bf16[2,256,512]{2,1,0:T(8,128)(2,1)S(1)}, u32[]{:S(2)}, u32[]{:S(2)}) %collective-permute-start.31) | collective-permute-done | bytes 524320 | tf_op jit(solution)/shard_map/ppermute | solution.py:157
  709.7 13.5 %shard_map.548 = (bf16[1024,512]{1,0:T(8,128)(2,1)S(1)}, bf16[1024,512]{1,0:T(8,128)(2,1)S(1)}, bf16[1024,512]{1,0:T(8,128)(2,1)S(1)}) custom-call(bf16[1024,512]{1,0:T(8,128)(2,1)S(1)} %get-tuple-element.43.q_ref, bf16[1024,512]{1,0:T(8,128)(2,1)S(1)} %get-tuple-element.44.k_ref, bf16[1024,512]{1,0:T(8,128)(2,1)S(1)} %copy-done.1, ...), custom_call_target="tpu_custom_call" | custom-call | flops 1342177280 | bytes 8388608 | tf_op jit(solution)/shard_map/pallas_call | solution.py:129
  732.0 23.1 %collective-permute-done.43 = bf16[2048,512]{1,0:T(8,128)(2,1)S(1)} collective-permute-done((bf16[2048,512]{1,0:T(8,128)(2,1)S(1)}, bf16[2048,512]{1,0:T(8,128)(2,1)S(1)}, u32[]{:S(2)}, u32[]{:S(2)}) %collective-permute-start.43) | collective-permute-done | bytes 2097184 | tf_op jit(solution)/shard_map/ppermute | solution.py:157
  759.3 64.0 %collective-permute-done.44 = bf16[1024,512]{1,0:T(8,128)(2,1)S(1)} collective-permute-done((bf16[1024,512]{1,0:T(8,128)(2,1)S(1)}, bf16[1024,512]{1,0:T(8,128)(2,1)S(1)}, u32[]{:S(2)}, u32[]{:S(2)}) %collective-permute-start.44) | collective-permute-done | bytes 1048608 | tf_op jit(solution)/shard_map/ppermute | solution.py:157
  869.8 13.1 %convolution_convert_fusion = bf16[2048,2048]{1,0:T(8,128)(2,1)} fusion(bf16[1024,2048]{1,0:T(8,128)(2,1)S(1)} %copy-done.238, bf16[256,2048]{1,0:T(8,128)(2,1)S(1)} %copy-done.147, bf16[256,2048]{1,0:T(8,128)(2,1)S(1)} %copy-done.146, bf16[256,2048]{1,0:T(8,128)(2,1)} %collective-permute-done.27, bf16[256,2048]{1,0:T(8,128)(2,1)} %multiply_convert_fusion.2), kind=kOutput, calls=%fused_computation.39 | convolution fusion | flops 8610906112 | bytes 16777216 | tf_op jit(solution)/shard_map/dot_general | solution.py:51
  893.0 20.3 %collective-permute-done.34 = bf16[2,256,1024]{2,1,0:T(8,128)(2,1)} collective-permute-done((bf16[2,256,1024]{2,1,0:T(8,128)(2,1)}, bf16[2,256,1024]{2,1,0:T(8,128)(2,1)}, u32[]{:S(2)}, u32[]{:S(2)}) %collective-permute-start.34) | collective-permute-done | bytes 1048608 | tf_op jit(solution)/shard_map/ppermute | solution.py:157
  983.8 19.4 %multiply_reduce_fusion.1 = (bf16[4,256]{1,0:T(4,128)(2,1)S(1)}, bf16[256,2048]{1,0:T(8,128)(2,1)}, bf16[256,2048]{1,0:T(8,128)(2,1)S(1)}, f32[256,2048]{1,0:T(8...) fusion(f32[256,2048]{1,0:T(8,128)} %get-tuple-element.156, ...), kind=kLoop, calls=%fused_computation.6 | loop fusion | flops 48230400 | bytes 26255360 | tf_op jit(solution)/shard_map/reduce_sum | solution.py:473
  1003.3 9.7 multiply_reduce_fusion.2
  1111.0 17.3 %collective-permute-done.50 = bf16[256,2048]{1,0:T(8,128)(2,1)S(1)} collective-permute-done((bf16[256,2048]{1,0:T(8,128)(2,1)}, bf16[256,2048]{1,0:T(8,128)(2,1)S(1)}, u32[]{:S(2)}, u32[]{:S(2)}) %collective-permute-start.50) | collective-permute-done | bytes 1048608 | tf_op jit(solution)/shard_map/ppermute | solution.py:157
  (1047 shorter events, 708.1 us)
Async XLA Ops:
  7.2 138.7 %all-gather.4.cloned.1.call-start = ((), (), s32[]{:S(2)}) async-start(), calls=%async_computation.4 | async-start | bytes 5242880 | tf_op jit(solution)/shard_map/all_gather | solution.py:172
  64.5 310.8 %all-gather.6.cloned.1.call-start = ((), (), s32[]{:S(2)}) async-start(), calls=%async_computation.5 | async-start | bytes 5242880 | tf_op jit(solution)/shard_map/all_gather | solution.py:172
  89.3 52.6 %collective-permute-start.11 = (bf16[256,2048]{1,0:T(8,128)(2,1)}, bf16[256,2048]{1,0:T(8,128)(2,1)}, u32[]{:S(2)}, u32[]{:S(2)}) collective-permute-start(bf16[256,2048]{1,0:T(8,128)(2,1)} %get-tuple-element.178), channel_id=1, source_target_pairs={{0,2},{1,3},{2,0},{3,1},{4,6},{5,7},{6,4},{7,5},{8,10},{9,11},{10,... | collective-permute-start | bytes 3145736 | tf_op jit(solution)/shard_map/ppermute | solution.py:157
  93.5 70.3 %collective-permute-start.13 = (bf16[256,2048]{1,0:T(8,128)(2,1)}, bf16[256,2048]{1,0:T(8,128)(2,1)}, u32[]{:S(2)}, u32[]{:S(2)}) collective-permute-start(bf16[256,2048]{1,0:T(8,128)(2,1)} %get-tuple-element.179), channel_id=1, source_target_pairs={{0,2},{1,3},{2,0},{3,1},{4,6},{5,7},{6,4},{7,5},{8,10},{9,11},{10,... | collective-permute-start | bytes 3145736 | tf_op jit(solution)/shard_map/ppermute | solution.py:157
  111.0 71.8 %collective-permute-start.7 = (bf16[2,256,2048]{2,1,0:T(8,128)(2,1)}, bf16[2,256,2048]{2,1,0:T(8,128)(2,1)}, u32[]{:S(2)}, u32[]{:S(2)}) collective-permute-start(bf16[2,256,2048]{2,1,0:T(8,128)(2,1)} %pad_maximum_fusion.5), channel_id=1, source_target_pairs={{0,1},{1,0},{2,3},{3,2},{4,5},{5,4},{6,7},{7,6},{8,9},{9,8},{10,11... | collective-permute-start | bytes 6291464 | tf_op jit(solution)/shard_map/ppermute | solution.py:157
  144.5 45.9 %collective-permute-start.12 = (bf16[2,256,2048]{2,1,0:T(8,128)(2,1)}, bf16[2,256,2048]{2,1,0:T(8,128)(2,1)}, u32[]{:S(2)}, u32[]{:S(2)}) collective-permute-start(bf16[2,256,2048]{2,1,0:T(8,128)(2,1)} %pad_maximum_fusion.6), channel_id=1, source_target_pairs={{0,1},{1,0},{2,3},{3,2},{4,5},{5,4},{6,7},{7,6},{8,9},{9,8},{10,11... | collective-permute-start | bytes 6291464 | tf_op jit(solution)/shard_map/ppermute | solution.py:157
  145.9 93.8 %collective-permute-start.10 = (bf16[1024,2048]{1,0:T(8,128)(2,1)}, bf16[1024,2048]{1,0:T(8,128)(2,1)}, u32[]{:S(2)}, u32[]{:S(2)}) collective-permute-start(bf16[1024,2048]{1,0:T(8,128)(2,1)} %all-gather.4.cloned.1.call-done), channel_id=1, source_target_pairs={{0,4},{1,5},{2,6},{3,7},{4,0},{5,1},{6,2},{7,3},{8,12},{9,13},{10,... | collective-permute-start | bytes 12582920 | tf_op jit(solution)/shard_map/ppermute | solution.py:157
  163.9 162.5 %collective-permute-start.24 = (bf16[256,2048]{1,0:T(8,128)(2,1)}, bf16[256,2048]{1,0:T(8,128)(2,1)}, u32[]{:S(2)}, u32[]{:S(2)}) collective-permute-start(bf16[256,2048]{1,0:T(8,128)(2,1)} %get-tuple-element.183), channel_id=1, source_target_pairs={{0,4},{1,5},{2,6},{3,7},{4,0},{5,1},{6,2},{7,3},{8,12},{9,13},{10,... | collective-permute-start | bytes 3145736 | tf_op jit(solution)/shard_map/ppermute | solution.py:157
  170.4 324.1 %all-gather.8.cloned.1.call-start = ((), (), s32[]{:S(2)}) async-start(), calls=%async_computation.6 | async-start | bytes 10485760 | tf_op jit(solution)/shard_map/all_gather | solution.py:172
  241.9 45.7 %collective-permute-start.17 = (bf16[2048,512]{1,0:T(8,128)(2,1)S(1)}, bf16[2048,512]{1,0:T(8,128)(2,1)S(1)}, u32[]{:S(2)}, u32[]{:S(2)}) collective-permute-start(bf16[2048,512]{1,0:T(8,128)(2,1)S(1)} %get-tuple-element.211), channel_id=1, source_target_pairs={{0,2},{1,3},{2,0},{3,1},{4,6},{5,7},{6,4},{7,5},{8,10},{9,11},{10,... | collective-permute-start | bytes 6291464 | tf_op jit(solution)/shard_map/ppermute | solution.py:157
  290.5 48.0 %collective-permute-start.18 = (bf16[2,2048,512]{2,1,0:T(8,128)(2,1)}, bf16[2,2048,512]{2,1,0:T(8,128)(2,1)}, u32[]{:S(2)}, u32[]{:S(2)}) collective-permute-start(bf16[2,2048,512]{2,1,0:T(8,128)(2,1)} %pad_maximum_fusion.1), channel_id=1, source_target_pairs={{0,1},{1,0},{2,3},{3,2},{4,5},{5,4},{6,7},{7,6},{8,9},{9,8},{10,11... | collective-permute-start | bytes 12582920 | tf_op jit(solution)/shard_map/ppermute | solution.py:157
  329.6 733.9 %reduce-scatter.9.cloned.1.call-start = ((), (), s32[]{:S(2)}) async-start(), calls=%async_computation.9 | async-start | bytes 5242880 | tf_op jit(solution)/shard_map/reduce_scatter | solution.py:175
  375.3 93.3 %collective-permute-start.23 = (bf16[1024,2048]{1,0:T(8,128)(2,1)}, bf16[1024,2048]{1,0:T(8,128)(2,1)}, u32[]{:S(2)}, u32[]{:S(2)}) collective-permute-start(bf16[1024,2048]{1,0:T(8,128)(2,1)} %all-gather.6.cloned.1.call-done), channel_id=1, source_target_pairs={{0,4},{1,5},{2,6},{3,7},{4,0},{5,1},{6,2},{7,3},{8,12},{9,13},{10,... | collective-permute-start | bytes 12582920 | tf_op jit(solution)/shard_map/ppermute | solution.py:157
  565.9 93.3 %collective-permute-start.47 = (bf16[1024,2048]{1,0:T(8,128)(2,1)}, bf16[1024,2048]{1,0:T(8,128)(2,1)}, u32[]{:S(2)}, u32[]{:S(2)}) collective-permute-start(bf16[1024,2048]{1,0:T(8,128)(2,1)} %convolution_convert_fusion.2), channel_id=1, source_target_pairs={{0,4},{1,5},{2,6},{3,7},{4,0},{5,1},{6,2},{7,3},{8,12},{9,13},{10,... | collective-permute-start | bytes 12582920 | tf_op jit(solution)/shard_map/ppermute | solution.py:157
  570.3 41.4 %collective-permute-start.26 = (bf16[256,2048]{1,0:T(8,128)(2,1)}, bf16[256,2048]{1,0:T(8,128)(2,1)}, u32[]{:S(2)}, u32[]{:S(2)}) collective-permute-start(bf16[256,2048]{1,0:T(8,128)(2,1)} %fusion.37), channel_id=1, source_target_pairs={{0,2},{1,3},{2,0},{3,1},{4,6},{5,7},{6,4},{7,5},{8,10},{9,11},{10,... | collective-permute-start | bytes 3145736 | tf_op jit(solution)/shard_map/ppermute | solution.py:157
  622.3 82.3 %collective-permute-start.42 = (bf16[2,2048,512]{2,1,0:T(8,128)(2,1)}, bf16[2,2048,512]{2,1,0:T(8,128)(2,1)}, u32[]{:S(2)}, u32[]{:S(2)}) collective-permute-start(bf16[2,2048,512]{2,1,0:T(8,128)(2,1)} %pad_maximum_fusion.3), channel_id=1, source_target_pairs={{0,1},{1,0},{2,3},{3,2},{4,5},{5,4},{6,7},{7,6},{8,9},{9,8},{10,11... | collective-permute-start | bytes 12582920 | tf_op jit(solution)/shard_map/ppermute | solution.py:157
  667.0 397.9 %reduce-scatter.7.cloned.1.call-start = ((), (), s32[]{:S(2)}) async-start(), calls=%async_computation.8 | async-start | bytes 1310720 | tf_op jit(solution)/shard_map/reduce_scatter | solution.py:175
  707.1 48.0 %collective-permute-start.43 = (bf16[2048,512]{1,0:T(8,128)(2,1)S(1)}, bf16[2048,512]{1,0:T(8,128)(2,1)S(1)}, u32[]{:S(2)}, u32[]{:S(2)}) collective-permute-start(bf16[2048,512]{1,0:T(8,128)(2,1)S(1)} %fusion.6), channel_id=1, source_target_pairs={{0,2},{1,3},{2,0},{3,1},{4,6},{5,7},{6,4},{7,5},{8,10},{9,11},{10,... | collective-permute-start | bytes 6291464 | tf_op jit(solution)/shard_map/ppermute | solution.py:157
  730.4 101.2 %collective-permute-start.39 = (bf16[1024,1536]{0,1:T(8,128)(2,1)}, bf16[1024,1536]{0,1:T(8,128)(2,1)}, u32[]{:S(2)}, u32[]{:S(2)}) collective-permute-start(bf16[1024,1536]{0,1:T(8,128)(2,1)} %pad_maximum_fusion.4), channel_id=1, source_target_pairs={{0,4},{1,5},{2,6},{3,7},{4,0},{5,1},{6,2},{7,3},{8,12},{9,13},{10,... | collective-permute-start | bytes 9437192 | tf_op jit(solution)/shard_map/ppermute | solution.py:157
  757.8 65.6 %collective-permute-start.44 = (bf16[1024,512]{1,0:T(8,128)(2,1)S(1)}, bf16[1024,512]{1,0:T(8,128)(2,1)S(1)}, u32[]{:S(2)}, u32[]{:S(2)}) collective-permute-start(bf16[1024,512]{1,0:T(8,128)(2,1)S(1)} %slice.1262), channel_id=1, source_target_pairs={{0,4},{1,5},{2,6},{3,7},{4,0},{5,1},{6,2},{7,3},{8,12},{9,13},{10,... | collective-permute-start | bytes 3145736 | tf_op jit(solution)/shard_map/ppermute | solution.py:157
  824.7 258.8 %reduce-scatter.5.cloned.1.call-start = ((), (), s32[]{:S(2)}) async-start(), calls=%async_computation.7 | async-start | bytes 3932160 | tf_op jit(solution)/shard_map/reduce_scatter | solution.py:175
  835.7 264.1 %reduce-scatter.11.cloned.1.call-start = ((), (), s32[]{:S(2)}) async-start(), calls=%async_computation.10 | async-start | bytes 10485760 | tf_op jit(solution)/shard_map/reduce_scatter | solution.py:175
  869.1 44.2 %collective-permute-start.34 = (bf16[2,256,1024]{2,1,0:T(8,128)(2,1)}, bf16[2,256,1024]{2,1,0:T(8,128)(2,1)}, u32[]{:S(2)}, u32[]{:S(2)}) collective-permute-start(bf16[2,256,1024]{2,1,0:T(8,128)(2,1)} %fusion.47), channel_id=1, source_target_pairs={{0,2},{1,3},{2,0},{3,1},{4,6},{5,7},{6,4},{7,5},{8,10},{9,11},{10,... | collective-permute-start | bytes 3145736 | tf_op jit(solution)/shard_map/ppermute | solution.py:157
  886.0 60.5 %collective-permute-start.38 = (bf16[2,256,1024]{2,1,0:T(8,128)(2,1)}, bf16[2,256,1024]{2,1,0:T(8,128)(2,1)}, u32[]{:S(2)}, u32[]{:S(2)}) collective-permute-start(bf16[2,256,1024]{2,1,0:T(8,128)(2,1)} %fusion.49), channel_id=1, source_target_pairs={{0,2},{1,3},{2,0},{3,1},{4,6},{5,7},{6,4},{7,5},{8,10},{9,11},{10,... | collective-permute-start | bytes 3145736 | tf_op jit(solution)/shard_map/ppermute | solution.py:157
  (303 other events, 2853.6 us)
Sparse Core Ops, SparseCore 0:
  64.7 78.6 all-gather.3
  170.6 77.6 all-gather.5
  329.7 147.5 all-gather.7
  667.1 74.5 reduce-scatter.8
  824.9 26.1 reduce-scatter.6
  853.2 58.8 reduce-scatter.4
  914.5 148.4 reduce-scatter.10

commit v2 on v1

v2 whole, which is shorter than its diff:
```python
import functools
import math

import jax
import jax.numpy as jnp
from jax import lax
from jax.experimental import pallas as pl
from jax.experimental.pallas import tpu as pltpu
from jax.sharding import PartitionSpec as P

HD = 128
ROT = 32
PARAMS = 50416912

EPS_NORM = 1e-05
EPS_ADAM = 1e-06
DECAY_WEIGHT = 0.01
RATE_MATRIX = 0.3
RATE_VECTOR = 0.25
BETA = 0.5
NEGATIVE = -1e30
COST_SCALE = 200e3

BF = jnp.bfloat16
F32 = jnp.float32
TURNS = (0, 2, 1, 3)


def dot(left, right):
    return jnp.dot(left, right, preferred_element_type=F32)


def dot_tn(left, right):
    return lax.dot_general(left, right, (((0,), (0,)), ((), ())), preferred_element_type=F32)


def dot_nt(left, right):
    return lax.dot_general(left, right, (((1,), (1,)), ((), ())), preferred_element_type=F32)


def standardise(values):
    centred = values - jnp.mean(values, axis=-1, keepdims=True)
    scale = lax.rsqrt(jnp.mean(centred * centred, axis=-1, keepdims=True) + EPS_NORM)
    return centred * scale, scale


def norm_back(grad_xhat, xhat, scale):
    return scale * (
        grad_xhat
        - jnp.mean(grad_xhat, axis=-1, keepdims=True)
        - xhat * jnp.mean(grad_xhat * xhat, axis=-1, keepdims=True)
    )


def gelu_both(values):
    phi = 0.5 * (1.0 + lax.erf(values * math.sqrt(0.5)))
    bell = jnp.exp(-0.5 * values * values) * (1.0 / math.sqrt(2.0 * math.pi))
    return values * phi, phi + values * bell


def after(value, *first):
    return lax.optimization_barrier((value, first))[0]


SMEM = pl.BlockSpec(memory_space=pltpu.SMEM)


def fixed(array):
    shape = array.shape
    return pl.BlockSpec(
        shape, lambda *_: (0,) * len(shape), pipeline_mode=pl.Buffered(1)
    )


def run(kernel, cost, grid, ins, outs, scratch=()):
    return pl.pallas_call(
        kernel,
        grid=grid,
        in_specs=[spec for _, spec in ins],
        out_specs=[spec for _, _, spec in outs],
        out_shape=[jax.ShapeDtypeStruct(shape, kind) for shape, kind, _ in outs],
        scratch_shapes=list(scratch),
        compiler_params=pltpu.CompilerParams(vmem_limit_bytes=56 * 1024 * 1024),
        cost_estimate=pl.CostEstimate(
            flops=1024, bytes_accessed=int(COST_SCALE * cost), transcendentals=0
        ),
    )(*(array for array, _ in ins))


class Order:
    def __init__(self, where_ref, outer, block, quarter):
        self.rank, self.y = where_ref[0], where_ref[1]
        self.outer, self.block, self.quarter = outer, block, quarter

    def relative(self, k):
        start = (((k % 2) ^ self.y) * self.outer + k // 2) * self.block
        return pl.ds(pl.multiple_of(start, self.block), self.block)

    def natural(self, k):
        return slice(k * self.block, (k + 1) * self.block)

    def blocks(self):
        return range(2 * self.outer)

    def quarter_of(self, d):
        start = (self.rank ^ TURNS[d]) * self.quarter
        return pl.ds(pl.multiple_of(start, self.quarter), self.quarter)


def mixing_forward_kernel(
    order, where, h, w_mix, gain, bias, mixer, streams, normed, coef_out, pre_out
):
    order = order(where)
    hist_len, rows, width = h.shape
    step = 512
    xhat, _ = standardise(h[hist_len - 1].astype(F32))
    mix_normed = (xhat * gain[0:1, :]).astype(BF)
    pre = dot_nt(mix_normed, w_mix[...])
    hidden = gelu_both(pre)[0].astype(BF)
    coef = dot(hidden, mixer[...])
    pre_out[...] = pre
    coef_out[...] = coef
    for start in range(0, width, step):
        lanes = slice(start, start + step)
        parts = [h[j, :, lanes].astype(F32) for j in range(hist_len)]
        for a in range(4):
            first = a * hist_len
            total = coef[:, first : first + 1] * parts[0]
            for j in range(1, hist_len):
                total = total + coef[:, first + j : first + j + 1] * parts[j]
            streams[a, :, lanes] = total
    for a in range(3):
        xhat, _ = standardise(streams[a])
        low = (xhat * gain[1:2, :] + bias[0:1, :]).astype(BF)
        for k in order.blocks():
            normed[a, :, order.relative(k)] = low[:, order.natural(k)]


def turn(values, cos_table, sin_table):
    half_width = ROT // 2
    lane = lax.broadcasted_iota(jnp.int32, values.shape, 1)
    partner = jnp.where(
        lane < half_width,
        pltpu.roll(values, HD - half_width, axis=1),
        pltpu.roll(values, half_width, axis=1),
    )
    return values * cos_table + partner * sin_table


def head_scores(query, key):
    seq_len = query.shape[0]
    scores = dot_nt(query, key) * (1.0 / math.sqrt(HD))
    row = lax.broadcasted_iota(jnp.int32, (seq_len, seq_len), 0)
    column = lax.broadcasted_iota(jnp.int32, (seq_len, seq_len), 1)
    scores = jnp.where(row >= column, scores, NEGATIVE)
    exponent = jnp.exp(scores - jnp.max(scores, axis=-1, keepdims=True))
    return exponent / jnp.sum(exponent, axis=-1, keepdims=True)


def attention_forward_kernel(*refs):
    normed, (own, other, cos, sin) = refs[:4], refs[4:8]
    attended, query_rot, key_rot, value, made, held, arrived = refs[8:]
    quarter = attended.shape[1]
    half = own.shape[0]
    seq_len = cos.shape[0]
    copies = [
        pltpu.make_async_copy(normed[d], held.at[d], arrived.at[d]) for d in range(4)
    ]
    for copy in copies:
        copy.start()
    cos_table, sin_table = cos[...], sin[...]
    for d in range(4):
        copies[d].wait()
        rows = slice(d * seq_len, (d + 1) * seq_len)
        for a in range(3):
            lanes = slice(a * quarter, (a + 1) * quarter)
            made[a] = dot(held[d, a, :, :half], own[:, lanes]) + dot(
                held[d, a, :, half:], other[:, lanes]
            )
        value[rows, :] = made[2].astype(BF)
        for head in range(quarter // HD):
            lanes = slice(head * HD, (head + 1) * HD)
            query = turn(made[0, :, lanes], cos_table, sin_table).astype(BF)
            key = turn(made[1, :, lanes], cos_table, sin_table).astype(BF)
            query_rot[rows, lanes] = query
            key_rot[rows, lanes] = key
            probs = head_scores(query, key).astype(BF)
            attended[rows, lanes] = dot(probs, value[rows, lanes]).astype(BF)


def attention_backward_kernel(q, k, v, g, own, other, cos, sin, grads, *backs):
    quarter = q.shape[1]
    half = own.shape[0]
    scale = 1.0 / math.sqrt(HD)
    cos_table, sin_table = cos[...], -sin[...]
    for head in range(quarter // HD):
        lanes = slice(head * HD, (head + 1) * HD)
        query, key, grad = q[:, lanes], k[:, lanes], g[:, lanes]
        probs = head_scores(query, key)
        grad_probs = dot_nt(grad, v[:, lanes])
        centre = jnp.sum(probs * grad_probs, axis=-1, keepdims=True)
        grad_scores = (probs * (grad_probs - centre)).astype(BF)
        grads[0, :, lanes] = turn(dot(grad_scores, key) * scale, cos_table, sin_table).astype(BF)
        grads[1, :, lanes] = turn(
            dot_tn(grad_scores, query) * scale, cos_table, sin_table
        ).astype(BF)
        grads[2, :, lanes] = dot_tn(probs.astype(BF), grad).astype(BF)

    def send(back):
        for a in range(3):
            columns = slice(a * quarter, (a + 1) * quarter)
            back[a, :, :half] = dot_nt(grads[a], own[:, columns]).astype(BF)
            back[a, :, half:] = dot_nt(grads[a], other[:, columns]).astype(BF)

    for step in range(2):
        pl.when(pl.program_id(0) == step)(functools.partial(send, backs[step]))


def residual_kernel(order, where, *refs):
    order = order(where)
    parts, weights = refs[:4], refs[4:12]
    stream, gain, bias, residual, normed, attended, natural = refs[12:]
    half = weights[0].shape[0]
    for d in range(4):
        natural[:, order.quarter_of(d)] = parts[d][...]
    for k in order.blocks():
        attended[:, order.relative(k)] = natural[:, order.natural(k)]
    for d in range(4):
        columns = order.quarter_of(d)
        residual[:, columns] = (
            stream[0, :, columns]
            + dot(attended[:, :half], weights[2 * d][...])
            + dot(attended[:, half:], weights[2 * d + 1][...])
        )
    xhat, _ = standardise(residual[...])
    low = (xhat * gain[2:3, :] + bias[1:2, :]).astype(BF)
    for k in order.blocks():
        normed[:, order.relative(k)] = low[:, order.natural(k)]


def up_kernel(*refs):
    rows, (own, other, activated, slope) = refs[:4], refs[4:]
    half = own.shape[0]
    seq_len = rows[0].shape[0]
    for d in range(4):
        up = dot(rows[d][:, :half], own[...]) + dot(rows[d][:, half:], other[...])
        active, back = gelu_both(up)
        activated[d * seq_len : (d + 1) * seq_len, :] = active.astype(BF)
        slope[d * seq_len : (d + 1) * seq_len, :] = back


def down_grad_kernel(activated, *refs):
    rows, out = refs[:4], refs[4]
    seq_len = rows[0].shape[0]
    total = dot_tn(activated[:seq_len, :], rows[0][...])
    for d in range(1, 4):
        total = total + dot_tn(activated[d * seq_len : (d + 1) * seq_len, :], rows[d][...])
    out[...] = total.astype(BF)


def hidden_back_kernel(*refs):
    rows, (weight, slope, out) = refs[:4], refs[4:]
    seq_len = rows[0].shape[0]
    for d in range(4):
        part = slice(d * seq_len, (d + 1) * seq_len)
        out[part, :] = (dot_nt(rows[d][...], weight[...]) * slope[part, :]).astype(BF)


def down_kernel(activated, weight, *outs):
    total = dot(activated[...], weight[...]).astype(BF)
    seq_len = outs[0].shape[0]
    for d in range(4):
        outs[d][...] = total[d * seq_len : (d + 1) * seq_len]


def up_grad_kernel(*refs):
    rows, (grad, out) = refs[:4], refs[4:]
    seq_len = rows[0].shape[0]
    total = dot_tn(rows[0][...], grad[:seq_len, :])
    for d in range(1, 4):
        total = total + dot_tn(rows[d][...], grad[d * seq_len : (d + 1) * seq_len, :])
    out[...] = total.astype(BF)


def normed_back_kernel(pair, grad, own, other, *outs):
    step, steps = pl.program_id(0), pl.num_programs(0)
    seq_len = outs[0].shape[0]

    def send(weight):
        for d, out in zip(pair, outs):
            rows = slice(d * seq_len, (d + 1) * seq_len)
            out[...] = dot_nt(grad[rows, :], weight[...]).astype(BF)

    pl.when(step < steps // 2)(functools.partial(send, own))
    pl.when(step >= steps // 2)(functools.partial(send, other))


def residual_back_kernel(order, where, *refs):
    order = order(where)
    residual, gain, mine, from_core, from_x, grad_out = refs[:6]
    weights = refs[6:14]
    grad, grad_gain, grad_bias = refs[14:17]
    parts, wide, low = refs[17:21], refs[21], refs[22]
    half = weights[0].shape[0]
    for k in order.blocks():
        source = order.relative(k)
        wide[:, order.natural(k)] = (
            mine[:, source].astype(F32)
            + from_core[:, source].astype(F32)
            + from_x[:, source].astype(F32)
        )
    xhat, scale = standardise(residual[...])
    grad_y = wide[...]
    grad_gain[...] = jnp.sum(grad_y * xhat, axis=0, keepdims=True)
    grad_bias[...] = jnp.sum(grad_y, axis=0, keepdims=True)
    grad_x = norm_back(grad_y * gain[2:3, :], xhat, scale)
    grad[...] = (grad_out[...].astype(F32) + grad_x).astype(BF)
    for s in range(2):
        total = dot_nt(grad[:, order.quarter_of(0)], weights[s][...])
        for d in range(1, 4):
            total = total + dot_nt(grad[:, order.quarter_of(d)], weights[2 * d + s][...])
        low[:, s * half : (s + 1) * half] = total.astype(BF)
    for k in order.blocks():
        wide[:, order.natural(k)] = low[:, order.relative(k)].astype(F32)
    for d in range(4):
        parts[d][...] = wide[:, order.quarter_of(d)].astype(BF)


def out_grad_kernel(order, where, attended, grad, *outs):
    order = order(where)
    for d in range(4):
        outs[d][...] = dot_tn(attended[...], grad[:, order.quarter_of(d)]).astype(BF)


def in_grad_kernel(*refs):
    normed, (even, odd, out) = refs[:4], refs[4:]
    seq_len = normed[0].shape[1]
    total = None
    for d in range(4):
        rows = slice(d // 2 * seq_len, (d // 2 + 1) * seq_len)
        part = dot_tn(normed[d][0], (odd if d % 2 else even)[0, rows, :])
        total = part if total is None else total + part
    out[...] = total.astype(BF)


def mixing_backward_kernel(order, where, *refs):
    order = order(where)
    h, streams, coef_in, pre_in, mine, from_core, from_x, grad_residual = refs[:8]
    w_mix, gain, mixer = refs[8:11]
    grad_history, grad_mix, grad_mixer, grad_gains, grad_bias = refs[11:16]
    grad_streams = refs[16]
    hist_len, rows, width = h.shape
    step = 512

    @pl.when(pl.program_id(0) == 0)
    def _():
        grad_mix[...] = jnp.zeros_like(grad_mix)
        grad_mixer[...] = jnp.zeros_like(grad_mixer)
        grad_gains[...] = jnp.zeros_like(grad_gains)
        grad_bias[...] = jnp.zeros_like(grad_bias)

    for a in range(3):
        for k in order.blocks():
            source = order.relative(k)
            grad_streams[a, :, order.natural(k)] = (
                mine[a, :, source].astype(F32)
                + from_core[a, :, source].astype(F32)
                + from_x[a, :, source].astype(F32)
            )
        xhat, scale = standardise(streams[a])
        grad_y = grad_streams[a]
        grad_gains[1:2, :] += jnp.sum(grad_y * xhat, axis=0, keepdims=True)
        grad_bias[...] += jnp.sum(grad_y, axis=0, keepdims=True)
        grad_streams[a] = norm_back(grad_y * gain[1:2, :], xhat, scale)
    grad_streams[3] = grad_residual[...].astype(F32)

    coef = coef_in[...]
    columns = coef.shape[1]
    sums = [jnp.zeros((rows, 128), F32) for _ in range(columns)]
    for start in range(0, width, step):
        lanes = slice(start, start + step)
        grads = [grad_streams[a, :, lanes] for a in range(4)]
        for j in range(hist_len):
            part = h[j, :, lanes].astype(F32)
            back = coef[:, j : j + 1] * grads[0]
            for a in range(1, 4):
                at = a * hist_len + j
                back = back + coef[:, at : at + 1] * grads[a]
            for a in range(4):
                product = grads[a] * part
                folded = product[:, 0:128]
                for lane in range(128, step, 128):
                    folded = folded + product[:, lane : lane + 128]
                sums[a * hist_len + j] = sums[a * hist_len + j] + folded
            if j < hist_len - 1:
                grad_history[j, :, lanes] = back.astype(BF)
            else:
                grad_streams[3, :, lanes] = back
    lane = lax.broadcasted_iota(jnp.int32, (rows, columns), 1)
    grad_coef = jnp.zeros((rows, columns), F32)
    for at in range(columns):
        grad_coef = jnp.where(lane == at, jnp.sum(sums[at], axis=-1, keepdims=True), grad_coef)
    grad_coef = grad_coef.astype(BF)
    hidden, slope = gelu_both(pre_in[...])
    hidden = hidden.astype(BF)
    grad_mixer[...] += dot_tn(hidden, grad_coef)
    grad_pre = (dot_nt(grad_coef, mixer[...]) * slope).astype(BF)
    xhat, scale = standardise(h[hist_len - 1].astype(F32))
    grad_mix[...] += dot_tn(grad_pre, (xhat * gain[0:1, :]).astype(BF))
    grad_y = dot(grad_pre, w_mix[...])
    grad_gains[0:1, :] += jnp.sum(grad_y * xhat, axis=0, keepdims=True)
    grad_current = norm_back(grad_y * gain[0:1, :], xhat, scale)
    grad_history[hist_len - 1] = (grad_streams[3] + grad_current).astype(BF)


def rotary_tables(seq_len):
    half_width = ROT // 2
    frequency = 10000.0 ** (-(2.0 * jnp.arange(half_width, dtype=F32)) / ROT)
    angles = jnp.arange(seq_len, dtype=F32)[:, None] * frequency[None, :]
    cosine, sine = jnp.cos(angles), jnp.sin(angles)
    rest = HD - ROT
    cos_table = jnp.concatenate([cosine, cosine, jnp.ones((seq_len, rest), F32)], axis=1)
    sin_table = jnp.concatenate([-sine, sine, jnp.zeros((seq_len, rest), F32)], axis=1)
    return cos_table, sin_table


def moments_kernel(clip_ref, *refs):
    clip = clip_ref[0]
    step = 512

    @pl.when(pl.program_id(0) == 0)
    def _():
        for member in range(4):
            refs[24][member] = 0.0

    for member in range(4):
        grad, first, second, weight = refs[4 * member : 4 * member + 4]
        first_out, second_out = refs[16 + 2 * member : 18 + 2 * member]
        total = 0.0
        for start in range(0, grad.shape[1], step):
            lanes = slice(start, start + step)
            scaled = grad[:, lanes].astype(F32) * clip
            first_new = BETA * first[:, lanes] + (1.0 - BETA) * scaled
            second_new = BETA * second[:, lanes] + (1.0 - BETA) * scaled * scaled
            first_out[:, lanes] = first_new
            second_out[:, lanes] = second_new
            change = first_new / (jnp.sqrt(second_new) + EPS_ADAM) + DECAY_WEIGHT * weight[:, lanes]
            total = total + jnp.sum(change * change, axis=0, keepdims=True)
        refs[24][member] = refs[24][member] + jnp.sum(total)


def apply_kernel(trust_ref, *refs):
    step = 512
    for member in range(4):
        first, second, weight = refs[3 * member : 3 * member + 3]
        out, low = refs[12 + 2 * member : 14 + 2 * member]
        rate = RATE_MATRIX * trust_ref[member]
        for start in range(0, weight.shape[1], step):
            lanes = slice(start, start + step)
            old = weight[:, lanes]
            change = first[:, lanes] / (jnp.sqrt(second[:, lanes]) + EPS_ADAM) + DECAY_WEIGHT * old
            new = old - rate * change
            out[:, lanes] = new
            low[:, lanes] = new.astype(BF)


class Links:
    def __init__(self, devices, width):
        self.devices = devices
        index = lax.axis_index("dp")
        self.core = index & 1
        self.x = (index >> 1) & 1
        self.rank = index & 3
        self.index = index
        self.y_bit = 2
        self.block = 4 * width // devices
        while self.block % 128:
            self.y_bit += 1
            self.block *= 2
        self.inner = 1 << (self.y_bit - 2)
        self.outer = width // (2 * self.block)
        self.y = (index >> self.y_bit) & 1
        self.where = jnp.stack([self.rank, self.y]).astype(jnp.int32)
        groups = {}
        for j in range(devices):
            groups.setdefault((j & 3, (j >> self.y_bit) & 1), []).append(j)
        self.z_groups = list(groups.values())

    def swap(self, value, bit):
        return lax.ppermute(value, "dp", [(j, j ^ bit) for j in range(self.devices)])

    def swap_core(self, value):
        return self.swap(value, 1)

    def swap_x(self, value):
        return self.swap(value, 2)

    def swap_y(self, value):
        return self.swap(value, 1 << self.y_bit)

    def gather(self, value, groups):
        return lax.all_gather(value, "dp", axis=0, tiled=True, axis_index_groups=groups)

    def reduce(self, value, groups):
        return lax.psum_scatter(
            value, "dp", scatter_dimension=0, tiled=True, axis_index_groups=groups
        )

    def total(self, value):
        bit = 1
        while bit < self.devices:
            pair = value + self.swap(value, bit)
            if 2 * bit < self.devices:
                pair = pair + (self.swap(value, 2 * bit) + self.swap(value, 3 * bit))
            value = pair
            bit *= 4
        return value

    def to_absolute(self, parts):
        own, across_x, across_core, across_both = parts
        low_x = self.x == 0
        core_own = (jnp.where(low_x, own, across_x), jnp.where(low_x, across_x, own))
        core_other = (
            jnp.where(low_x, across_core, across_both),
            jnp.where(low_x, across_both, across_core),
        )
        low_core = self.core == 0
        ordered = []
        for mine, other in zip(core_own, core_other):
            ordered.append(jnp.where(low_core, mine, other))
            ordered.append(jnp.where(low_core, other, mine))
        return ordered

    def to_relative(self, parts):
        low_x, low_core = self.x == 0, self.core == 0
        near = [jnp.where(low_x, parts[c], parts[2 + c]) for c in (0, 1)]
        far = [jnp.where(low_x, parts[2 + c], parts[c]) for c in (0, 1)]
        return [
            jnp.where(low_core, near[0], near[1]),
            jnp.where(low_core, far[0], far[1]),
            jnp.where(low_core, near[1], near[0]),
            jnp.where(low_core, far[1], far[0]),
        ]

    def group_gather(self, value):
        across_x = self.swap_x(value)
        return [value, across_x, self.swap_core(value), self.swap_core(across_x)]

    def group_exchange(self, parts):
        own, for_x, for_core, for_both = parts
        from_both = self.swap_x(for_both)
        from_x = self.swap_x(for_x)
        return [own, from_x, self.swap_core(for_core), self.swap_core(from_both)]

    def group_reduce(self, own, for_x, for_core, for_both, *ties):
        from_both = self.swap_core(for_both)
        for_x = (for_x.astype(F32) + from_both.astype(F32)).astype(BF)
        return self.swap_core(for_core), self.swap_x(after(for_x, *ties)), for_x


def program(
    devices,
    history,
    d_out,
    group_ids,
    group_weight,
    attn_in,
    attn_out,
    ffn_up,
    ffn_down,
    mixer_in,
    mixer_out,
    norm_gain,
    norm_bias,
    first_attn_in,
    second_attn_in,
    first_attn_out,
    second_attn_out,
    first_ffn_up,
    second_ffn_up,
    first_ffn_down,
    second_ffn_down,
    first_mixer_in,
    second_mixer_in,
    first_mixer_out,
    second_mixer_out,
    first_norm_gain,
    second_norm_gain,
    first_norm_bias,
    second_norm_bias,
):
    hist_len, seq_len, width = history.shape
    links = Links(devices, width)
    order = functools.partial(
        Order, outer=links.outer, block=links.block, quarter=width // 4
    )
    with_order = lambda kernel: functools.partial(kernel, order)
    where = (links.where, SMEM)
    quarter, half = width // 4, width // 2
    rows = width // devices
    hidden = ffn_down.shape[0] * devices
    units = hidden // devices
    share = hidden // 4
    four = 4 * seq_len
    whole = lambda array: (array, fixed(array))

    low_attn = attn_in.astype(BF).reshape(rows, 3, 4, quarter)
    low_out = attn_out.astype(BF).reshape(rows, 1, 4, quarter)
    by_rank = jnp.concatenate([low_attn, low_out], axis=1)
    by_rank = [by_rank[:, :, r].reshape(rows, width) for r in range(4)]
    attn_parts = links.group_exchange(links.to_relative(by_rank))
    attn_block = jnp.concatenate(links.to_absolute(attn_parts), axis=0)

    low_up = ffn_up.astype(BF).reshape(rows, links.outer, 2, links.inner, 4, units)
    low_up = jnp.transpose(low_up, (4, 0, 1, 3, 2, 5)).reshape(4, rows, share)
    own, for_x, for_core, for_both = after(links.to_relative(list(low_up)), attn_parts[1])
    from_both = after(links.swap_x(for_both), attn_block)
    up_parts = [own, links.swap_x(for_x), links.swap_core(for_core), links.swap_core(from_both)]
    up_block = jnp.concatenate(links.to_absolute(up_parts), axis=0)

    low_down = ffn_down.astype(BF)
    other_down = links.swap_y(low_down)
    low_y = links.y == 0

    attn_own = links.gather(attn_block, links.z_groups)
    attn_other = links.swap_y(attn_own)
    up_own = links.gather(up_block, links.z_groups)
    up_other = links.swap_y(up_own)

    hidden_mix = mixer_in.shape[1]
    pack = jnp.concatenate([mixer_in.T, norm_gain, norm_bias], axis=0).astype(BF)
    bit = 1
    while bit < devices:
        other = links.swap(pack, bit)
        low = (links.index & bit) == 0
        pack = jnp.concatenate([jnp.where(low, pack, other), jnp.where(low, other, pack)], axis=1)
        bit *= 2
    w_mixer_in = pack[:hidden_mix]
    gain_table = pack[hidden_mix : hidden_mix + 3].astype(F32)
    bias_table = pack[hidden_mix + 3 :].astype(F32)
    mixer_low = mixer_out.astype(BF)

    tile = 64
    steps = (seq_len // tile,)
    columns = mixer_out.shape[1]
    row_tile = lambda *lead: pl.BlockSpec(
        lead + (tile, width), lambda t: (0,) * len(lead) + (t, 0)
    )
    narrow = pl.BlockSpec((tile, columns), lambda t: (t, 0))
    pre_narrow = pl.BlockSpec((tile, hidden_mix), lambda t: (t, 0))
    streams, normed, coef, mix_pre = run(
        with_order(mixing_forward_kernel),
        14,
        steps,
        [
            where,
            (history, row_tile(hist_len)),
            whole(w_mixer_in),
            whole(gain_table),
            whole(bias_table),
            whole(mixer_low),
        ],
        [
            ((4, seq_len, width), F32, row_tile(4)),
            ((3, seq_len, width), BF, row_tile(3)),
            ((seq_len, columns), F32, narrow),
            ((seq_len, hidden_mix), F32, pre_narrow),
        ],
    )

    low_down, other_down = after((low_down, other_down), normed)
    down_block = jnp.concatenate(
        [jnp.where(low_y, low_down, other_down), jnp.where(low_y, other_down, low_down)], axis=0
    )
    w_down = links.gather(down_block, links.z_groups)

    tables = [whole(table) for table in rotary_tables(seq_len)]
    normed_four = links.group_gather(normed)
    attn_weights = [
        (
            array,
            pl.BlockSpec((half, 3 * quarter), lambda s: (0, 0), pipeline_mode=pl.Buffered(1)),
        )
        for array in (attn_own, attn_other)
    ]
    out_mine = [array[:, 3 * quarter :] for array in (attn_own, attn_other)]
    out_x = [links.swap_x(array) for array in out_mine]
    group_count = group_weight.shape[0]
    seq_weight = jnp.sum(
        jnp.where(jnp.arange(group_count, dtype=jnp.int32) == group_ids[0], group_weight, 0.0)
    )
    grad_out = (d_out.astype(F32) * seq_weight).astype(BF)
    grad_out = after(grad_out, normed_four[1])
    grad_out_x = links.swap_x(grad_out)
    seq_block = pl.BlockSpec((seq_len, quarter), lambda s: (s, 0))
    attn_other_now = after(attn_other, grad_out_x)
    anywhere = pl.BlockSpec(memory_space=pl.ANY)
    four_quarter = pl.BlockSpec((four, quarter), lambda _: (0, 0))
    attended, query_rot, key_rot, value = run(
        attention_forward_kernel,
        16,
        (1,),
        [(part, anywhere) for part in normed_four]
        + [(attn_own, attn_weights[0][1]), (attn_other_now, attn_weights[0][1])]
        + tables,
        [((four, quarter), BF, four_quarter)] * 4,
        [
            pltpu.VMEM((3, seq_len, quarter), F32),
            pltpu.VMEM((4, 3, seq_len, width), BF),
            pltpu.SemaphoreType.DMA((4,)),
        ],
    )
    out_x = after(out_x, attended)
    out_halves = [
        [out_mine[k], out_x[k], links.swap_core(out_mine[k]), links.swap_core(out_x[k])]
        for k in range(2)
    ]
    w_out = [out_halves[k][d] for d in range(4) for k in range(2)]
    attended = links.group_exchange(
        [attended[d * seq_len : (d + 1) * seq_len] for d in range(4)]
    )
    one_row = ((1, width), F32, pl.BlockSpec((1, width), lambda *_: (0, 0)))
    full = lambda kind: (
        (seq_len, width),
        kind,
        pl.BlockSpec((seq_len, width), lambda *_: (0, 0)),
    )
    residual, ffn_normed, attended_rel = run(
        with_order(residual_kernel),
        9,
        (1,),
        [where]
        + [whole(part) for part in attended]
        + [whole(part) for part in w_out]
        + [
            (
                streams,
                pl.BlockSpec(
                    (1, seq_len, width), lambda _: (3, 0, 0), pipeline_mode=pl.Buffered(1)
                ),
            ),
            whole(gain_table),
            whole(bias_table),
        ],
        [full(F32), full(BF), full(BF)],
        [pltpu.VMEM((seq_len, width), BF)],
    )

    ffn_four = links.group_gather(ffn_normed)
    wide = 256
    column_tile = lambda count: pl.BlockSpec((count, wide), lambda t: (0, t))
    line_tile = lambda count: pl.BlockSpec((wide, count), lambda t: (t, 0))
    activated, slope = run(
        up_kernel,
        17,
        (share // wide,),
        [whole(part) for part in ffn_four]
        + [(up_own, column_tile(half)), (up_other, column_tile(half))],
        [((four, share), BF, column_tile(four)), ((four, share), F32, column_tile(four))],
    )

    grad_out_x = after(grad_out_x, activated)
    grad_out_four = [
        grad_out,
        grad_out_x,
        links.swap_core(grad_out),
        links.swap_core(grad_out_x),
    ]

    (grad_down,) = run(
        down_grad_kernel,
        14,
        (share // wide,),
        [(activated, column_tile(four))] + [whole(part) for part in grad_out_four],
        [((share, width), BF, line_tile(width))],
    )
    down_sums = links.reduce(grad_down, links.z_groups)

    (grad_up,) = run(
        hidden_back_kernel,
        16,
        (share // wide,),
        [whole(part) for part in grad_out_four]
        + [(w_down, line_tile(width)), (after(slope, grad_down), column_tile(four))],
        [((four, share), BF, column_tile(four))],
    )

    def whole_rows(block):
        parts = list(block.reshape(4, rows, block.shape[1]))
        parts = links.to_absolute(links.group_exchange(links.to_relative(parts)))
        return jnp.stack(parts, axis=1)

    tiles = half // wide

    def normed_back(pair, grad):
        return run(
            functools.partial(normed_back_kernel, pair),
            11,
            (2 * tiles,),
            [
                whole(grad),
                (up_own, pl.BlockSpec((wide, share), lambda t: (jnp.minimum(t, tiles - 1), 0))),
                (up_other, pl.BlockSpec((wide, share), lambda t: (jnp.maximum(t - tiles, 0), 0))),
            ],
            [((seq_len, width), BF, column_tile(seq_len))] * 2,
        )

    def up_grad(first, count, grad):
        block = pl.BlockSpec((seq_len, wide), lambda t: (0, first + t))
        (out,) = run(
            up_grad_kernel,
            9,
            (count,),
            [(part, block) for part in ffn_four] + [whole(grad)],
            [((count * wide, share), BF, line_tile(share))],
        )
        return out

    for_x, for_both = normed_back((1, 3), grad_up)
    up_first = up_grad(tiles, 1, after(grad_up, for_both))
    up_theirs_first = links.swap_y(up_first)
    up_rest = up_grad(tiles + 1, tiles - 1, after(grad_up, up_first))
    up_theirs_rest = links.swap_y(up_rest)
    own, for_core = normed_back((0, 2), after(grad_up, up_rest))
    up_grad_own = up_grad(0, tiles, after(grad_up, own))
    from_core, from_x, _ = links.group_reduce(own, for_x, for_core, for_both)
    from_x = after(from_x, up_grad_own, up_theirs_first)
    part_out = ((seq_len, quarter), BF, pl.BlockSpec((seq_len, quarter), lambda _: (0, 0)))
    back = run(
        with_order(residual_back_kernel),
        11,
        (1,),
        [
            where,
            whole(residual),
            whole(gain_table),
            whole(own),
            whole(from_core),
            whole(from_x),
            whole(grad_out),
        ]
        + [whole(part) for part in w_out],
        [full(BF), one_row, one_row] + [part_out] * 4,
        [pltpu.VMEM((seq_len, width), F32), pltpu.VMEM((seq_len, width), BF)],
    )
    grad_residual, grad_gain_ffn, grad_bias_ffn = back[:3]

    heads_own, for_x, for_core, for_both = back[3:]
    from_both, from_x = links.swap_x(for_both), links.swap_x(for_x)
    grad_heads = [
        heads_own,
        from_x,
        links.swap_core(for_core),
        links.swap_core(from_both),
    ]

    line = 512
    out_parts = run(
        with_order(out_grad_kernel),
        7,
        (width // line,),
        [
            where,
            (attended_rel, pl.BlockSpec((seq_len, line), lambda t: (0, t))),
            whole(grad_residual),
        ],
        [((width, quarter), BF, pl.BlockSpec((line, quarter), lambda t: (t, 0)))] * 4,
    )
    out_parts = after(out_parts, from_x, from_both)
    out_both, out_core = links.swap_core(out_parts[3]), links.swap_core(out_parts[2])

    def attention_back(first, *ties):
        heads = jnp.concatenate([grad_heads[first], grad_heads[first + 2]], axis=0)
        block = pl.BlockSpec((seq_len, quarter), lambda s: (first + 2 * s, 0))
        back_out = (
            (3, seq_len, width),
            BF,
            pl.BlockSpec((3, seq_len, width), lambda s: (0, 0, 0)),
        )
        return run(
            attention_backward_kernel,
            15,
            (2,),
            [(query_rot, block), (key_rot, block), (value, block)]
            + [(after(heads, *ties), seq_block)]
            + attn_weights
            + tables,
            [
                (
                    (3, 2 * seq_len, quarter),
                    BF,
                    pl.BlockSpec((3, seq_len, quarter), lambda s: (0, s, 0)),
                ),
                back_out,
                back_out,
            ],
        )

    plus = lambda mine, theirs: (mine.astype(F32) + theirs.astype(F32)).astype(BF)
    proj_odd, for_x, for_both = attention_back(1)
    out_for_x = plus(out_parts[1], after(out_both, for_both))
    out_x = links.swap_x(out_for_x)
    proj_even, own, for_core = attention_back(0, out_for_x)
    from_core, from_x, for_x = links.group_reduce(own, for_x, for_core, for_both)
    proj_even = after(proj_even, for_x)

    def in_grad(s, proj):
        block = pl.BlockSpec((1, seq_len, wide), lambda a, t: (a, 0, s * tiles + t))
        proj_block = pl.BlockSpec((1, 2 * seq_len, quarter), lambda a, t: (a, 0, 0))
        (out,) = run(
            in_grad_kernel,
            12,
            (3, tiles),
            [(part, block) for part in normed_four] + [(proj, proj_block), (proj_odd, proj_block)],
            [((half, 3 * quarter), BF, pl.BlockSpec((wide, quarter), lambda a, t: (t, a)))],
        )
        return out

    in_grad_other = in_grad(1, proj_even)
    in_theirs = links.swap_y(in_grad_other)
    in_grad_own = in_grad(0, after(proj_even, in_grad_other))

    up_theirs = jnp.concatenate(
        [up_theirs_first, after(up_theirs_rest, in_grad_own, out_x)]
    )
    up_both = after(plus(up_grad_own, up_theirs), down_sums)
    up_sums = links.reduce(up_both, links.z_groups)
    out_x = after(out_x, up_both)
    out_grad = out_parts[0].astype(F32) + out_core.astype(F32) + out_x.astype(F32)
    out_theirs = links.swap_y(out_grad[half:].astype(BF))
    down_parts = run(
        down_kernel,
        14,
        (width // wide,),
        [whole(after(activated, up_both)), (w_down, column_tile(share))],
        [((seq_len, width), BF, column_tile(seq_len))] * 4,
    )
    down_core, down_x, down_for_x = links.group_reduce(*down_parts, from_x)
    out_state = (
        residual + down_parts[0].astype(F32) + down_core.astype(F32) + down_x.astype(F32)
    ).astype(BF)

    in_theirs = after(in_theirs, down_for_x)
    attn_both = jnp.concatenate(
        [plus(in_grad_own, in_theirs), plus(out_grad[:half], out_theirs)], axis=1
    )
    attn_both = after(attn_both, up_sums, from_x, from_core)
    attn_sums = links.reduce(attn_both, links.z_groups)

    fixed_out = lambda shape: (
        shape,
        F32,
        pl.BlockSpec(shape, lambda t: (0, 0)),
    )
    grad_history, grad_mixer_in, grad_mixer_out, grad_gains, grad_bias_attn = run(
        with_order(mixing_backward_kernel),
        25,
        steps,
        [
            where,
            (history, row_tile(hist_len)),
            (streams, row_tile(3)),
            (coef, narrow),
            (mix_pre, pre_narrow),
            (own, row_tile(3)),
            (from_core, row_tile(3)),
            (from_x, row_tile(3)),
            (after(grad_residual, attn_both), row_tile()),
            whole(w_mixer_in),
            whole(gain_table),
            whole(mixer_low),
        ],
        [
            ((hist_len, seq_len, width), BF, row_tile(hist_len)),
            fixed_out((hidden_mix, width)),
            fixed_out((hidden_mix, columns)),
            fixed_out((2, width)),
            fixed_out((1, width)),
        ],
        [pltpu.VMEM((4, tile, width), F32)],
    )

    down_sums, up_sums = after(down_sums, attn_both), after(up_sums, attn_both)
    down_sums = down_sums.reshape(2, units, width)
    down_mine = jnp.where(low_y, down_sums[0], down_sums[1])
    down_theirs = jnp.where(low_y, down_sums[1], down_sums[0])
    shard_down = down_mine.astype(F32) + links.swap_y(down_theirs).astype(F32)
    shard_up = jnp.transpose(
        whole_rows(up_sums).reshape(rows, 4, links.outer, links.inner, 2, units),
        (0, 2, 4, 3, 1, 5),
    ).reshape(rows, hidden)

    small = jnp.concatenate(
        [grad_mixer_in, grad_gains, grad_gain_ffn, grad_bias_attn, grad_bias_ffn], axis=0
    )
    small = after(small, shard_up, shard_down, down_x)
    bits = [links.y_bit] + [k for k in reversed(range(2, devices.bit_length() - 1)) if k != links.y_bit]
    pieces = small.reshape((small.shape[0],) + (2,) * (devices.bit_length() - 3) + (4 * rows,))
    left = list(reversed(range(2, devices.bit_length() - 1)))
    for k in bits:
        axis = 1 + left.index(k)
        left.remove(k)
        low = (links.index & (1 << k)) == 0
        first = lax.index_in_dim(pieces, 0, axis, keepdims=False)
        second = lax.index_in_dim(pieces, 1, axis, keepdims=False)
        pieces = jnp.where(low, first, second) + links.swap(
            jnp.where(low, second, first), 1 << k
        )
    small = pieces
    small = small + links.swap_x(small)
    small = small + links.swap_core(small)
    small = lax.dynamic_slice_in_dim(small, links.rank * rows, rows, axis=1)
    mixer_grad = links.total(grad_mixer_out)
    square = lambda array: jnp.sum(jnp.square(array.astype(F32)))
    early_squares = square(up_sums) + square(shard_down) + square(small)
    early_squares = early_squares + square(mixer_grad) / devices
    attn_sums = after(attn_sums, shard_up, early_squares)
    attn_rows = whole_rows(attn_sums).reshape(rows, 4, 4, quarter)
    attn_rows = jnp.transpose(attn_rows, (0, 2, 1, 3)).reshape(rows, 4 * width)
    shard_in, shard_out = attn_rows[:, : 3 * width], attn_rows[:, 3 * width :]
    grads = (
        shard_in,
        shard_out,
        shard_up,
        shard_down,
        small[:hidden_mix].T,
        mixer_grad,
        small[hidden_mix : hidden_mix + 3],
        small[hidden_mix + 3 :],
    )

    weights = (attn_in, attn_out, ffn_up, ffn_down, mixer_in, mixer_out, norm_gain, norm_bias)
    firsts = (
        first_attn_in,
        first_attn_out,
        first_ffn_up,
        first_ffn_down,
        first_mixer_in,
        first_mixer_out,
        first_norm_gain,
        first_norm_bias,
    )
    seconds = (
        second_attn_in,
        second_attn_out,
        second_ffn_up,
        second_ffn_down,
        second_mixer_in,
        second_mixer_out,
        second_norm_gain,
        second_norm_bias,
    )

    def portion(member, amount):
        return amount / devices if member == 5 else amount

    weights_later = after(weights, coef)
    local_squares = early_squares + square(attn_sums)
    local_weight_sq = [portion(member, square(weights_later[member])) for member in range(6)]
    sums = links.total(jnp.stack([local_squares] + local_weight_sq))
    squares, weight_sq = sums[0], sums[1:]
    global_norm = jnp.sqrt(squares)
    clip = 0.3 * math.sqrt(PARAMS) / (global_norm + 1e-06)
    parts = rows // 16
    slab = lambda array: pl.BlockSpec(
        (array.shape[0] // parts, array.shape[1]), lambda t: (t, 0)
    )
    slabs = lambda *arrays: [(array, slab(array)) for array in arrays]
    made = lambda array, kind: (array.shape, kind, slab(array))
    ins, outs = [(clip[None], SMEM)], []
    for member in range(4):
        ins += slabs(grads[member], firsts[member], seconds[member], weights[member])
        outs += [made(weights[member], F32)] * 2
    outs.append(((4,), F32, SMEM))
    moments = run(moments_kernel, 14, (parts,), ins, outs)
    firsts_new, seconds_new = list(moments[0:8:2]), list(moments[1:8:2])
    local_update_sq = moments[8]
    steps_small = []
    for member in range(4, 8):
        scaled = grads[member] * clip
        first_new = BETA * firsts[member] + (1.0 - BETA) * scaled
        second_new = BETA * seconds[member] + (1.0 - BETA) * scaled * scaled
        step_value = first_new / (jnp.sqrt(second_new) + EPS_ADAM)
        if member < 6:
            step_value = step_value + DECAY_WEIGHT * weights[member]
        firsts_new.append(first_new)
        seconds_new.append(second_new)
        steps_small.append(step_value)
    small_sq = [portion(4 + k, jnp.sum(steps_small[k] * steps_small[k])) for k in range(2)]
    update_sq = links.total(jnp.concatenate([local_update_sq, jnp.stack(small_sq)]))
    weight_norm = jnp.sqrt(weight_sq)
    update_norm = jnp.sqrt(update_sq)
    trust = weight_norm / (update_norm + 1e-06)
    lamb_stats = jnp.stack([weight_norm, update_norm, trust], axis=1)
    ins, outs = [(trust, SMEM)], []
    for member in range(4):
        ins += slabs(firsts_new[member], seconds_new[member], weights[member])
        outs += [made(weights[member], F32), made(weights[member], BF)]
    applied = run(apply_kernel, 10, (parts,), ins, outs)
    results = []
    for member in range(8):
        if member < 4:
            updated, low = applied[2 * member], applied[2 * member + 1]
        else:
            rate = RATE_MATRIX * trust[member] if member < 6 else RATE_VECTOR
            updated = weights[member] - rate * steps_small[member - 4]
            low = updated.astype(BF)
        results += [updated, low, firsts_new[member], seconds_new[member]]
    return (out_state, grad_history, global_norm, lamb_stats, *results)


def solution(mesh):
    rows, columns, whole = P("dp", None), P(None, "dp"), P()
    middle = P(None, "dp", None)
    matrices = (rows,) * 5 + (whole,) + (columns,) * 2
    moments = tuple(spec for spec in matrices for _ in range(2))
    results = tuple(spec for spec in matrices for _ in range(4))
    return jax.shard_map(
        functools.partial(program, mesh.shape["dp"]),
        mesh=mesh,
        in_specs=(middle, rows, P("dp"), whole) + matrices + moments,
        out_specs=(rows, middle, whole, whole) + results,
        check_vma=False,
    )
```

time: 1250 us -> 826 us (0.66)
  Pallas kernels: 25.5 us -> 278 us
  local copies, waits for them, and re-layouts: 244 us -> 38.1 us
  other arithmetic: 275 us -> 80.2 us
  matrix products: 167 us -> 0 us
  waiting for transfers between devices: 438 us -> 331 us
    pallas_call x2 -> x21, Pallas kernels: 25.5 us -> 278 us  [run(): pl.pallas_call(kernel, grid=grid, in_specs=[spec for _, spec in ins], out...]
    dot_general x45 -> x0, matrix products: 167 us -> none  [the longest x15 63.2 us: dot_nt(): lax.dot_general(left, right, (((1,), (1,)), ((), ())), preferred_element_...]
    ppermute x66 -> x90, waiting for transfers between devices: 426 us -> 313 us  [swap(): lax.ppermute(value, 'dp', [(j, j ^ bit) for j in range(self.devices)])]
    reduce_sum x37 -> x13, other arithmetic: 99.4 us -> 17.3 us  [the longest x11 16.1 us: program(): square = lambda array: jnp.sum(jnp.square(array.astype(F32)))]
    concatenate x38 -> x1, local copies, waits for them, and re-layouts: 72.2 us -> 1.82 us  [program(): jnp.concatenate([grad_mixer_in, grad_gains, grad_gain_ffn, grad_bias_attn...]
    unnamed x549 -> x104, local copies, waits for them, and re-layouts: 58.3 us -> 8.08 us
    another operation x35 -> x3, other arithmetic: 39.5 us -> 0.6 us  [the longest x1 0.59 us: __init__(): self.where = jnp.stack([self.rank, self.y]).astype(jnp.int32)]
    select_n x8 -> x1, local copies, waits for them, and re-layouts: 22.8 us -> 0.18 us  [to_relative(): jnp.where(low_core, near[0], near[1])]
  transfers between devices with their start and end apart: 79 -> 96, of which waited for: 40 -> 48; matrix products, arithmetic and copies ran while one was open for 43% -> 10% of each run, Pallas kernels for 2% -> 31%
where the time goes in v2:
time: 826 us; the launch traced here: 817 us
  waiting for transfers between devices  331 us (40%)
  Pallas kernels  278 us (34%)
  other arithmetic  80.2 us (10%)
  starting transfers between devices  66.2 us (8%)
  local copies, waits for them, and re-layouts  38.1 us (5%)
  between operations  23.3 us (3%)
    ppermute x90, waiting for transfers between devices, swap(): lax.ppermute(value, 'dp', [(j, j ^ bit) for j in range(self.devices)])  313 us
    pallas_call x21, Pallas kernels, run(): pl.pallas_call(kernel, grid=grid, in_specs=[spec for _, spec in ins], out...  278 us
    ppermute x90, starting transfers between devices, swap(): lax.ppermute(value, 'dp', [(j, j ^ bit) for j in range(self.devices)])  65.7 us
    all_gather x3, waiting for transfers between devices, gather(): lax.all_gather(value, 'dp', axis=0, tiled=True, axis_index_groups=groups)  17.9 us
  transfers between devices with their start and end apart: 96, of which 48 were waited for; matrix products, arithmetic and copies ran while one was open for 10% of the time, Pallas kernels for 31%

profile of v2, /device:TPU:0, one launch (start us, length us, event | category | flops | bytes accessed | tf_op | source)
XLA Modules:
  0.0 816.6 jit_solution(9739498145944110960)
XLA Ops:
  69.9 11.5 %collective-permute-done.4 = bf16[41,1024]{1,0:T(8,128)(2,1)S(1)} collective-permute-done((bf16[41,1024]{1,0:T(8,128)(2,1)S(1)}, bf16[41,1024]{1,0:T(8,128)(2,1)S(1)}, u32[]{:S(2)}, u32[]{:S(2)}) %collective-permute-start.4) | collective-permute-done | bytes 84000 | tf_op jit(solution)/shard_map/ppermute | solution.py:490
  83.4 14.2 %shard_map.547 = (f32[4,256,2048]{2,1,0:T(8,128)}, bf16[3,256,2048]{2,1,0:T(8,128)(2,1)}, f32[256,36]{1,0:T(8,128)}, f32[256,36]{1,0:T(8,128)}) custom-call(s32[2]{0:T(128)} %pad_add_fusion.where, bf16[9,256,2048]{2,1,0:T(8,128)(2,1)} %refs_0_.1, bf16[36,2048]{1,0:T(8,128)(2,1)} %fusion.7.w_mix.refs_8_, f32[3,2048]{1,0:T(4,128)} %fusion.15.gain.refs_13_.refs_1_.refs_9_, ...), custom_call_target="tpu_custom_call" | custom-call | flops 1024 | bytes 2800000 | tf_op jit(solution)/shard_map/pallas_call | solution.py:76
  102.3 14.2 %all-gather.4.cloned.1.call-done.refs_4_.own = bf16[1024,2048]{1,0:T(8,128)(2,1)} async-done(((bf16[256,2048]{1,0:T(8,128)(2,1)}), bf16[1024,2048]{1,0:T(8,128)(2,1)}) %all-gather.4.cloned.1.call-update) | async-done | bytes 4194320 | tf_op jit(solution)/shard_map/all_gather | solution.py:502
  118.0 51.3 %collective-permute-done.5.refs_1_ = bf16[3,256,2048]{2,1,0:T(8,128)(2,1)} collective-permute-done((bf16[3,256,2048]{2,1,0:T(8,128)(2,1)}, bf16[3,256,2048]{2,1,0:T(8,128)(2,1)}, u32[]{:S(2)}, u32[]{:S(2)}) %collective-permute-start.5) | collective-permute-done | bytes 3145760 | tf_op jit(solution)/shard_map/ppermute | solution.py:490
  177.0 32.0 %collective-permute-done.12.refs_5_.other = bf16[1024,2048]{1,0:T(8,128)(2,1)S(1)} collective-permute-done((bf16[1024,2048]{1,0:T(8,128)(2,1)}, bf16[1024,2048]{1,0:T(8,128)(2,1)S(1)}, u32[]{:S(2)}, u32[]{:S(2)}) %collective-permute-start.12) | collective-permute-done | bytes 4194336 | tf_op jit(solution)/shard_map/ppermute | solution.py:490
  216.8 16.2 %shard_map.548 = (bf16[1024,512]{1,0:T(8,128)(2,1)}, bf16[1024,512]{1,0:T(8,128)(2,1)}, bf16[1024,512]{1,0:T(8,128)(2,1)}, bf16[1024,512]{1,0:T(8,128)(2,1)}) custom-call(bf16[3,256,2048]{2,1,0:T(8,128)(2,1)} %get-tuple-element.140.refs_0_, bf16[3,256,2048]{2,1,0:T(8,128)(2,1)} %collective-permute-done.5.refs_1_, ...), custom_call_target="tpu_custom_call" | custom-call | flops 1024 | bytes 3200000 | tf_op jit(solution)/shard_map/pallas_call | solution.py:76
  260.7 19.9 %shard_map.549 = (f32[256,2048]{1,0:T(8,128)}, bf16[256,2048]{1,0:T(8,128)(2,1)}, bf16[256,2048]{1,0:T(8,128)(2,1)}) custom-call(s32[2]{0:T(128)} %pad_add_fusion.where, bf16[256,512]{1,0:T(8,128)(2,1)} %get-tuple-element.304.refs_0_, bf16[256,512]{1,0:T(8,128)(2,1)} %copy-done.26, bf16[256,512]{1,0:T(8,128)(2,1)} %copy-done.27, ...), custom_call_target="tpu_custom_call" | custom-call | flops 1024 | bytes 1800000 | tf_op jit(solution)/shard_map/pallas_call | solution.py:76
  282.0 24.0 %collective-permute-done.24.refs_1_ = bf16[256,2048]{1,0:T(8,128)(2,1)S(1)} collective-permute-done((bf16[256,2048]{1,0:T(8,128)(2,1)}, bf16[256,2048]{1,0:T(8,128)(2,1)S(1)}, u32[]{:S(2)}, u32[]{:S(2)}) %collective-permute-start.24) | collective-permute-done | bytes 1048608 | tf_op jit(solution)/shard_map/ppermute | solution.py:490
  309.4 17.0 %shard_map.550 = (bf16[1024,2048]{1,0:T(8,128)(2,1)}, f32[1024,2048]{1,0:T(8,128)}) custom-call(bf16[256,2048]{1,0:T(8,128)(2,1)} %get-tuple-element.148.refs_0_, bf16[256,2048]{1,0:T(8,128)(2,1)} %copy-done.6, bf16[256,2048]{1,0:T(8,128)(2,1)} %copy-done.7, bf16[256,2048]{1,0:T(8,128)(2,1)} %collective-permute-done.26.refs_3_, ...), custom_call_target="tpu_custom_call" | custom-call | flops 1024 | bytes 3400000 | tf_op jit(solution)/shard_map/pallas_call | solution.py:76
  330.3 14.1 %shard_map.551 = bf16[2048,2048]{1,0:T(8,128)(2,1)} custom-call(bf16[1024,2048]{1,0:T(8,128)(2,1)} %get-tuple-element.194.activated, bf16[256,2048]{1,0:T(8,128)(2,1)} %copy-done.5, bf16[256,2048]{1,0:T(8,128)(2,1)} %collective-permute-done.13.refs_1_, bf16[256,2048]{1,0:T(8,128)(2,1)} %collective-permute-done.32.refs_2_, bf16[256,2048]{1,0:T(8,128)(2,1)} %copy-done.13), custom_call_target="tpu_custom_call" | custom-call | flops 1024 | bytes 2800000 | tf_op jit(solution)/shard_map/pallas_call | solution.py:76
  348.3 16.1 %shard_map.552.grad.refs_4_ = bf16[1024,2048]{1,0:T(8,128)(2,1)} custom-call(bf16[256,2048]{1,0:T(8,128)(2,1)} %copy-done.5, bf16[256,2048]{1,0:T(8,128)(2,1)} %collective-permute-done.13.refs_1_, bf16[256,2048]{1,0:T(8,128)(2,1)} %collective-permute-done.32.refs_2_, bf16[256,2048]{1,0:T(8,128)(2,1)} %copy-done.13, ...), custom_call_target="tpu_custom_call" | custom-call | flops 1024 | bytes 3200000 | tf_op jit(solution)/shard_map/pallas_call | solution.py:76
  364.4 11.5 %shard_map.553 = (bf16[256,2048]{1,0:T(8,128)(2,1)}, bf16[256,2048]{1,0:T(8,128)(2,1)}) custom-call(bf16[1024,2048]{1,0:T(8,128)(2,1)} %shard_map.552.grad.refs_4_, bf16[1024,2048]{1,0:T(8,128)(2,1)} %all-gather.6.cloned.1.call-done.refs_4_.own, bf16[1024,2048]{1,0:T(8,128)(2,1)} %copy-done.1), custom_call_target="tpu_custom_call" | custom-call | flops 1024 | bytes 2200000 | tf_op jit(solution)/shard_map/pallas_call | solution.py:76
  391.4 11.5 %shard_map.556 = (bf16[256,2048]{1,0:T(8,128)(2,1)}, bf16[256,2048]{1,0:T(8,128)(2,1)}) custom-call(bf16[1024,2048]{1,0:T(8,128)(2,1)} %shard_map.552.grad.refs_4_, bf16[1024,2048]{1,0:T(8,128)(2,1)} %all-gather.6.cloned.1.call-done.refs_4_.own, bf16[1024,2048]{1,0:T(8,128)(2,1)} %copy-done.1), custom_call_target="tpu_custom_call" | custom-call | flops 1024 | bytes 2200000 | tf_op jit(solution)/shard_map/pallas_call | solution.py:76
  416.7 11.2 %shard_map.558 = (bf16[256,2048]{1,0:T(8,128)(2,1)}, f32[1,2048]{1,0:T(1,128)}, f32[1,2048]{1,0:T(1,128)}, bf16[256,512]{1,0:T(8,128)(2,1)}, bf16[256,512]{1,0:T...) custom-call(s32[2]{0:T(128)} %pad_add_fusion.where, f32[256,2048]{1,0:T(8,128)} %get-tuple-element.147.refs_0_, ...), custom_call_target="tpu_custom_call" | custom-call | flops 1024 | bytes 2200000 | tf_op jit(solution)/shard_map/pallas_call | solution.py:76
  446.5 15.2 %shard_map.560 = (bf16[3,512,512]{2,1,0:T(8,128)(2,1)}, bf16[3,256,2048]{2,1,0:T(8,128)(2,1)}, bf16[3,256,2048]{2,1,0:T(8,128)(2,1)}) custom-call(bf16[1024,512]{1,0:T(8,128)(2,1)} %get-tuple-element.166.q, bf16[1024,512]{1,0:T(8,128)(2,1)} %get-tuple-element.167.k, bf16[1024,512]{1,0:T(8,128)(2,1)} %get-tuple-element.168.v, ...), custom_call_target="tpu_custom_call" | custom-call | flops 1024 | bytes 3000000 | tf_op jit(solution)/shard_map/pallas_call | solution.py:76
  468.6 15.7 %shard_map.561 = (bf16[3,512,512]{2,1,0:T(8,128)(2,1)}, bf16[3,256,2048]{2,1,0:T(8,128)(2,1)}, bf16[3,256,2048]{2,1,0:T(8,128)(2,1)}) custom-call(bf16[1024,512]{1,0:T(8,128)(2,1)} %get-tuple-element.166.q, bf16[1024,512]{1,0:T(8,128)(2,1)} %get-tuple-element.167.k, bf16[1024,512]{1,0:T(8,128)(2,1)} %get-tuple-element.168.v, ...), custom_call_target="tpu_custom_call" | custom-call | flops 1024 | bytes 3000000 | tf_op jit(solution)/shard_map/pallas_call | solution.py:76
  489.6 12.3 %shard_map.562 = bf16[1024,1536]{1,0:T(8,128)(2,1)} custom-call(bf16[3,256,2048]{2,1,0:T(8,128)(2,1)} %get-tuple-element.140.refs_0_, bf16[3,256,2048]{2,1,0:T(8,128)(2,1)} %collective-permute-done.5.refs_1_, bf16[3,256,2048]{2,1,0:T(8,128)(2,1)} %collective-permute-done.6.refs_2_, bf16[3,256,2048]{2,1,0:T(8,128)(2,1)} %collective-permute-done.7.refs_3_, ...), custom_call_target="tpu_custom_call" | custom-call | flops 1024 | bytes 2400000 | tf_op jit(solution)/shard_map/pallas_call | solution.py:76
  501.9 12.4 %shard_map.563 = bf16[1024,1536]{1,0:T(8,128)(2,1)} custom-call(bf16[3,256,2048]{2,1,0:T(8,128)(2,1)} %get-tuple-element.140.refs_0_, bf16[3,256,2048]{2,1,0:T(8,128)(2,1)} %collective-permute-done.5.refs_1_, bf16[3,256,2048]{2,1,0:T(8,128)(2,1)} %collective-permute-done.6.refs_2_, bf16[3,256,2048]{2,1,0:T(8,128)(2,1)} %collective-permute-done.7.refs_3_, ...), custom_call_target="tpu_custom_call" | custom-call | flops 1024 | bytes 2400000 | tf_op jit(solution)/shard_map/pallas_call | solution.py:76
  514.3 18.3 %collective-permute-done.36 = bf16[768,2048]{1,0:T(8,128)(2,1)} collective-permute-done((bf16[768,2048]{1,0:T(8,128)(2,1)}, bf16[768,2048]{1,0:T(8,128)(2,1)}, u32[]{:S(2)}, u32[]{:S(2)}) %collective-permute-start.36) | collective-permute-done | bytes 3145760 | tf_op jit(solution)/shard_map/ppermute | solution.py:490
  539.7 13.5 %shard_map.564 = (bf16[256,2048]{1,0:T(8,128)(2,1)}, bf16[256,2048]{1,0:T(8,128)(2,1)}, bf16[256,2048]{1,0:T(8,128)(2,1)}, bf16[256,2048]{1,0:T(8,128)(2,1)}) custom-call(bf16[1024,2048]{1,0:T(8,128)(2,1)} %get-tuple-element.194.activated, bf16[2048,2048]{1,0:T(8,128)(2,1)} %all-gather.8.cloned.1.call-done.refs_4_.weight), custom_call_target="tpu_custom_call" | custom-call | flops 1024 | bytes 2800000 | tf_op jit(solution)/shard_map/pallas_call | solution.py:76
  559.7 49.1 %collective-permute-done.52 = bf16[1024,1536]{1,0:T(8,128)(2,1)S(1)} collective-permute-done((bf16[1024,1536]{1,0:T(8,128)(2,1)}, bf16[1024,1536]{1,0:T(8,128)(2,1)S(1)}, u32[]{:S(2)}, u32[]{:S(2)}) %collective-permute-start.52) | collective-permute-done | bytes 3145760 | tf_op jit(solution)/shard_map/ppermute | solution.py:490
  608.7 22.0 %collective-permute-done.54 = bf16[1024,512]{1,0:T(8,128)(2,1)S(1)} collective-permute-done((bf16[1024,512]{1,0:T(8,128)(2,1)S(1)}, bf16[1024,512]{1,0:T(8,128)(2,1)S(1)}, u32[]{:S(2)}, u32[]{:S(2)}) %collective-permute-start.54) | collective-permute-done | bytes 1048608 | tf_op jit(solution)/shard_map/ppermute | solution.py:490
  653.3 25.4 %shard_map.565 = (bf16[9,256,2048]{2,1,0:T(8,128)(2,1)}, f32[36,2048]{1,0:T(8,128)}, f32[36,36]{1,0:T(8,128)}, f32[2,2048]{1,0:T(2,128)}, f32[1,2048]{1,0:T(1,128)}) custom-call(s32[2]{0:T(128)} %pad_add_fusion.where, bf16[9,256,2048]{2,1,0:T(8,128)(2,1)} %refs_0_.1, f32[4,256,2048]{2,1,0:T(8,128)} %get-tuple-element.146.refs_12_.refs_1_, ...), custom_call_target="tpu_custom_call" | custom-call | flops 1024 | bytes 5000000 | tf_op jit(solution)/shard_map/pallas_call | solution.py:76
  762.0 13.9 %shard_map.566 = (f32[64,6144]{1,0:T(8,128)}, f32[64,6144]{1,0:T(8,128)}, f32[64,2048]{1,0:T(8,128)}, f32[64,2048]{1,0:T(8,128)}, f32[64,8192]{1,0:T(8,128)}, /*...) custom-call(f32[1]{0:T(128)} %bitcast.21.clip_ref, bf16[64,6144]{1,0:T(8,128)(2,1)} %slice.165.refs_0_, ...), custom_call_target="tpu_custom_call" | custom-call | flops 1024 | bytes 2800000 | tf_op jit(solution)/shard_map/pallas_call | solution.py:76
  (423 shorter events, 330.5 us)
Async XLA Ops:
  7.2 109.2 %all-gather.4.cloned.1.call-start = ((), (), s32[]{:S(2)}) async-start(), calls=%async_computation.3 | async-start | bytes 5242880 | tf_op jit(solution)/shard_map/all_gather | solution.py:502
  30.0 183.6 %all-gather.6.cloned.1.call-start = ((), (), s32[]{:S(2)}) async-start(), calls=%async_computation.4 | async-start | bytes 5242880 | tf_op jit(solution)/shard_map/all_gather | solution.py:502
  50.8 297.5 %all-gather.8.cloned.1.call-start = ((), (), s32[]{:S(2)}) async-start(), calls=%async_computation.5 | async-start | bytes 10485760 | tf_op jit(solution)/shard_map/all_gather | solution.py:502
  100.6 436.8 %reduce-scatter.4.cloned.1.call-start = ((), (), s32[]{:S(2)}) async-start(), calls=%async_computation.6 | async-start | bytes 10485760 | tf_op jit(solution)/shard_map/reduce_scatter | solution.py:505
  100.6 68.7 %collective-permute-start.5 = (bf16[3,256,2048]{2,1,0:T(8,128)(2,1)}, bf16[3,256,2048]{2,1,0:T(8,128)(2,1)}, u32[]{:S(2)}, u32[]{:S(2)}) collective-permute-start(bf16[3,256,2048]{2,1,0:T(8,128)(2,1)} %get-tuple-element.140.refs_0_), channel_id=1, source_target_pairs={{0,2},{1,3},{2,0},{3,1},{4,6},{5,7},{6,4},{7,5},{8,10},{9,11},{10,... | collective-permute-start | bytes 9437192 | tf_op jit(solution)/shard_map/ppermute | solution.py:490
  116.5 92.5 %collective-permute-start.12 = (bf16[1024,2048]{1,0:T(8,128)(2,1)}, bf16[1024,2048]{1,0:T(8,128)(2,1)S(1)}, u32[]{:S(2)}, u32[]{:S(2)}) collective-permute-start(bf16[1024,2048]{1,0:T(8,128)(2,1)} %all-gather.4.cloned.1.call-done.refs_4_.own), channel_id=1, source_target_pairs={{0,4},{1,5},{2,6},{3,7},{4,0},{5,1},{6,2},{7,3},{8,12},{9,13},{10,... | collective-permute-start | bytes 12582920 | tf_op jit(solution)/shard_map/ppermute | solution.py:490
  118.0 95.6 %collective-permute-start.6 = (bf16[3,256,2048]{2,1,0:T(8,128)(2,1)}, bf16[3,256,2048]{2,1,0:T(8,128)(2,1)}, u32[]{:S(2)}, u32[]{:S(2)}) collective-permute-start(bf16[3,256,2048]{2,1,0:T(8,128)(2,1)} %get-tuple-element.140.refs_0_), channel_id=1, source_target_pairs={{0,1},{1,0},{2,3},{3,2},{4,5},{5,4},{6,7},{7,6},{8,9},{9,8},{10,11... | collective-permute-start | bytes 9437192 | tf_op jit(solution)/shard_map/ppermute | solution.py:490
  169.3 47.4 %collective-permute-start.7 = (bf16[3,256,2048]{2,1,0:T(8,128)(2,1)}, bf16[3,256,2048]{2,1,0:T(8,128)(2,1)}, u32[]{:S(2)}, u32[]{:S(2)}) collective-permute-start(bf16[3,256,2048]{2,1,0:T(8,128)(2,1)} %collective-permute-done.5.refs_1_), channel_id=1, source_target_pairs={{0,1},{1,0},{2,3},{3,2},{4,5},{5,4},{6,7},{7,6},{8,9},{9,8},{10,11... | collective-permute-start | bytes 9437192 | tf_op jit(solution)/shard_map/ppermute | solution.py:490
  172.7 40.9 %collective-permute-start.13 = (bf16[256,2048]{1,0:T(8,128)(2,1)S(1)}, bf16[256,2048]{1,0:T(8,128)(2,1)}, u32[]{:S(2)}, u32[]{:S(2)}) collective-permute-start(bf16[256,2048]{1,0:T(8,128)(2,1)S(1)} %multiply_convert_fusion.refs_0_.refs_5_), channel_id=1, source_target_pairs={{0,2},{1,3},{2,0},{3,1},{4,6},{5,7},{6,4},{7,5},{8,10},{9,11},{10,... | collective-permute-start | bytes 3145736 | tf_op jit(solution)/shard_map/ppermute | solution.py:490
  176.4 58.6 %collective-permute-start.18 = (bf16[1024,512]{1,0:T(8,128)(2,1)}, bf16[1024,512]{1,0:T(8,128)(2,1)}, u32[]{:S(2)}, u32[]{:S(2)}) collective-permute-start(bf16[1024,512]{1,0:T(8,128)(2,1)} %slice.155.refs_4_.refs_6_), channel_id=1, source_target_pairs={{0,2},{1,3},{2,0},{3,1},{4,6},{5,7},{6,4},{7,5},{8,10},{9,11},{10,... | collective-permute-start | bytes 3145736 | tf_op jit(solution)/shard_map/ppermute | solution.py:490
  213.6 93.2 %collective-permute-start.31 = (bf16[1024,2048]{1,0:T(8,128)(2,1)}, bf16[1024,2048]{1,0:T(8,128)(2,1)S(1)}, u32[]{:S(2)}, u32[]{:S(2)}) collective-permute-start(bf16[1024,2048]{1,0:T(8,128)(2,1)} %all-gather.6.cloned.1.call-done.refs_4_.own), channel_id=1, source_target_pairs={{0,4},{1,5},{2,6},{3,7},{4,0},{5,1},{6,2},{7,3},{8,12},{9,13},{10,... | collective-permute-start | bytes 12582920 | tf_op jit(solution)/shard_map/ppermute | solution.py:490
  216.7 43.3 %collective-permute-start.21 = (bf16[1024,512]{1,0:T(8,128)(2,1)}, bf16[1024,512]{1,0:T(8,128)(2,1)}, u32[]{:S(2)}, u32[]{:S(2)}) collective-permute-start(bf16[1024,512]{1,0:T(8,128)(2,1)} %slice.156.refs_5_.refs_7_), channel_id=1, source_target_pairs={{0,1},{1,0},{2,3},{3,2},{4,5},{5,4},{6,7},{7,6},{8,9},{9,8},{10,11... | collective-permute-start | bytes 3145736 | tf_op jit(solution)/shard_map/ppermute | solution.py:490
  344.5 290.3 %reduce-scatter.6.cloned.1.call-start = ((), (), s32[]{:S(2)}) async-start(), calls=%async_computation.7 | async-start | bytes 5242880 | tf_op jit(solution)/shard_map/reduce_scatter | solution.py:505
  462.2 70.5 %collective-permute-start.36 = (bf16[768,2048]{1,0:T(8,128)(2,1)}, bf16[768,2048]{1,0:T(8,128)(2,1)}, u32[]{:S(2)}, u32[]{:S(2)}) collective-permute-start(bf16[768,2048]{1,0:T(8,128)(2,1)} %shard_map.555), channel_id=1, source_target_pairs={{0,4},{1,5},{2,6},{3,7},{4,0},{5,1},{6,2},{7,3},{8,12},{9,13},{10,... | collective-permute-start | bytes 9437192 | tf_op jit(solution)/shard_map/ppermute | solution.py:490
  464.6 68.0 %collective-permute-start.46 = (bf16[2048,512]{1,0:T(8,128)(2,1)}, bf16[2048,512]{1,0:T(8,128)(2,1)}, u32[]{:S(2)}, u32[]{:S(2)}) collective-permute-start(bf16[2048,512]{1,0:T(8,128)(2,1)} %add_convert_fusion.3), channel_id=1, source_target_pairs={{0,2},{1,3},{2,0},{3,1},{4,6},{5,7},{6,4},{7,5},{8,10},{9,11},{10,... | collective-permute-start | bytes 6291464 | tf_op jit(solution)/shard_map/ppermute | solution.py:490
  537.4 189.8 %reduce-scatter.8.cloned.1.call-start = ((), (), s32[]{:S(2)}) async-start(), calls=%async_computation.8 | async-start | bytes 5242880 | tf_op jit(solution)/shard_map/reduce_scatter | solution.py:505
  537.6 71.2 %collective-permute-start.52 = (bf16[1024,1536]{1,0:T(8,128)(2,1)}, bf16[1024,1536]{1,0:T(8,128)(2,1)S(1)}, u32[]{:S(2)}, u32[]{:S(2)}) collective-permute-start(bf16[1024,1536]{1,0:T(8,128)(2,1)} %shard_map.562), channel_id=1, source_target_pairs={{0,4},{1,5},{2,6},{3,7},{4,0},{5,1},{6,2},{7,3},{8,12},{9,13},{10,... | collective-permute-start | bytes 9437192 | tf_op jit(solution)/shard_map/ppermute | solution.py:490
  538.2 96.6 %collective-permute-start.51 = (bf16[3,256,2048]{2,1,0:T(8,128)(2,1)}, bf16[3,256,2048]{2,1,0:T(8,128)(2,1)}, u32[]{:S(2)}, u32[]{:S(2)}) collective-permute-start(bf16[3,256,2048]{2,1,0:T(8,128)(2,1)} %get-tuple-element.203), channel_id=1, source_target_pairs={{0,1},{1,0},{2,3},{3,2},{4,5},{5,4},{6,7},{7,6},{8,9},{9,8},{10,11... | collective-permute-start | bytes 9437192 | tf_op jit(solution)/shard_map/ppermute | solution.py:490
  538.3 96.4 %collective-permute-start.49 = (bf16[3,256,2048]{2,1,0:T(8,128)(2,1)}, bf16[3,256,2048]{2,1,0:T(8,128)(2,1)}, u32[]{:S(2)}, u32[]{:S(2)}) collective-permute-start(bf16[3,256,2048]{2,1,0:T(8,128)(2,1)} %add_convert_fusion.2), channel_id=1, source_target_pairs={{0,2},{1,3},{2,0},{3,1},{4,6},{5,7},{6,4},{7,5},{8,10},{9,11},{10,... | collective-permute-start | bytes 9437192 | tf_op jit(solution)/shard_map/ppermute | solution.py:490
  556.6 74.2 %collective-permute-start.54 = (bf16[1024,512]{1,0:T(8,128)(2,1)S(1)}, bf16[1024,512]{1,0:T(8,128)(2,1)S(1)}, u32[]{:S(2)}, u32[]{:S(2)}) collective-permute-start(bf16[1024,512]{1,0:T(8,128)(2,1)S(1)} %slice.290), channel_id=1, source_target_pairs={{0,4},{1,5},{2,6},{3,7},{4,0},{5,1},{6,2},{7,3},{8,12},{9,13},{10,... | collective-permute-start | bytes 3145736 | tf_op jit(solution)/shard_map/ppermute | solution.py:490
  641.3 39.2 %collective-permute-start.56 = (bf16[64,2048]{1,0:T(8,128)(2,1)S(1)}, bf16[64,2048]{1,0:T(8,128)(2,1)S(1)}, u32[]{:S(2)}, u32[]{:S(2)}) collective-permute-start(bf16[64,2048]{1,0:T(8,128)(2,1)S(1)} %get-tuple-element.291), channel_id=1, source_target_pairs={{0,2},{1,3},{2,0},{3,1},{4,6},{5,7},{6,4},{7,5},{8,10},{9,11},{10,... | collective-permute-start | bytes 786440 | tf_op jit(solution)/shard_map/ppermute | solution.py:490
  641.9 39.0 %collective-permute-start.57 = (bf16[64,2048]{1,0:T(8,128)(2,1)S(1)}, bf16[64,2048]{1,0:T(8,128)(2,1)S(1)}, u32[]{:S(2)}, u32[]{:S(2)}) collective-permute-start(bf16[64,2048]{1,0:T(8,128)(2,1)S(1)} %get-tuple-element.269), channel_id=1, source_target_pairs={{0,1},{1,0},{2,3},{3,2},{4,5},{5,4},{6,7},{7,6},{8,9},{9,8},{10,11... | collective-permute-start | bytes 786440 | tf_op jit(solution)/shard_map/ppermute | solution.py:490
  642.9 49.1 %collective-permute-start.55 = (bf16[256,2048]{1,0:T(8,128)(2,1)}, bf16[256,2048]{1,0:T(8,128)(2,1)}, u32[]{:S(2)}, u32[]{:S(2)}) collective-permute-start(bf16[256,2048]{1,0:T(8,128)(2,1)} %broadcast_select_fusion), channel_id=1, source_target_pairs={{0,4},{1,5},{2,6},{3,7},{4,0},{5,1},{6,2},{7,3},{8,12},{9,13},{10,... | collective-permute-start | bytes 3145736 | tf_op jit(solution)/shard_map/ppermute | solution.py:490
  650.5 46.1 %collective-permute-start.50 = (bf16[256,2048]{1,0:T(8,128)(2,1)}, bf16[256,2048]{1,0:T(8,128)(2,1)}, u32[]{:S(2)}, u32[]{:S(2)}) collective-permute-start(bf16[256,2048]{1,0:T(8,128)(2,1)} %add_convert_fusion.5), channel_id=1, source_target_pairs={{0,2},{1,3},{2,0},{3,1},{4,6},{5,7},{6,4},{7,5},{8,10},{9,11},{10,... | collective-permute-start | bytes 3145736 | tf_op jit(solution)/shard_map/ppermute | solution.py:490
  (122 other events, 1715.1 us)
Sparse Core Ops, SparseCore 0:
  30.1 86.3 all-gather.3
  118.6 79.2 all-gather.5
  200.1 148.1 all-gather.7
  350.5 142.6 reduce-scatter.3
  537.5 75.9 reduce-scatter.5
  634.9 75.9 reduce-scatter.7

commit v3 on v2

--- a/solution.py
+++ b/solution.py
@@ -20,6 +20,7 @@
 BETA = 0.5
 NEGATIVE = -1e30
 COST_SCALE = 200e3
+PLACE_COST = 450
 
 BF = jnp.bfloat16
 F32 = jnp.float32
@@ -206,14 +207,15 @@
         ).astype(BF)
         grads[2, :, lanes] = dot_tn(probs.astype(BF), grad).astype(BF)
 
-    def send(back):
+    def send(outs):
         for a in range(3):
             columns = slice(a * quarter, (a + 1) * quarter)
-            back[a, :, :half] = dot_nt(grads[a], own[:, columns]).astype(BF)
-            back[a, :, half:] = dot_nt(grads[a], other[:, columns]).astype(BF)
+            outs[a][:, :half] = dot_nt(grads[a], own[:, columns]).astype(BF)
+            outs[a][:, half:] = dot_nt(grads[a], other[:, columns]).astype(BF)
 
     for step in range(2):
-        pl.when(pl.program_id(0) == step)(functools.partial(send, backs[step]))
+        outs = backs[3 * step : 3 * step + 3]
+        pl.when(pl.program_id(0) == step)(functools.partial(send, outs))
 
 
 def residual_kernel(order, where, *refs):
@@ -345,10 +347,11 @@
 
 def mixing_backward_kernel(order, where, *refs):
     order = order(where)
-    h, streams, coef_in, pre_in, mine, from_core, from_x, grad_residual = refs[:8]
-    w_mix, gain, mixer = refs[8:11]
-    grad_history, grad_mix, grad_mixer, grad_gains, grad_bias = refs[11:16]
-    grad_streams = refs[16]
+    h, streams, coef_in, pre_in = refs[:4]
+    mine, from_core, from_x = refs[4:7], refs[7:10], refs[10]
+    grad_residual, w_mix, gain, mixer = refs[11:15]
+    grad_history, grad_mix, grad_mixer, grad_gains, grad_bias = refs[15:20]
+    grad_streams = refs[20]
     hist_len, rows, width = h.shape
     step = 512
 
@@ -363,8 +366,8 @@
         for k in order.blocks():
             source = order.relative(k)
             grad_streams[a, :, order.natural(k)] = (
-                mine[a, :, source].astype(F32)
-                + from_core[a, :, source].astype(F32)
+                mine[a][:, source].astype(F32)
+                + from_core[a][:, source].astype(F32)
                 + from_x[a, :, source].astype(F32)
             )
         xhat, scale = standardise(streams[a])
@@ -424,18 +427,34 @@
     return cos_table, sin_table
 
 
-def moments_kernel(clip_ref, *refs):
+def place_kernel(order, where, *refs):
+    order = order(where)
+    parts, (weight_in, weight_out) = refs[:4], refs[4:]
+    quarter = order.quarter
+    for d in range(4):
+        for a in range(4):
+            start = (a % 3) * 4 * quarter + (order.rank ^ TURNS[d]) * quarter
+            lanes = pl.ds(pl.multiple_of(start, quarter), quarter)
+            target = weight_out if a == 3 else weight_in
+            if a == 3:
+                lanes = order.quarter_of(d)
+            target[:, lanes] = parts[d][:, a * quarter : (a + 1) * quarter]
+
+
+def moments_kernel(share, clip_ref, *refs):
     clip = clip_ref[0]
     step = 512
 
     @pl.when(pl.program_id(0) == 0)
     def _():
         for member in range(4):
-            refs[24][member] = 0.0
+            refs[26][member] = 0.0
+        refs[26][4] = jnp.sum(refs[16][...] * refs[16][...])
+        refs[26][5] = jnp.sum(refs[17][...] * refs[17][...]) * share
 
     for member in range(4):
         grad, first, second, weight = refs[4 * member : 4 * member + 4]
-        first_out, second_out = refs[16 + 2 * member : 18 + 2 * member]
+        first_out, second_out = refs[18 + 2 * member : 20 + 2 * member]
         total = 0.0
         for start in range(0, grad.shape[1], step):
             lanes = slice(start, start + step)
@@ -446,14 +465,14 @@
             second_out[:, lanes] = second_new
             change = first_new / (jnp.sqrt(second_new) + EPS_ADAM) + DECAY_WEIGHT * weight[:, lanes]
             total = total + jnp.sum(change * change, axis=0, keepdims=True)
-        refs[24][member] = refs[24][member] + jnp.sum(total)
+        refs[26][member] = refs[26][member] + jnp.sum(total)
 
 
 def apply_kernel(trust_ref, *refs):
     step = 512
     for member in range(4):
         first, second, weight = refs[3 * member : 3 * member + 3]
-        out, low = refs[12 + 2 * member : 14 + 2 * member]
+        out, low = refs[20 + 2 * member : 22 + 2 * member]
         rate = RATE_MATRIX * trust_ref[member]
         for start in range(0, weight.shape[1], step):
             lanes = slice(start, start + step)
@@ -462,6 +481,16 @@
             new = old - rate * change
             out[:, lanes] = new
             low[:, lanes] = new.astype(BF)
+
+    @pl.when(pl.program_id(0) == 0)
+    def _():
+        for member in range(4):
+            change, weight = refs[12 + 2 * member : 14 + 2 * member]
+            out, low = refs[28 + 2 * member : 30 + 2 * member]
+            rate = RATE_MATRIX * trust_ref[4 + member] if member < 2 else RATE_VECTOR
+            new = weight[...] - rate * change[...]
+            out[...] = new
+            low[...] = new.astype(BF)
 
 
 class Links:
@@ -547,10 +576,8 @@
         return [value, across_x, self.swap_core(value), self.swap_core(across_x)]
 
     def group_exchange(self, parts):
-        own, for_x, for_core, for_both = parts
-        from_both = self.swap_x(for_both)
-        from_x = self.swap_x(for_x)
-        return [own, from_x, self.swap_core(for_core), self.swap_core(from_both)]
+        own, *others = parts
+        return [own] + [self.swap(part, turn) for part, turn in zip(others, TURNS[1:])]
 
     def group_reduce(self, own, for_x, for_core, for_both, *ties):
         from_both = self.swap_core(for_both)
@@ -613,9 +640,8 @@
 
     low_up = ffn_up.astype(BF).reshape(rows, links.outer, 2, links.inner, 4, units)
     low_up = jnp.transpose(low_up, (4, 0, 1, 3, 2, 5)).reshape(4, rows, share)
-    own, for_x, for_core, for_both = after(links.to_relative(list(low_up)), attn_parts[1])
-    from_both = after(links.swap_x(for_both), attn_block)
-    up_parts = [own, links.swap_x(for_x), links.swap_core(for_core), links.swap_core(from_both)]
+    up_parts = after(links.to_relative(list(low_up)), attn_parts[1], attn_parts[3])
+    up_parts = links.group_exchange(up_parts)
     up_block = jnp.concatenate(links.to_absolute(up_parts), axis=0)
 
     low_down = ffn_down.astype(BF)
@@ -785,10 +811,12 @@
         [((four, share), BF, column_tile(four))],
     )
 
-    def whole_rows(block):
+    def rows_of_four(block):
         parts = list(block.reshape(4, rows, block.shape[1]))
-        parts = links.to_absolute(links.group_exchange(links.to_relative(parts)))
-        return jnp.stack(parts, axis=1)
+        return links.group_exchange(links.to_relative(parts))
+
+    def whole_rows(parts):
+        return jnp.stack(links.to_absolute(parts), axis=1)
 
     tiles = half // wide
 
@@ -819,7 +847,9 @@
     for_x, for_both = normed_back((1, 3), grad_up)
     up_first = up_grad(tiles, 1, after(grad_up, for_both))
     up_theirs_first = links.swap_y(up_first)
-    up_rest = up_grad(tiles + 1, tiles - 1, after(grad_up, up_first))
+    up_second = up_grad(tiles + 1, 1, after(grad_up, up_first))
+    up_theirs_second = links.swap_y(up_second)
+    up_rest = up_grad(tiles + 2, tiles - 2, after(grad_up, up_second))
     up_theirs_rest = links.swap_y(up_rest)
     own, for_core = normed_back((0, 2), after(grad_up, up_rest))
     up_grad_own = up_grad(0, tiles, after(grad_up, own))
@@ -845,14 +875,7 @@
     )
     grad_residual, grad_gain_ffn, grad_bias_ffn = back[:3]
 
-    heads_own, for_x, for_core, for_both = back[3:]
-    from_both, from_x = links.swap_x(for_both), links.swap_x(for_x)
-    grad_heads = [
-        heads_own,
-        from_x,
-        links.swap_core(for_core),
-        links.swap_core(from_both),
-    ]
+    grad_heads = links.group_exchange(back[3:])
 
     line = 512
     out_parts = run(
@@ -866,18 +889,14 @@
         ],
         [((width, quarter), BF, pl.BlockSpec((line, quarter), lambda t: (t, 0)))] * 4,
     )
-    out_parts = after(out_parts, from_x, from_both)
-    out_both, out_core = links.swap_core(out_parts[3]), links.swap_core(out_parts[2])
+    out_parts = after(out_parts, grad_heads[1], grad_heads[3])
+    out_both = [links.swap_core(out_parts[3][k * half : (k + 1) * half]) for k in range(2)]
+    out_core = links.swap_core(out_parts[2])
 
     def attention_back(first, *ties):
         heads = jnp.concatenate([grad_heads[first], grad_heads[first + 2]], axis=0)
         block = pl.BlockSpec((seq_len, quarter), lambda s: (first + 2 * s, 0))
-        back_out = (
-            (3, seq_len, width),
-            BF,
-            pl.BlockSpec((3, seq_len, width), lambda s: (0, 0, 0)),
-        )
-        return run(
+        proj, *backs = run(
             attention_backward_kernel,
             15,
             (2,),
@@ -890,18 +909,24 @@
                     (3, 2 * seq_len, quarter),
                     BF,
                     pl.BlockSpec((3, seq_len, quarter), lambda s: (0, s, 0)),
-                ),
-                back_out,
-                back_out,
-            ],
+                )
+            ]
+            + [full(BF)] * 6,
         )
+        return proj, backs[:3], backs[3:]
 
     plus = lambda mine, theirs: (mine.astype(F32) + theirs.astype(F32)).astype(BF)
-    proj_odd, for_x, for_both = attention_back(1)
-    out_for_x = plus(out_parts[1], after(out_both, for_both))
-    out_x = links.swap_x(out_for_x)
+    proj_odd, for_x, for_both = attention_back(1, up_theirs_second)
+    out_both = after(out_both, for_both)
+    out_for_x = [plus(out_parts[1][k * half : (k + 1) * half], out_both[k]) for k in range(2)]
+    out_x_other = links.swap_x(out_for_x[1])
+    out_x_own = links.swap_x(out_for_x[0])
     proj_even, own, for_core = attention_back(0, out_for_x)
-    from_core, from_x, for_x = links.group_reduce(own, for_x, for_core, for_both)
+    back_own = own
+    from_both = [links.swap_core(part) for part in for_both]
+    back_core = [links.swap_core(part) for part in for_core]
+    for_x = jnp.stack([plus(part, other) for part, other in zip(for_x, from_both)])
+    back_x = links.swap_x(for_x)
     proj_even = after(proj_even, for_x)
 
     def in_grad(s, proj):
@@ -921,13 +946,17 @@
     in_grad_own = in_grad(0, after(proj_even, in_grad_other))
 
     up_theirs = jnp.concatenate(
-        [up_theirs_first, after(up_theirs_rest, in_grad_own, out_x)]
+        [up_theirs_first, up_theirs_second, after(up_theirs_rest, in_grad_own, out_x_other)]
     )
     up_both = after(plus(up_grad_own, up_theirs), down_sums)
     up_sums = links.reduce(up_both, links.z_groups)
-    out_x = after(out_x, up_both)
-    out_grad = out_parts[0].astype(F32) + out_core.astype(F32) + out_x.astype(F32)
-    out_theirs = links.swap_y(out_grad[half:].astype(BF))
+    three = lambda k, theirs: (
+        out_parts[0][k * half : (k + 1) * half].astype(F32)
+        + out_core[k * half : (k + 1) * half].astype(F32)
+        + theirs.astype(F32)
+    )
+    out_theirs = links.swap_y(three(1, after(out_x_other, up_both)).astype(BF))
+
     down_parts = run(
         down_kernel,
         14,
@@ -935,17 +964,24 @@
         [whole(after(activated, up_both)), (w_down, column_tile(share))],
         [((seq_len, width), BF, column_tile(seq_len))] * 4,
     )
-    down_core, down_x, down_for_x = links.group_reduce(*down_parts, from_x)
-    out_state = (
-        residual + down_parts[0].astype(F32) + down_core.astype(F32) + down_x.astype(F32)
-    ).astype(BF)
+    down_core = links.swap_core(down_parts[2])
+    down_for_x = plus(down_parts[1], links.swap_core(down_parts[3]))
+
+    weights = (attn_in, attn_out, ffn_up, ffn_down, mixer_in, mixer_out, norm_gain, norm_bias)
+    square = lambda array: jnp.sum(jnp.square(array.astype(F32)))
+
+    def portion(member, amount):
+        return amount / devices if member == 5 else amount
+
 
     in_theirs = after(in_theirs, down_for_x)
     attn_both = jnp.concatenate(
-        [plus(in_grad_own, in_theirs), plus(out_grad[:half], out_theirs)], axis=1
-    )
-    attn_both = after(attn_both, up_sums, from_x, from_core)
+        [plus(in_grad_own, in_theirs), plus(three(0, out_x_own), out_theirs)], axis=1
+    )
+    attn_both = after(attn_both, up_sums, back_x, back_core)
+    up_four = rows_of_four(after(up_sums, attn_both))
     attn_sums = links.reduce(attn_both, links.z_groups)
+
 
     fixed_out = lambda shape: (
         shape,
@@ -954,7 +990,7 @@
     )
     grad_history, grad_mixer_in, grad_mixer_out, grad_gains, grad_bias_attn = run(
         with_order(mixing_backward_kernel),
-        25,
+        450,
         steps,
         [
             where,
@@ -962,9 +998,10 @@
             (streams, row_tile(3)),
             (coef, narrow),
             (mix_pre, pre_narrow),
-            (own, row_tile(3)),
-            (from_core, row_tile(3)),
-            (from_x, row_tile(3)),
+        ]
+        + [(part, row_tile()) for part in (*back_own, *back_core)]
+        + [
+            (back_x, row_tile(3)),
             (after(grad_residual, attn_both), row_tile()),
             whole(w_mixer_in),
             whole(gain_table),
@@ -980,44 +1017,56 @@
         [pltpu.VMEM((4, tile, width), F32)],
     )
 
-    down_sums, up_sums = after(down_sums, attn_both), after(up_sums, attn_both)
+    shard_up = jnp.transpose(
+        whole_rows(up_four).reshape(rows, 4, links.outer, links.inner, 2, units),
+        (0, 2, 4, 3, 1, 5),
+    ).reshape(rows, hidden)
+
+    down_x = links.swap_x(after(down_for_x, grad_gains))
+    small = jnp.concatenate(
+        [grad_mixer_in, grad_gains, grad_gain_ffn, grad_bias_attn, grad_bias_ffn], axis=0
+    )
+    top = devices.bit_length() - 2
+    inner = 1 << (links.y_bit - 2)
+    pieces = small.reshape(small.shape[0], devices // (8 * inner), 2, inner * 4 * rows)
+    take = lambda array, at, axis: lax.dynamic_index_in_dim(array, at, axis, keepdims=False)
+    pieces = take(pieces, links.y, 2) + links.swap_y(take(pieces, 1 - links.y, 2))
+    down_sums = after(down_sums, pieces)
     down_sums = down_sums.reshape(2, units, width)
     down_mine = jnp.where(low_y, down_sums[0], down_sums[1])
     down_theirs = jnp.where(low_y, down_sums[1], down_sums[0])
-    shard_down = down_mine.astype(F32) + links.swap_y(down_theirs).astype(F32)
-    shard_up = jnp.transpose(
-        whole_rows(up_sums).reshape(rows, 4, links.outer, links.inner, 2, units),
-        (0, 2, 4, 3, 1, 5),
-    ).reshape(rows, hidden)
-
-    small = jnp.concatenate(
-        [grad_mixer_in, grad_gains, grad_gain_ffn, grad_bias_attn, grad_bias_ffn], axis=0
-    )
-    small = after(small, shard_up, shard_down, down_x)
-    bits = [links.y_bit] + [k for k in reversed(range(2, devices.bit_length() - 1)) if k != links.y_bit]
-    pieces = small.reshape((small.shape[0],) + (2,) * (devices.bit_length() - 3) + (4 * rows,))
-    left = list(reversed(range(2, devices.bit_length() - 1)))
-    for k in bits:
-        axis = 1 + left.index(k)
-        left.remove(k)
-        low = (links.index & (1 << k)) == 0
-        first = lax.index_in_dim(pieces, 0, axis, keepdims=False)
-        second = lax.index_in_dim(pieces, 1, axis, keepdims=False)
-        pieces = jnp.where(low, first, second) + links.swap(
-            jnp.where(low, second, first), 1 << k
-        )
-    small = pieces
-    small = small + links.swap_x(small)
-    small = small + links.swap_core(small)
-    small = lax.dynamic_slice_in_dim(small, links.rank * rows, rows, axis=1)
+    down_theirs = links.swap_y(down_theirs)
+    shard_down = down_mine.astype(F32) + down_theirs.astype(F32)
+    bits = [k for k in range(top, 1, -1) if k != links.y_bit]
+    while bits:
+        pair, bits = bits[:2], bits[2:]
+        pieces = pieces.reshape(small.shape[0], 1 << len(pair), -1)
+        at = sum(((links.index >> k) & 1) << e for e, k in enumerate(reversed(pair)))
+        total = take(pieces, at, 1)
+        for turn in range(1, 1 << len(pair)):
+            mask = sum(((turn >> e) & 1) << k for e, k in enumerate(reversed(pair)))
+            total = total + links.swap(take(pieces, at ^ turn, 1), mask)
+        pieces = total
+    pieces = after(pieces, down_theirs).reshape(small.shape[0], 4, rows)
+    small = take(pieces, links.rank, 1)
+    for turn in TURNS[1:]:
+        small = small + links.swap(take(pieces, links.rank ^ turn, 1), turn)
     mixer_grad = links.total(grad_mixer_out)
-    square = lambda array: jnp.sum(jnp.square(array.astype(F32)))
     early_squares = square(up_sums) + square(shard_down) + square(small)
     early_squares = early_squares + square(mixer_grad) / devices
-    attn_sums = after(attn_sums, shard_up, early_squares)
-    attn_rows = whole_rows(attn_sums).reshape(rows, 4, 4, quarter)
-    attn_rows = jnp.transpose(attn_rows, (0, 2, 1, 3)).reshape(rows, 4 * width)
-    shard_in, shard_out = attn_rows[:, : 3 * width], attn_rows[:, 3 * width :]
+    attn_sums = after(attn_sums, shard_up, shard_down)
+    block_of = lambda array_shape: pl.BlockSpec(array_shape, lambda t: (0, 0))
+    shard_in, shard_out = run(
+        with_order(place_kernel),
+        PLACE_COST,
+        (1,),
+        [where] + [whole(part) for part in rows_of_four(attn_sums)],
+        [
+            ((rows, 3 * width), BF, block_of((rows, 3 * width))),
+            ((rows, width), BF, block_of((rows, width))),
+        ],
+    )
+
     grads = (
         shard_in,
         shard_out,
@@ -1029,7 +1078,6 @@
         small[hidden_mix + 3 :],
     )
 
-    weights = (attn_in, attn_out, ffn_up, ffn_down, mixer_in, mixer_out, norm_gain, norm_bias)
     firsts = (
         first_attn_in,
         first_attn_out,
@@ -1051,11 +1099,8 @@
         second_norm_bias,
     )
 
-    def portion(member, amount):
-        return amount / devices if member == 5 else amount
-
+    local_squares = early_squares + square(attn_sums)
     weights_later = after(weights, coef)
-    local_squares = early_squares + square(attn_sums)
     local_weight_sq = [portion(member, square(weights_later[member])) for member in range(6)]
     sums = links.total(jnp.stack([local_squares] + local_weight_sq))
     squares, weight_sq = sums[0], sums[1:]
@@ -1071,11 +1116,8 @@
     for member in range(4):
         ins += slabs(grads[member], firsts[member], seconds[member], weights[member])
         outs += [made(weights[member], F32)] * 2
-    outs.append(((4,), F32, SMEM))
-    moments = run(moments_kernel, 14, (parts,), ins, outs)
-    firsts_new, seconds_new = list(moments[0:8:2]), list(moments[1:8:2])
-    local_update_sq = moments[8]
-    steps_small = []
+    outs.append(((6,), F32, SMEM))
+    small_new, steps_small = [], []
     for member in range(4, 8):
         scaled = grads[member] * clip
         first_new = BETA * firsts[member] + (1.0 - BETA) * scaled
@@ -1083,11 +1125,20 @@
         step_value = first_new / (jnp.sqrt(second_new) + EPS_ADAM)
         if member < 6:
             step_value = step_value + DECAY_WEIGHT * weights[member]
-        firsts_new.append(first_new)
-        seconds_new.append(second_new)
+        small_new.append((first_new, second_new))
         steps_small.append(step_value)
-    small_sq = [portion(4 + k, jnp.sum(steps_small[k] * steps_small[k])) for k in range(2)]
-    update_sq = links.total(jnp.concatenate([local_update_sq, jnp.stack(small_sq)]))
+    ins += [whole(steps_small[0]), whole(steps_small[1])]
+    moments = run(
+        functools.partial(moments_kernel, 1.0 / devices), 14, (parts,), ins, outs
+    )
+    down_x = after(down_x, moments[8])
+    out_state = (
+        residual + down_parts[0].astype(F32) + down_core.astype(F32) + down_x.astype(F32)
+    ).astype(BF)
+
+    firsts_new = list(moments[0:8:2]) + [first for first, _ in small_new]
+    seconds_new = list(moments[1:8:2]) + [second for _, second in small_new]
+    update_sq = links.total(moments[8])
     weight_norm = jnp.sqrt(weight_sq)
     update_norm = jnp.sqrt(update_sq)
     trust = weight_norm / (update_norm + 1e-06)
@@ -1096,16 +1147,15 @@
     for member in range(4):
         ins += slabs(firsts_new[member], seconds_new[member], weights[member])
         outs += [made(weights[member], F32), made(weights[member], BF)]
+    for member in range(4, 8):
+        shape = weights[member].shape
+        spec = pl.BlockSpec(shape, lambda t: (0, 0))
+        ins += [(steps_small[member - 4], spec), (weights[member], spec)]
+        outs += [(shape, F32, spec), (shape, BF, spec)]
     applied = run(apply_kernel, 10, (parts,), ins, outs)
     results = []
     for member in range(8):
-        if member < 4:
-            updated, low = applied[2 * member], applied[2 * member + 1]
-        else:
-            rate = RATE_MATRIX * trust[member] if member < 6 else RATE_VECTOR
-            updated = weights[member] - rate * steps_small[member - 4]
-            low = updated.astype(BF)
-        results += [updated, low, firsts_new[member], seconds_new[member]]
+        results += [*applied[2 * member : 2 * member + 2], firsts_new[member], seconds_new[member]]
     return (out_state, grad_history, global_norm, lamb_stats, *results)
 
 

time: 826 us -> 827 us (level)
  starting transfers between devices: 66.2 us -> 85.5 us
  waiting for transfers between devices: 331 us -> 322 us
    all_gather x3, waiting for transfers between devices: 17.9 us -> 0.02 us  [gather(): lax.all_gather(value, 'dp', axis=0, tiled=True, axis_index_groups=groups)]
    all_gather x3, starting transfers between devices: 0.38 us -> 11.3 us  [gather(): lax.all_gather(value, 'dp', axis=0, tiled=True, axis_index_groups=groups)]
    ppermute x90 -> x93, waiting for transfers between devices: 313 us -> 321 us  [swap(): lax.ppermute(value, 'dp', [(j, j ^ bit) for j in range(self.devices)])]
    ppermute x90 -> x93, starting transfers between devices: 65.7 us -> 74 us  [swap(): lax.ppermute(value, 'dp', [(j, j ^ bit) for j in range(self.devices)])]
    pallas_call x21 -> x23, Pallas kernels: 278 us -> 275 us  [run(): pl.pallas_call(kernel, grid=grid, in_specs=[spec for _, spec in ins], out...]
  transfers between devices with their start and end apart: 96 -> 99, of which waited for: 48 -> 39; matrix products, arithmetic and copies ran while one was open for 10% -> 12% of each run, Pallas kernels for 31% -> 32%
where the time goes in v3:
time: 827 us; the launch traced here: 820 us
  waiting for transfers between devices  322 us (39%)
  Pallas kernels  275 us (33%)
  starting transfers between devices  85.5 us (10%)
  other arithmetic  77.5 us (9%)
  local copies, waits for them, and re-layouts  39.7 us (5%)
  between operations  21.3 us (3%)
    ppermute x93, waiting for transfers between devices, swap(): lax.ppermute(value, 'dp', [(j, j ^ bit) for j in range(self.devices)])  321 us
    pallas_call x23, Pallas kernels, run(): pl.pallas_call(kernel, grid=grid, in_specs=[spec for _, spec in ins], out...  275 us
    ppermute x93, starting transfers between devices, swap(): lax.ppermute(value, 'dp', [(j, j ^ bit) for j in range(self.devices)])  74 us
  transfers between devices with their start and end apart: 99, of which 39 were waited for; matrix products, arithmetic and copies ran while one was open for 12% of the time, Pallas kernels for 32%

profile of v3, /device:TPU:0, one launch (start us, length us, event | category | flops | bytes accessed | tf_op | source)
XLA Modules:
  0.0 820.2 jit_solution(8164305375175439083)
XLA Ops:
  51.6 11.2 %all-gather.8.cloned.1.call-start = ((), (), s32[]{:S(2)}) async-start(), calls=%async_computation.5 | async-start | bytes 10485760 | tf_op jit(solution)/shard_map/all_gather | solution.py:531
  82.2 11.5 %collective-permute-done.4 = bf16[41,1024]{1,0:T(8,128)(2,1)S(1)} collective-permute-done((bf16[41,1024]{1,0:T(8,128)(2,1)S(1)}, bf16[41,1024]{1,0:T(8,128)(2,1)S(1)}, u32[]{:S(2)}, u32[]{:S(2)}) %collective-permute-start.4) | collective-permute-done | bytes 84000 | tf_op jit(solution)/shard_map/ppermute | solution.py:519
  95.7 14.2 %shard_map.547 = (f32[4,256,2048]{2,1,0:T(8,128)}, bf16[3,256,2048]{2,1,0:T(8,128)(2,1)}, f32[256,36]{1,0:T(8,128)}, f32[256,36]{1,0:T(8,128)}) custom-call(s32[2]{0:T(128)} %pad_add_fusion.where, bf16[9,256,2048]{2,1,0:T(8,128)(2,1)} %refs_0_.1, bf16[36,2048]{1,0:T(8,128)(2,1)} %fusion.7.w_mix.refs_12_, f32[3,2048]{1,0:T(4,128)} %fusion.19.gain.refs_13_.refs_1_, ...), custom_call_target="tpu_custom_call" | custom-call | flops 1024 | bytes 2800000 | tf_op jit(solution)/shard_map/pallas_call | solution.py:77
  118.5 62.6 %collective-permute-done.5.refs_1_ = bf16[3,256,2048]{2,1,0:T(8,128)(2,1)} collective-permute-done((bf16[3,256,2048]{2,1,0:T(8,128)(2,1)}, bf16[3,256,2048]{2,1,0:T(8,128)(2,1)}, u32[]{:S(2)}, u32[]{:S(2)}) %collective-permute-start.5) | collective-permute-done | bytes 3145760 | tf_op jit(solution)/shard_map/ppermute | solution.py:519
  188.8 20.7 %collective-permute-done.11.refs_5_.other = bf16[1024,2048]{1,0:T(8,128)(2,1)S(1)} collective-permute-done((bf16[1024,2048]{1,0:T(8,128)(2,1)}, bf16[1024,2048]{1,0:T(8,128)(2,1)S(1)}, u32[]{:S(2)}, u32[]{:S(2)}) %collective-permute-start.11) | collective-permute-done | bytes 4194336 | tf_op jit(solution)/shard_map/ppermute | solution.py:519
  217.6 16.2 %shard_map.548 = (bf16[1024,512]{1,0:T(8,128)(2,1)}, bf16[1024,512]{1,0:T(8,128)(2,1)}, bf16[1024,512]{1,0:T(8,128)(2,1)}, bf16[1024,512]{1,0:T(8,128)(2,1)}) custom-call(bf16[3,256,2048]{2,1,0:T(8,128)(2,1)} %get-tuple-element.161.refs_0_, bf16[3,256,2048]{2,1,0:T(8,128)(2,1)} %collective-permute-done.5.refs_1_, ...), custom_call_target="tpu_custom_call" | custom-call | flops 1024 | bytes 3200000 | tf_op jit(solution)/shard_map/pallas_call | solution.py:77
  233.9 21.2 %collective-permute-done.17.refs_7_.refs_9_ = bf16[1024,512]{1,0:T(8,128)(2,1)} collective-permute-done((bf16[1024,512]{1,0:T(8,128)(2,1)}, bf16[1024,512]{1,0:T(8,128)(2,1)}, u32[]{:S(2)}, u32[]{:S(2)}) %collective-permute-start.17) | collective-permute-done | bytes 1048608 | tf_op jit(solution)/shard_map/ppermute | solution.py:519
  286.8 24.1 %collective-permute-done.22.refs_1_ = bf16[256,2048]{1,0:T(8,128)(2,1)S(1)} collective-permute-done((bf16[256,2048]{1,0:T(8,128)(2,1)}, bf16[256,2048]{1,0:T(8,128)(2,1)S(1)}, u32[]{:S(2)}, u32[]{:S(2)}) %collective-permute-start.22) | collective-permute-done | bytes 1048608 | tf_op jit(solution)/shard_map/ppermute | solution.py:519
  315.2 17.1 %shard_map.550 = (bf16[1024,2048]{1,0:T(8,128)(2,1)}, f32[1024,2048]{1,0:T(8,128)}) custom-call(bf16[256,2048]{1,0:T(8,128)(2,1)} %get-tuple-element.169.refs_0_, bf16[256,2048]{1,0:T(8,128)(2,1)} %copy-done.4, bf16[256,2048]{1,0:T(8,128)(2,1)} %collective-permute-done.23.refs_2_, bf16[256,2048]{1,0:T(8,128)(2,1)} %collective-permute-done.24.refs_3_, ...), custom_call_target="tpu_custom_call" | custom-call | flops 1024 | bytes 3400000 | tf_op jit(solution)/shard_map/pallas_call | solution.py:77
  336.1 14.1 %shard_map.551 = bf16[2048,2048]{1,0:T(8,128)(2,1)} custom-call(bf16[1024,2048]{1,0:T(8,128)(2,1)} %get-tuple-element.221.activated, bf16[256,2048]{1,0:T(8,128)(2,1)} %copy-done.6, bf16[256,2048]{1,0:T(8,128)(2,1)} %collective-permute-done.12.refs_1_, bf16[256,2048]{1,0:T(8,128)(2,1)} %collective-permute-done.29.refs_2_, bf16[256,2048]{1,0:T(8,128)(2,1)} %copy-done.13), custom_call_target="tpu_custom_call" | custom-call | flops 1024 | bytes 2800000 | tf_op jit(solution)/shard_map/pallas_call | solution.py:77
  350.3 15.9 %shard_map.552.grad.refs_4_ = bf16[1024,2048]{1,0:T(8,128)(2,1)} custom-call(bf16[256,2048]{1,0:T(8,128)(2,1)} %copy-done.6, bf16[256,2048]{1,0:T(8,128)(2,1)} %collective-permute-done.12.refs_1_, bf16[256,2048]{1,0:T(8,128)(2,1)} %collective-permute-done.29.refs_2_, bf16[256,2048]{1,0:T(8,128)(2,1)} %copy-done.13, ...), custom_call_target="tpu_custom_call" | custom-call | flops 1024 | bytes 3200000 | tf_op jit(solution)/shard_map/pallas_call | solution.py:77
  366.2 11.5 %shard_map.553 = (bf16[256,2048]{1,0:T(8,128)(2,1)}, bf16[256,2048]{1,0:T(8,128)(2,1)}) custom-call(bf16[1024,2048]{1,0:T(8,128)(2,1)} %shard_map.552.grad.refs_4_, bf16[1024,2048]{1,0:T(8,128)(2,1)} %all-gather.6.cloned.1.call-done.refs_4_.own, bf16[1024,2048]{1,0:T(8,128)(2,1)} %copy-done.1), custom_call_target="tpu_custom_call" | custom-call | flops 1024 | bytes 2200000 | tf_op jit(solution)/shard_map/pallas_call | solution.py:77
  397.8 11.5 %shard_map.557 = (bf16[256,2048]{1,0:T(8,128)(2,1)}, bf16[256,2048]{1,0:T(8,128)(2,1)}) custom-call(bf16[1024,2048]{1,0:T(8,128)(2,1)} %shard_map.552.grad.refs_4_, bf16[1024,2048]{1,0:T(8,128)(2,1)} %all-gather.6.cloned.1.call-done.refs_4_.own, bf16[1024,2048]{1,0:T(8,128)(2,1)} %copy-done.1), custom_call_target="tpu_custom_call" | custom-call | flops 1024 | bytes 2200000 | tf_op jit(solution)/shard_map/pallas_call | solution.py:77
  423.0 11.2 %shard_map.559 = (bf16[256,2048]{1,0:T(8,128)(2,1)}, f32[1,2048]{1,0:T(1,128)}, f32[1,2048]{1,0:T(1,128)}, bf16[256,512]{1,0:T(8,128)(2,1)}, bf16[256,512]{1,0:T...) custom-call(s32[2]{0:T(128)} %pad_add_fusion.where, f32[256,2048]{1,0:T(8,128)} %get-tuple-element.168.refs_0_, ...), custom_call_target="tpu_custom_call" | custom-call | flops 1024 | bytes 2200000 | tf_op jit(solution)/shard_map/pallas_call | solution.py:77
  452.4 15.5 %shard_map.561 = (bf16[3,512,512]{2,1,0:T(8,128)(2,1)}, bf16[256,2048]{1,0:T(8,128)(2,1)}, bf16[256,2048]{1,0:T(8,128)(2,1)}, bf16[256,2048]{1,0:T(8,128)(2,1)},...) custom-call(bf16[1024,512]{1,0:T(8,128)(2,1)} %get-tuple-element.187.q, ...), custom_call_target="tpu_custom_call" | custom-call | flops 1024 | bytes 3000000 | tf_op jit(solution)/shard_map/pallas_call | solution.py:77
  478.4 15.2 %shard_map.562 = (bf16[3,512,512]{2,1,0:T(8,128)(2,1)}, bf16[256,2048]{1,0:T(8,128)(2,1)}, bf16[256,2048]{1,0:T(8,128)(2,1)}, bf16[256,2048]{1,0:T(8,128)(2,1)},...) custom-call(bf16[1024,512]{1,0:T(8,128)(2,1)} %get-tuple-element.187.q, ...), custom_call_target="tpu_custom_call" | custom-call | flops 1024 | bytes 3000000 | tf_op jit(solution)/shard_map/pallas_call | solution.py:77
  497.3 12.4 %shard_map.563 = bf16[1024,1536]{1,0:T(8,128)(2,1)} custom-call(bf16[3,256,2048]{2,1,0:T(8,128)(2,1)} %get-tuple-element.161.refs_0_, bf16[3,256,2048]{2,1,0:T(8,128)(2,1)} %collective-permute-done.5.refs_1_, bf16[3,256,2048]{2,1,0:T(8,128)(2,1)} %collective-permute-done.6.refs_2_, bf16[3,256,2048]{2,1,0:T(8,128)(2,1)} %collective-permute-done.7.refs_3_, ...), custom_call_target="tpu_custom_call" | custom-call | flops 1024 | bytes 2400000 | tf_op jit(solution)/shard_map/pallas_call | solution.py:77
  509.7 12.4 %shard_map.564 = bf16[1024,1536]{1,0:T(8,128)(2,1)} custom-call(bf16[3,256,2048]{2,1,0:T(8,128)(2,1)} %get-tuple-element.161.refs_0_, bf16[3,256,2048]{2,1,0:T(8,128)(2,1)} %collective-permute-done.5.refs_1_, bf16[3,256,2048]{2,1,0:T(8,128)(2,1)} %collective-permute-done.6.refs_2_, bf16[3,256,2048]{2,1,0:T(8,128)(2,1)} %collective-permute-done.7.refs_3_, ...), custom_call_target="tpu_custom_call" | custom-call | flops 1024 | bytes 2400000 | tf_op jit(solution)/shard_map/pallas_call | solution.py:77
  529.7 14.0 %shard_map.565 = (bf16[256,2048]{1,0:T(8,128)(2,1)}, bf16[256,2048]{1,0:T(8,128)(2,1)}, bf16[256,2048]{1,0:T(8,128)(2,1)}, bf16[256,2048]{1,0:T(8,128)(2,1)}) custom-call(bf16[1024,2048]{1,0:T(8,128)(2,1)} %get-tuple-element.221.activated, bf16[2048,2048]{1,0:T(8,128)(2,1)} %all-gather.8.cloned.1.call-done.refs_4_.weight), custom_call_target="tpu_custom_call" | custom-call | flops 1024 | bytes 2800000 | tf_op jit(solution)/shard_map/pallas_call | solution.py:77
  548.8 49.5 %collective-permute-done.53 = bf16[1024,1536]{1,0:T(8,128)(2,1)S(1)} collective-permute-done((bf16[1024,1536]{1,0:T(8,128)(2,1)}, bf16[1024,1536]{1,0:T(8,128)(2,1)S(1)}, u32[]{:S(2)}, u32[]{:S(2)}) %collective-permute-start.53) | collective-permute-done | bytes 3145760 | tf_op jit(solution)/shard_map/ppermute | solution.py:519
  598.3 23.1 %collective-permute-done.55 = bf16[1024,512]{1,0:T(8,128)(2,1)S(1)} collective-permute-done((bf16[1024,512]{1,0:T(8,128)(2,1)}, bf16[1024,512]{1,0:T(8,128)(2,1)S(1)}, u32[]{:S(2)}, u32[]{:S(2)}) %collective-permute-start.55) | collective-permute-done | bytes 1048608 | tf_op jit(solution)/shard_map/ppermute | solution.py:519
  635.3 26.0 %shard_map.566 = (bf16[9,256,2048]{2,1,0:T(8,128)(2,1)}, f32[36,2048]{1,0:T(8,128)}, f32[36,36]{1,0:T(8,128)}, f32[2,2048]{1,0:T(2,128)}, f32[1,2048]{1,0:T(1,128)}) custom-call(s32[2]{0:T(128)} %pad_add_fusion.where, bf16[9,256,2048]{2,1,0:T(8,128)(2,1)} %refs_0_.1, f32[4,256,2048]{2,1,0:T(8,128)} %get-tuple-element.167.refs_12_.refs_1_, ...), custom_call_target="tpu_custom_call" | custom-call | flops 1024 | bytes 90000000 | tf_op jit(solution)/shard_map/pallas_call | solution.py:77
  768.3 13.7 %shard_map.568 = (f32[64,6144]{1,0:T(8,128)}, f32[64,6144]{1,0:T(8,128)}, f32[64,2048]{1,0:T(8,128)}, f32[64,2048]{1,0:T(8,128)}, f32[64,8192]{1,0:T(8,128)}, /*...) custom-call(f32[1]{0:T(128)} %bitcast.19.clip_ref, ...), custom_call_target="tpu_custom_call" | custom-call | flops 1024 | bytes 2800000 | tf_op jit(solution)/shard_map/pallas_call | solution.py:77
  797.4 11.3 %shard_map.569 = (f32[64,6144]{1,0:T(8,128)}, bf16[64,6144]{1,0:T(8,128)(2,1)}, f32[64,2048]{1,0:T(8,128)}, bf16[64,2048]{1,0:T(8,128)(2,1)}, f32[64,8192]{1,0:T...) custom-call(f32[6]{0:T(128)} %get-tuple-element.509.trust_ref, ...), custom_call_target="tpu_custom_call" | custom-call | flops 1024 | bytes 2000000 | tf_op jit(solution)/shard_map/pallas_call | solution.py:77
  (444 shorter events, 342.7 us)
Async XLA Ops:
  7.2 109.8 %all-gather.4.cloned.1.call-start = ((), (), s32[]{:S(2)}) async-start(), calls=%async_computation.3 | async-start | bytes 5242880 | tf_op jit(solution)/shard_map/all_gather | solution.py:531
  30.0 184.2 %all-gather.6.cloned.1.call-start = ((), (), s32[]{:S(2)}) async-start(), calls=%async_computation.4 | async-start | bytes 5242880 | tf_op jit(solution)/shard_map/all_gather | solution.py:531
  51.6 298.7 %all-gather.8.cloned.1.call-start = ((), (), s32[]{:S(2)}) async-start(), calls=%async_computation.5 | async-start | bytes 10485760 | tf_op jit(solution)/shard_map/all_gather | solution.py:531
  112.8 414.1 %reduce-scatter.4.cloned.1.call-start = ((), (), s32[]{:S(2)}) async-start(), calls=%async_computation.6 | async-start | bytes 10485760 | tf_op jit(solution)/shard_map/reduce_scatter | solution.py:534
  112.9 68.2 %collective-permute-start.5 = (bf16[3,256,2048]{2,1,0:T(8,128)(2,1)}, bf16[3,256,2048]{2,1,0:T(8,128)(2,1)}, u32[]{:S(2)}, u32[]{:S(2)}) collective-permute-start(bf16[3,256,2048]{2,1,0:T(8,128)(2,1)} %get-tuple-element.161.refs_0_), channel_id=1, source_target_pairs={{0,2},{1,3},{2,0},{3,1},{4,6},{5,7},{6,4},{7,5},{8,10},{9,11},{10,... | collective-permute-start | bytes 9437192 | tf_op jit(solution)/shard_map/ppermute | solution.py:519
  117.0 92.5 %collective-permute-start.11 = (bf16[1024,2048]{1,0:T(8,128)(2,1)}, bf16[1024,2048]{1,0:T(8,128)(2,1)S(1)}, u32[]{:S(2)}, u32[]{:S(2)}) collective-permute-start(bf16[1024,2048]{1,0:T(8,128)(2,1)} %all-gather.4.cloned.1.call-done.refs_4_.own), channel_id=1, source_target_pairs={{0,4},{1,5},{2,6},{3,7},{4,0},{5,1},{6,2},{7,3},{8,12},{9,13},{10,... | collective-permute-start | bytes 12582920 | tf_op jit(solution)/shard_map/ppermute | solution.py:519
  118.5 95.6 %collective-permute-start.6 = (bf16[3,256,2048]{2,1,0:T(8,128)(2,1)}, bf16[3,256,2048]{2,1,0:T(8,128)(2,1)}, u32[]{:S(2)}, u32[]{:S(2)}) collective-permute-start(bf16[3,256,2048]{2,1,0:T(8,128)(2,1)} %get-tuple-element.161.refs_0_), channel_id=1, source_target_pairs={{0,1},{1,0},{2,3},{3,2},{4,5},{5,4},{6,7},{7,6},{8,9},{9,8},{10,11... | collective-permute-start | bytes 9437192 | tf_op jit(solution)/shard_map/ppermute | solution.py:519
  188.2 45.7 %collective-permute-start.16 = (bf16[1024,512]{1,0:T(8,128)(2,1)}, bf16[1024,512]{1,0:T(8,128)(2,1)}, u32[]{:S(2)}, u32[]{:S(2)}) collective-permute-start(bf16[1024,512]{1,0:T(8,128)(2,1)} %slice.138.refs_4_.refs_6_), channel_id=1, source_target_pairs={{0,2},{1,3},{2,0},{3,1},{4,6},{5,7},{6,4},{7,5},{8,10},{9,11},{10,... | collective-permute-start | bytes 3145736 | tf_op jit(solution)/shard_map/ppermute | solution.py:519
  212.6 42.5 %collective-permute-start.17 = (bf16[1024,512]{1,0:T(8,128)(2,1)}, bf16[1024,512]{1,0:T(8,128)(2,1)}, u32[]{:S(2)}, u32[]{:S(2)}) collective-permute-start(bf16[1024,512]{1,0:T(8,128)(2,1)} %slice.139.refs_5_.refs_7_), channel_id=1, source_target_pairs={{0,2},{1,3},{2,0},{3,1},{4,6},{5,7},{6,4},{7,5},{8,10},{9,11},{10,... | collective-permute-start | bytes 3145736 | tf_op jit(solution)/shard_map/ppermute | solution.py:519
  214.1 97.4 %collective-permute-start.28 = (bf16[1024,2048]{1,0:T(8,128)(2,1)}, bf16[1024,2048]{1,0:T(8,128)(2,1)S(1)}, u32[]{:S(2)}, u32[]{:S(2)}) collective-permute-start(bf16[1024,2048]{1,0:T(8,128)(2,1)} %all-gather.6.cloned.1.call-done.refs_4_.own), channel_id=1, source_target_pairs={{0,4},{1,5},{2,6},{3,7},{4,0},{5,1},{6,2},{7,3},{8,12},{9,13},{10,... | collective-permute-start | bytes 12582920 | tf_op jit(solution)/shard_map/ppermute | solution.py:519
  215.6 42.0 %collective-permute-start.18 = (bf16[1024,512]{1,0:T(8,128)(2,1)}, bf16[1024,512]{1,0:T(8,128)(2,1)S(1)}, u32[]{:S(2)}, u32[]{:S(2)}) collective-permute-start(bf16[1024,512]{1,0:T(8,128)(2,1)} %slice.138.refs_4_.refs_6_), channel_id=1, source_target_pairs={{0,1},{1,0},{2,3},{3,2},{4,5},{5,4},{6,7},{7,6},{8,9},{9,8},{10,11... | collective-permute-start | bytes 3145736 | tf_op jit(solution)/shard_map/ppermute | solution.py:519
  217.1 58.6 %collective-permute-start.19 = (bf16[1024,512]{1,0:T(8,128)(2,1)}, bf16[1024,512]{1,0:T(8,128)(2,1)}, u32[]{:S(2)}, u32[]{:S(2)}) collective-permute-start(bf16[1024,512]{1,0:T(8,128)(2,1)} %slice.139.refs_5_.refs_7_), channel_id=1, source_target_pairs={{0,1},{1,0},{2,3},{3,2},{4,5},{5,4},{6,7},{7,6},{8,9},{9,8},{10,11... | collective-permute-start | bytes 3145736 | tf_op jit(solution)/shard_map/ppermute | solution.py:519
  350.3 277.0 %reduce-scatter.6.cloned.1.call-start = ((), (), s32[]{:S(2)}) async-start(), calls=%async_computation.7 | async-start | bytes 5242880 | tf_op jit(solution)/shard_map/reduce_scatter | solution.py:534
  409.4 42.0 %collective-permute-start.33 = (bf16[256,2048]{1,0:T(8,128)(2,1)S(1)}, bf16[256,2048]{1,0:T(8,128)(2,1)S(1)}, u32[]{:S(2)}, u32[]{:S(2)}) collective-permute-start(bf16[256,2048]{1,0:T(8,128)(2,1)S(1)} %copy-done.18), channel_id=1, source_target_pairs={{0,4},{1,5},{2,6},{3,7},{4,0},{5,1},{6,2},{7,3},{8,12},{9,13},{10,... | collective-permute-start | bytes 3145736 | tf_op jit(solution)/shard_map/ppermute | solution.py:519
  471.3 50.9 %collective-permute-start.34 = (bf16[512,2048]{1,0:T(8,128)(2,1)}, bf16[512,2048]{1,0:T(8,128)(2,1)}, u32[]{:S(2)}, u32[]{:S(2)}) collective-permute-start(bf16[512,2048]{1,0:T(8,128)(2,1)} %shard_map.556), channel_id=1, source_target_pairs={{0,4},{1,5},{2,6},{3,7},{4,0},{5,1},{6,2},{7,3},{8,12},{9,13},{10,... | collective-permute-start | bytes 6291464 | tf_op jit(solution)/shard_map/ppermute | solution.py:519
  476.3 45.8 %collective-permute-start.46 = (bf16[1024,512]{1,0:T(8,128)(2,1)}, bf16[1024,512]{1,0:T(8,128)(2,1)}, u32[]{:S(2)}, u32[]{:S(2)}) collective-permute-start(bf16[1024,512]{1,0:T(8,128)(2,1)} %get-tuple-element.453), channel_id=1, source_target_pairs={{0,2},{1,3},{2,0},{3,1},{4,6},{5,7},{6,4},{7,5},{8,10},{9,11},{10,... | collective-permute-start | bytes 3145736 | tf_op jit(solution)/shard_map/ppermute | solution.py:519
  527.0 202.9 %reduce-scatter.8.cloned.1.call-start = ((), (), s32[]{:S(2)}) async-start(), calls=%async_computation.8 | async-start | bytes 5242880 | tf_op jit(solution)/shard_map/reduce_scatter | solution.py:534
  527.2 71.1 %collective-permute-start.53 = (bf16[1024,1536]{1,0:T(8,128)(2,1)}, bf16[1024,1536]{1,0:T(8,128)(2,1)S(1)}, u32[]{:S(2)}, u32[]{:S(2)}) collective-permute-start(bf16[1024,1536]{1,0:T(8,128)(2,1)} %shard_map.563), channel_id=1, source_target_pairs={{0,4},{1,5},{2,6},{3,7},{4,0},{5,1},{6,2},{7,3},{8,12},{9,13},{10,... | collective-permute-start | bytes 9437192 | tf_op jit(solution)/shard_map/ppermute | solution.py:519
  528.6 98.6 %collective-permute-start.52 = (bf16[3,256,2048]{2,1,0:T(8,128)(2,1)}, bf16[3,256,2048]{2,1,0:T(8,128)(2,1)}, u32[]{:S(2)}, u32[]{:S(2)}) collective-permute-start(bf16[3,256,2048]{2,1,0:T(8,128)(2,1)} %pad_maximum_fusion.1), channel_id=1, source_target_pairs={{0,2},{1,3},{2,0},{3,1},{4,6},{5,7},{6,4},{7,5},{8,10},{9,11},{10,... | collective-permute-start | bytes 9437192 | tf_op jit(solution)/shard_map/ppermute | solution.py:519
  543.7 77.7 %collective-permute-start.55 = (bf16[1024,512]{1,0:T(8,128)(2,1)}, bf16[1024,512]{1,0:T(8,128)(2,1)S(1)}, u32[]{:S(2)}, u32[]{:S(2)}) collective-permute-start(bf16[1024,512]{1,0:T(8,128)(2,1)} %get-tuple-element.454), channel_id=1, source_target_pairs={{0,2},{1,3},{2,0},{3,1},{4,6},{5,7},{6,4},{7,5},{8,10},{9,11},{10,... | collective-permute-start | bytes 3145736 | tf_op jit(solution)/shard_map/ppermute | solution.py:519
  546.8 74.6 %collective-permute-start.56 = (bf16[1024,512]{1,0:T(8,128)(2,1)S(1)}, bf16[1024,512]{1,0:T(8,128)(2,1)S(1)}, u32[]{:S(2)}, u32[]{:S(2)}) collective-permute-start(bf16[1024,512]{1,0:T(8,128)(2,1)S(1)} %add_convert_fusion.4), channel_id=1, source_target_pairs={{0,4},{1,5},{2,6},{3,7},{4,0},{5,1},{6,2},{7,3},{8,12},{9,13},{10,... | collective-permute-start | bytes 3145736 | tf_op jit(solution)/shard_map/ppermute | solution.py:519
  547.5 79.8 %collective-permute-start.49 = (bf16[256,2048]{1,0:T(8,128)(2,1)}, bf16[256,2048]{1,0:T(8,128)(2,1)}, u32[]{:S(2)}, u32[]{:S(2)}) collective-permute-start(bf16[256,2048]{1,0:T(8,128)(2,1)} %get-tuple-element.231), channel_id=1, source_target_pairs={{0,1},{1,0},{2,3},{3,2},{4,5},{5,4},{6,7},{7,6},{8,9},{9,8},{10,11... | collective-permute-start | bytes 3145736 | tf_op jit(solution)/shard_map/ppermute | solution.py:519
  701.1 82.9 %collective-permute-start.47 = (bf16[256,2048]{1,0:T(8,128)(2,1)}, bf16[256,2048]{1,0:T(8,128)(2,1)}, u32[]{:S(2)}, u32[]{:S(2)}) collective-permute-start(bf16[256,2048]{1,0:T(8,128)(2,1)} %get-tuple-element.223), channel_id=1, source_target_pairs={{0,1},{1,0},{2,3},{3,2},{4,5},{5,4},{6,7},{7,6},{8,9},{9,8},{10,11... | collective-permute-start | bytes 3145736 | tf_op jit(solution)/shard_map/ppermute | solution.py:519
  701.9 82.1 %collective-permute-start.57 = (bf16[256,2048]{1,0:T(8,128)(2,1)}, bf16[256,2048]{1,0:T(8,128)(2,1)}, u32[]{:S(2)}, u32[]{:S(2)}) collective-permute-start(bf16[256,2048]{1,0:T(8,128)(2,1)} %add_convert_fusion.5), channel_id=1, source_target_pairs={{0,2},{1,3},{2,0},{3,1},{4,6},{5,7},{6,4},{7,5},{8,10},{9,11},{10,... | collective-permute-start | bytes 3145736 | tf_op jit(solution)/shard_map/ppermute | solution.py:519
  (132 other events, 1682.1 us)
Sparse Core Ops, SparseCore 0:
  30.1 86.8 all-gather.3
  119.2 79.2 all-gather.5
  200.7 148.1 all-gather.7
  351.1 147.9 reduce-scatter.3
  527.1 80.0 reduce-scatter.5
  627.4 83.7 reduce-scatter.7

commit v4 on v3

--- a/solution.py
+++ b/solution.py
@@ -1026,17 +1026,18 @@
     small = jnp.concatenate(
         [grad_mixer_in, grad_gains, grad_gain_ffn, grad_bias_attn, grad_bias_ffn], axis=0
     )
+    down_sums = after(down_sums, attn_both)
+    down_sums = down_sums.reshape(2, units, width)
+    down_mine = jnp.where(low_y, down_sums[0], down_sums[1])
+    down_theirs = jnp.where(low_y, down_sums[1], down_sums[0])
+    down_theirs = links.swap_y(down_theirs)
+    shard_down = down_mine.astype(F32) + down_theirs.astype(F32)
+    small = after(small, down_theirs)
     top = devices.bit_length() - 2
     inner = 1 << (links.y_bit - 2)
     pieces = small.reshape(small.shape[0], devices // (8 * inner), 2, inner * 4 * rows)
     take = lambda array, at, axis: lax.dynamic_index_in_dim(array, at, axis, keepdims=False)
     pieces = take(pieces, links.y, 2) + links.swap_y(take(pieces, 1 - links.y, 2))
-    down_sums = after(down_sums, pieces)
-    down_sums = down_sums.reshape(2, units, width)
-    down_mine = jnp.where(low_y, down_sums[0], down_sums[1])
-    down_theirs = jnp.where(low_y, down_sums[1], down_sums[0])
-    down_theirs = links.swap_y(down_theirs)
-    shard_down = down_mine.astype(F32) + down_theirs.astype(F32)
     bits = [k for k in range(top, 1, -1) if k != links.y_bit]
     while bits:
         pair, bits = bits[:2], bits[2:]
@@ -1047,7 +1048,7 @@
             mask = sum(((turn >> e) & 1) << k for e, k in enumerate(reversed(pair)))
             total = total + links.swap(take(pieces, at ^ turn, 1), mask)
         pieces = total
-    pieces = after(pieces, down_theirs).reshape(small.shape[0], 4, rows)
+    pieces = pieces.reshape(small.shape[0], 4, rows)
     small = take(pieces, links.rank, 1)
     for turn in TURNS[1:]:
         small = small + links.swap(take(pieces, links.rank ^ turn, 1), turn)

time: 827 us -> 838 us (1.013)
  transfers between devices with their start and end apart: 99 -> 99, of which waited for: 39 -> 38; matrix products, arithmetic and copies ran while one was open for 12% -> 12% of each run, Pallas kernels for 32% -> 32%
where the time goes in v4:
time: 838 us; the launch traced here: 832 us
  waiting for transfers between devices  329 us (39%)
  Pallas kernels  275 us (33%)
  starting transfers between devices  89.6 us (11%)
  other arithmetic  78.2 us (9%)
  local copies, waits for them, and re-layouts  38.8 us (5%)
  between operations  21.4 us (3%)
    ppermute x93, waiting for transfers between devices, swap(): lax.ppermute(value, 'dp', [(j, j ^ bit) for j in range(self.devices)])  328 us
    pallas_call x23, Pallas kernels, run(): pl.pallas_call(kernel, grid=grid, in_specs=[spec for _, spec in ins], out...  275 us
    ppermute x93, starting transfers between devices, swap(): lax.ppermute(value, 'dp', [(j, j ^ bit) for j in range(self.devices)])  78.1 us
  transfers between devices with their start and end apart: 99, of which 38 were waited for; matrix products, arithmetic and copies ran while one was open for 12% of the time, Pallas kernels for 32%

profile of v4, /device:TPU:0, one launch (start us, length us, event | category | flops | bytes accessed | tf_op | source)
XLA Modules:
  0.0 831.6 jit_solution(4979138890723679831)
XLA Ops:
  51.6 11.3 %all-gather.8.cloned.1.call-start = ((), (), s32[]{:S(2)}) async-start(), calls=%async_computation.5 | async-start | bytes 10485760 | tf_op jit(solution)/shard_map/all_gather | solution.py:531
  82.2 11.5 %collective-permute-done.4 = bf16[41,1024]{1,0:T(8,128)(2,1)S(1)} collective-permute-done((bf16[41,1024]{1,0:T(8,128)(2,1)S(1)}, bf16[41,1024]{1,0:T(8,128)(2,1)S(1)}, u32[]{:S(2)}, u32[]{:S(2)}) %collective-permute-start.4) | collective-permute-done | bytes 84000 | tf_op jit(solution)/shard_map/ppermute | solution.py:519
  95.7 14.2 %shard_map.547 = (f32[4,256,2048]{2,1,0:T(8,128)}, bf16[3,256,2048]{2,1,0:T(8,128)(2,1)}, f32[256,36]{1,0:T(8,128)}, f32[256,36]{1,0:T(8,128)}) custom-call(s32[2]{0:T(128)} %pad_add_fusion.where, bf16[9,256,2048]{2,1,0:T(8,128)(2,1)} %refs_0_.1, bf16[36,2048]{1,0:T(8,128)(2,1)} %fusion.7.w_mix.refs_12_, f32[3,2048]{1,0:T(4,128)} %fusion.19.gain.refs_13_.refs_1_, ...), custom_call_target="tpu_custom_call" | custom-call | flops 1024 | bytes 2800000 | tf_op jit(solution)/shard_map/pallas_call | solution.py:77
  118.5 62.5 %collective-permute-done.5.refs_1_ = bf16[3,256,2048]{2,1,0:T(8,128)(2,1)} collective-permute-done((bf16[3,256,2048]{2,1,0:T(8,128)(2,1)}, bf16[3,256,2048]{2,1,0:T(8,128)(2,1)}, u32[]{:S(2)}, u32[]{:S(2)}) %collective-permute-start.5) | collective-permute-done | bytes 3145760 | tf_op jit(solution)/shard_map/ppermute | solution.py:519
  188.8 20.8 %collective-permute-done.11.refs_5_.other = bf16[1024,2048]{1,0:T(8,128)(2,1)S(1)} collective-permute-done((bf16[1024,2048]{1,0:T(8,128)(2,1)}, bf16[1024,2048]{1,0:T(8,128)(2,1)S(1)}, u32[]{:S(2)}, u32[]{:S(2)}) %collective-permute-start.11) | collective-permute-done | bytes 4194336 | tf_op jit(solution)/shard_map/ppermute | solution.py:519
  217.6 16.2 %shard_map.548 = (bf16[1024,512]{1,0:T(8,128)(2,1)}, bf16[1024,512]{1,0:T(8,128)(2,1)}, bf16[1024,512]{1,0:T(8,128)(2,1)}, bf16[1024,512]{1,0:T(8,128)(2,1)}) custom-call(bf16[3,256,2048]{2,1,0:T(8,128)(2,1)} %get-tuple-element.161.refs_0_, bf16[3,256,2048]{2,1,0:T(8,128)(2,1)} %collective-permute-done.5.refs_1_, ...), custom_call_target="tpu_custom_call" | custom-call | flops 1024 | bytes 3200000 | tf_op jit(solution)/shard_map/pallas_call | solution.py:77
  233.9 21.2 %collective-permute-done.17.refs_7_.refs_9_ = bf16[1024,512]{1,0:T(8,128)(2,1)} collective-permute-done((bf16[1024,512]{1,0:T(8,128)(2,1)}, bf16[1024,512]{1,0:T(8,128)(2,1)}, u32[]{:S(2)}, u32[]{:S(2)}) %collective-permute-start.17) | collective-permute-done | bytes 1048608 | tf_op jit(solution)/shard_map/ppermute | solution.py:519
  287.4 24.1 %collective-permute-done.22.refs_1_ = bf16[256,2048]{1,0:T(8,128)(2,1)S(1)} collective-permute-done((bf16[256,2048]{1,0:T(8,128)(2,1)}, bf16[256,2048]{1,0:T(8,128)(2,1)S(1)}, u32[]{:S(2)}, u32[]{:S(2)}) %collective-permute-start.22) | collective-permute-done | bytes 1048608 | tf_op jit(solution)/shard_map/ppermute | solution.py:519
  315.8 17.1 %shard_map.550 = (bf16[1024,2048]{1,0:T(8,128)(2,1)}, f32[1024,2048]{1,0:T(8,128)}) custom-call(bf16[256,2048]{1,0:T(8,128)(2,1)} %get-tuple-element.169.refs_0_, bf16[256,2048]{1,0:T(8,128)(2,1)} %copy-done.4, bf16[256,2048]{1,0:T(8,128)(2,1)} %collective-permute-done.23.refs_2_, bf16[256,2048]{1,0:T(8,128)(2,1)} %collective-permute-done.24.refs_3_, ...), custom_call_target="tpu_custom_call" | custom-call | flops 1024 | bytes 3400000 | tf_op jit(solution)/shard_map/pallas_call | solution.py:77
  336.7 14.1 %shard_map.551 = bf16[2048,2048]{1,0:T(8,128)(2,1)} custom-call(bf16[1024,2048]{1,0:T(8,128)(2,1)} %get-tuple-element.221.activated, bf16[256,2048]{1,0:T(8,128)(2,1)} %copy-done.6, bf16[256,2048]{1,0:T(8,128)(2,1)} %collective-permute-done.12.refs_1_, bf16[256,2048]{1,0:T(8,128)(2,1)} %collective-permute-done.29.refs_2_, bf16[256,2048]{1,0:T(8,128)(2,1)} %copy-done.13), custom_call_target="tpu_custom_call" | custom-call | flops 1024 | bytes 2800000 | tf_op jit(solution)/shard_map/pallas_call | solution.py:77
  350.9 15.9 %shard_map.552.grad.refs_4_ = bf16[1024,2048]{1,0:T(8,128)(2,1)} custom-call(bf16[256,2048]{1,0:T(8,128)(2,1)} %copy-done.6, bf16[256,2048]{1,0:T(8,128)(2,1)} %collective-permute-done.12.refs_1_, bf16[256,2048]{1,0:T(8,128)(2,1)} %collective-permute-done.29.refs_2_, bf16[256,2048]{1,0:T(8,128)(2,1)} %copy-done.13, ...), custom_call_target="tpu_custom_call" | custom-call | flops 1024 | bytes 3200000 | tf_op jit(solution)/shard_map/pallas_call | solution.py:77
  366.8 11.5 %shard_map.553 = (bf16[256,2048]{1,0:T(8,128)(2,1)}, bf16[256,2048]{1,0:T(8,128)(2,1)}) custom-call(bf16[1024,2048]{1,0:T(8,128)(2,1)} %shard_map.552.grad.refs_4_, bf16[1024,2048]{1,0:T(8,128)(2,1)} %all-gather.6.cloned.1.call-done.refs_4_.own, bf16[1024,2048]{1,0:T(8,128)(2,1)} %copy-done.1), custom_call_target="tpu_custom_call" | custom-call | flops 1024 | bytes 2200000 | tf_op jit(solution)/shard_map/pallas_call | solution.py:77
  398.4 11.5 %shard_map.557 = (bf16[256,2048]{1,0:T(8,128)(2,1)}, bf16[256,2048]{1,0:T(8,128)(2,1)}) custom-call(bf16[1024,2048]{1,0:T(8,128)(2,1)} %shard_map.552.grad.refs_4_, bf16[1024,2048]{1,0:T(8,128)(2,1)} %all-gather.6.cloned.1.call-done.refs_4_.own, bf16[1024,2048]{1,0:T(8,128)(2,1)} %copy-done.1), custom_call_target="tpu_custom_call" | custom-call | flops 1024 | bytes 2200000 | tf_op jit(solution)/shard_map/pallas_call | solution.py:77
  423.6 11.2 %shard_map.559 = (bf16[256,2048]{1,0:T(8,128)(2,1)}, f32[1,2048]{1,0:T(1,128)}, f32[1,2048]{1,0:T(1,128)}, bf16[256,512]{1,0:T(8,128)(2,1)}, bf16[256,512]{1,0:T...) custom-call(s32[2]{0:T(128)} %pad_add_fusion.where, f32[256,2048]{1,0:T(8,128)} %get-tuple-element.168.refs_0_, ...), custom_call_target="tpu_custom_call" | custom-call | flops 1024 | bytes 2200000 | tf_op jit(solution)/shard_map/pallas_call | solution.py:77
  453.0 15.5 %shard_map.561 = (bf16[3,512,512]{2,1,0:T(8,128)(2,1)}, bf16[256,2048]{1,0:T(8,128)(2,1)}, bf16[256,2048]{1,0:T(8,128)(2,1)}, bf16[256,2048]{1,0:T(8,128)(2,1)},...) custom-call(bf16[1024,512]{1,0:T(8,128)(2,1)} %get-tuple-element.187.q, ...), custom_call_target="tpu_custom_call" | custom-call | flops 1024 | bytes 3000000 | tf_op jit(solution)/shard_map/pallas_call | solution.py:77
  479.0 15.2 %shard_map.562 = (bf16[3,512,512]{2,1,0:T(8,128)(2,1)}, bf16[256,2048]{1,0:T(8,128)(2,1)}, bf16[256,2048]{1,0:T(8,128)(2,1)}, bf16[256,2048]{1,0:T(8,128)(2,1)},...) custom-call(bf16[1024,512]{1,0:T(8,128)(2,1)} %get-tuple-element.187.q, ...), custom_call_target="tpu_custom_call" | custom-call | flops 1024 | bytes 3000000 | tf_op jit(solution)/shard_map/pallas_call | solution.py:77
  497.9 12.3 %shard_map.563 = bf16[1024,1536]{1,0:T(8,128)(2,1)} custom-call(bf16[3,256,2048]{2,1,0:T(8,128)(2,1)} %get-tuple-element.161.refs_0_, bf16[3,256,2048]{2,1,0:T(8,128)(2,1)} %collective-permute-done.5.refs_1_, bf16[3,256,2048]{2,1,0:T(8,128)(2,1)} %collective-permute-done.6.refs_2_, bf16[3,256,2048]{2,1,0:T(8,128)(2,1)} %collective-permute-done.7.refs_3_, ...), custom_call_target="tpu_custom_call" | custom-call | flops 1024 | bytes 2400000 | tf_op jit(solution)/shard_map/pallas_call | solution.py:77
  510.2 12.4 %shard_map.564 = bf16[1024,1536]{1,0:T(8,128)(2,1)} custom-call(bf16[3,256,2048]{2,1,0:T(8,128)(2,1)} %get-tuple-element.161.refs_0_, bf16[3,256,2048]{2,1,0:T(8,128)(2,1)} %collective-permute-done.5.refs_1_, bf16[3,256,2048]{2,1,0:T(8,128)(2,1)} %collective-permute-done.6.refs_2_, bf16[3,256,2048]{2,1,0:T(8,128)(2,1)} %collective-permute-done.7.refs_3_, ...), custom_call_target="tpu_custom_call" | custom-call | flops 1024 | bytes 2400000 | tf_op jit(solution)/shard_map/pallas_call | solution.py:77
  530.2 14.1 %shard_map.565 = (bf16[256,2048]{1,0:T(8,128)(2,1)}, bf16[256,2048]{1,0:T(8,128)(2,1)}, bf16[256,2048]{1,0:T(8,128)(2,1)}, bf16[256,2048]{1,0:T(8,128)(2,1)}) custom-call(bf16[1024,2048]{1,0:T(8,128)(2,1)} %get-tuple-element.221.activated, bf16[2048,2048]{1,0:T(8,128)(2,1)} %all-gather.8.cloned.1.call-done.refs_4_.weight), custom_call_target="tpu_custom_call" | custom-call | flops 1024 | bytes 2800000 | tf_op jit(solution)/shard_map/pallas_call | solution.py:77
  549.4 49.5 %collective-permute-done.53 = bf16[1024,1536]{1,0:T(8,128)(2,1)S(1)} collective-permute-done((bf16[1024,1536]{1,0:T(8,128)(2,1)}, bf16[1024,1536]{1,0:T(8,128)(2,1)S(1)}, u32[]{:S(2)}, u32[]{:S(2)}) %collective-permute-start.53) | collective-permute-done | bytes 3145760 | tf_op jit(solution)/shard_map/ppermute | solution.py:519
  598.9 23.0 %collective-permute-done.55 = bf16[1024,512]{1,0:T(8,128)(2,1)S(1)} collective-permute-done((bf16[1024,512]{1,0:T(8,128)(2,1)}, bf16[1024,512]{1,0:T(8,128)(2,1)S(1)}, u32[]{:S(2)}, u32[]{:S(2)}) %collective-permute-start.55) | collective-permute-done | bytes 1048608 | tf_op jit(solution)/shard_map/ppermute | solution.py:519
  635.9 26.2 %shard_map.566 = (bf16[9,256,2048]{2,1,0:T(8,128)(2,1)}, f32[36,2048]{1,0:T(8,128)}, f32[36,36]{1,0:T(8,128)}, f32[2,2048]{1,0:T(2,128)}, f32[1,2048]{1,0:T(1,128)}) custom-call(s32[2]{0:T(128)} %pad_add_fusion.where, bf16[9,256,2048]{2,1,0:T(8,128)(2,1)} %refs_0_.1, f32[4,256,2048]{2,1,0:T(8,128)} %get-tuple-element.167.refs_12_.refs_1_, ...), custom_call_target="tpu_custom_call" | custom-call | flops 1024 | bytes 90000000 | tf_op jit(solution)/shard_map/pallas_call | solution.py:77
  673.0 19.0 %collective-permute-done.69 = f32[36,36]{1,0:T(8,128)S(1)} collective-permute-done((f32[36,36]{1,0:T(8,128)S(1)}, f32[36,36]{1,0:T(8,128)S(1)}, u32[]{:S(2)}, u32[]{:S(2)}) %collective-permute-start.69) | collective-permute-done | bytes 5216 | tf_op jit(solution)/shard_map/ppermute | solution.py:519
  777.4 13.9 %shard_map.568 = (f32[64,6144]{1,0:T(8,128)}, f32[64,6144]{1,0:T(8,128)}, f32[64,2048]{1,0:T(8,128)}, f32[64,2048]{1,0:T(8,128)}, f32[64,8192]{1,0:T(8,128)}, /*...) custom-call(f32[1]{0:T(128)} %bitcast.19.clip_ref, ...), custom_call_target="tpu_custom_call" | custom-call | flops 1024 | bytes 2800000 | tf_op jit(solution)/shard_map/pallas_call | solution.py:77
  (446 shorter events, 346.1 us)
Async XLA Ops:
  7.2 109.8 %all-gather.4.cloned.1.call-start = ((), (), s32[]{:S(2)}) async-start(), calls=%async_computation.3 | async-start | bytes 5242880 | tf_op jit(solution)/shard_map/all_gather | solution.py:531
  30.0 184.2 %all-gather.6.cloned.1.call-start = ((), (), s32[]{:S(2)}) async-start(), calls=%async_computation.4 | async-start | bytes 5242880 | tf_op jit(solution)/shard_map/all_gather | solution.py:531
  51.6 299.3 %all-gather.8.cloned.1.call-start = ((), (), s32[]{:S(2)}) async-start(), calls=%async_computation.5 | async-start | bytes 10485760 | tf_op jit(solution)/shard_map/all_gather | solution.py:531
  112.8 414.6 %reduce-scatter.4.cloned.1.call-start = ((), (), s32[]{:S(2)}) async-start(), calls=%async_computation.6 | async-start | bytes 10485760 | tf_op jit(solution)/shard_map/reduce_scatter | solution.py:534
  112.9 68.2 %collective-permute-start.5 = (bf16[3,256,2048]{2,1,0:T(8,128)(2,1)}, bf16[3,256,2048]{2,1,0:T(8,128)(2,1)}, u32[]{:S(2)}, u32[]{:S(2)}) collective-permute-start(bf16[3,256,2048]{2,1,0:T(8,128)(2,1)} %get-tuple-element.161.refs_0_), channel_id=1, source_target_pairs={{0,2},{1,3},{2,0},{3,1},{4,6},{5,7},{6,4},{7,5},{8,10},{9,11},{10,... | collective-permute-start | bytes 9437192 | tf_op jit(solution)/shard_map/ppermute | solution.py:519
  117.0 92.5 %collective-permute-start.11 = (bf16[1024,2048]{1,0:T(8,128)(2,1)}, bf16[1024,2048]{1,0:T(8,128)(2,1)S(1)}, u32[]{:S(2)}, u32[]{:S(2)}) collective-permute-start(bf16[1024,2048]{1,0:T(8,128)(2,1)} %all-gather.4.cloned.1.call-done.refs_4_.own), channel_id=1, source_target_pairs={{0,4},{1,5},{2,6},{3,7},{4,0},{5,1},{6,2},{7,3},{8,12},{9,13},{10,... | collective-permute-start | bytes 12582920 | tf_op jit(solution)/shard_map/ppermute | solution.py:519
  118.5 95.6 %collective-permute-start.6 = (bf16[3,256,2048]{2,1,0:T(8,128)(2,1)}, bf16[3,256,2048]{2,1,0:T(8,128)(2,1)}, u32[]{:S(2)}, u32[]{:S(2)}) collective-permute-start(bf16[3,256,2048]{2,1,0:T(8,128)(2,1)} %get-tuple-element.161.refs_0_), channel_id=1, source_target_pairs={{0,1},{1,0},{2,3},{3,2},{4,5},{5,4},{6,7},{7,6},{8,9},{9,8},{10,11... | collective-permute-start | bytes 9437192 | tf_op jit(solution)/shard_map/ppermute | solution.py:519
  188.2 45.7 %collective-permute-start.16 = (bf16[1024,512]{1,0:T(8,128)(2,1)}, bf16[1024,512]{1,0:T(8,128)(2,1)}, u32[]{:S(2)}, u32[]{:S(2)}) collective-permute-start(bf16[1024,512]{1,0:T(8,128)(2,1)} %slice.138.refs_4_.refs_6_), channel_id=1, source_target_pairs={{0,2},{1,3},{2,0},{3,1},{4,6},{5,7},{6,4},{7,5},{8,10},{9,11},{10,... | collective-permute-start | bytes 3145736 | tf_op jit(solution)/shard_map/ppermute | solution.py:519
  212.6 42.5 %collective-permute-start.17 = (bf16[1024,512]{1,0:T(8,128)(2,1)}, bf16[1024,512]{1,0:T(8,128)(2,1)}, u32[]{:S(2)}, u32[]{:S(2)}) collective-permute-start(bf16[1024,512]{1,0:T(8,128)(2,1)} %slice.139.refs_5_.refs_7_), channel_id=1, source_target_pairs={{0,2},{1,3},{2,0},{3,1},{4,6},{5,7},{6,4},{7,5},{8,10},{9,11},{10,... | collective-permute-start | bytes 3145736 | tf_op jit(solution)/shard_map/ppermute | solution.py:519
  214.1 98.0 %collective-permute-start.28 = (bf16[1024,2048]{1,0:T(8,128)(2,1)}, bf16[1024,2048]{1,0:T(8,128)(2,1)S(1)}, u32[]{:S(2)}, u32[]{:S(2)}) collective-permute-start(bf16[1024,2048]{1,0:T(8,128)(2,1)} %all-gather.6.cloned.1.call-done.refs_4_.own), channel_id=1, source_target_pairs={{0,4},{1,5},{2,6},{3,7},{4,0},{5,1},{6,2},{7,3},{8,12},{9,13},{10,... | collective-permute-start | bytes 12582920 | tf_op jit(solution)/shard_map/ppermute | solution.py:519
  215.6 42.0 %collective-permute-start.18 = (bf16[1024,512]{1,0:T(8,128)(2,1)}, bf16[1024,512]{1,0:T(8,128)(2,1)S(1)}, u32[]{:S(2)}, u32[]{:S(2)}) collective-permute-start(bf16[1024,512]{1,0:T(8,128)(2,1)} %slice.138.refs_4_.refs_6_), channel_id=1, source_target_pairs={{0,1},{1,0},{2,3},{3,2},{4,5},{5,4},{6,7},{7,6},{8,9},{9,8},{10,11... | collective-permute-start | bytes 3145736 | tf_op jit(solution)/shard_map/ppermute | solution.py:519
  217.1 58.5 %collective-permute-start.19 = (bf16[1024,512]{1,0:T(8,128)(2,1)}, bf16[1024,512]{1,0:T(8,128)(2,1)}, u32[]{:S(2)}, u32[]{:S(2)}) collective-permute-start(bf16[1024,512]{1,0:T(8,128)(2,1)} %slice.139.refs_5_.refs_7_), channel_id=1, source_target_pairs={{0,1},{1,0},{2,3},{3,2},{4,5},{5,4},{6,7},{7,6},{8,9},{9,8},{10,11... | collective-permute-start | bytes 3145736 | tf_op jit(solution)/shard_map/ppermute | solution.py:519
  350.8 276.9 %reduce-scatter.6.cloned.1.call-start = ((), (), s32[]{:S(2)}) async-start(), calls=%async_computation.7 | async-start | bytes 5242880 | tf_op jit(solution)/shard_map/reduce_scatter | solution.py:534
  410.0 42.0 %collective-permute-start.33 = (bf16[256,2048]{1,0:T(8,128)(2,1)S(1)}, bf16[256,2048]{1,0:T(8,128)(2,1)S(1)}, u32[]{:S(2)}, u32[]{:S(2)}) collective-permute-start(bf16[256,2048]{1,0:T(8,128)(2,1)S(1)} %copy-done.18), channel_id=1, source_target_pairs={{0,4},{1,5},{2,6},{3,7},{4,0},{5,1},{6,2},{7,3},{8,12},{9,13},{10,... | collective-permute-start | bytes 3145736 | tf_op jit(solution)/shard_map/ppermute | solution.py:519
  471.9 50.7 %collective-permute-start.34 = (bf16[512,2048]{1,0:T(8,128)(2,1)}, bf16[512,2048]{1,0:T(8,128)(2,1)}, u32[]{:S(2)}, u32[]{:S(2)}) collective-permute-start(bf16[512,2048]{1,0:T(8,128)(2,1)} %shard_map.556), channel_id=1, source_target_pairs={{0,4},{1,5},{2,6},{3,7},{4,0},{5,1},{6,2},{7,3},{8,12},{9,13},{10,... | collective-permute-start | bytes 6291464 | tf_op jit(solution)/shard_map/ppermute | solution.py:519
  477.0 45.6 %collective-permute-start.46 = (bf16[1024,512]{1,0:T(8,128)(2,1)}, bf16[1024,512]{1,0:T(8,128)(2,1)}, u32[]{:S(2)}, u32[]{:S(2)}) collective-permute-start(bf16[1024,512]{1,0:T(8,128)(2,1)} %get-tuple-element.453), channel_id=1, source_target_pairs={{0,2},{1,3},{2,0},{3,1},{4,6},{5,7},{6,4},{7,5},{8,10},{9,11},{10,... | collective-permute-start | bytes 3145736 | tf_op jit(solution)/shard_map/ppermute | solution.py:519
  527.4 211.5 %reduce-scatter.8.cloned.1.call-start = ((), (), s32[]{:S(2)}) async-start(), calls=%async_computation.8 | async-start | bytes 5242880 | tf_op jit(solution)/shard_map/reduce_scatter | solution.py:534
  527.8 71.1 %collective-permute-start.53 = (bf16[1024,1536]{1,0:T(8,128)(2,1)}, bf16[1024,1536]{1,0:T(8,128)(2,1)S(1)}, u32[]{:S(2)}, u32[]{:S(2)}) collective-permute-start(bf16[1024,1536]{1,0:T(8,128)(2,1)} %shard_map.563), channel_id=1, source_target_pairs={{0,4},{1,5},{2,6},{3,7},{4,0},{5,1},{6,2},{7,3},{8,12},{9,13},{10,... | collective-permute-start | bytes 9437192 | tf_op jit(solution)/shard_map/ppermute | solution.py:519
  529.2 98.5 %collective-permute-start.52 = (bf16[3,256,2048]{2,1,0:T(8,128)(2,1)}, bf16[3,256,2048]{2,1,0:T(8,128)(2,1)}, u32[]{:S(2)}, u32[]{:S(2)}) collective-permute-start(bf16[3,256,2048]{2,1,0:T(8,128)(2,1)} %pad_maximum_fusion.1), channel_id=1, source_target_pairs={{0,2},{1,3},{2,0},{3,1},{4,6},{5,7},{6,4},{7,5},{8,10},{9,11},{10,... | collective-permute-start | bytes 9437192 | tf_op jit(solution)/shard_map/ppermute | solution.py:519
  544.3 77.6 %collective-permute-start.55 = (bf16[1024,512]{1,0:T(8,128)(2,1)}, bf16[1024,512]{1,0:T(8,128)(2,1)S(1)}, u32[]{:S(2)}, u32[]{:S(2)}) collective-permute-start(bf16[1024,512]{1,0:T(8,128)(2,1)} %get-tuple-element.454), channel_id=1, source_target_pairs={{0,2},{1,3},{2,0},{3,1},{4,6},{5,7},{6,4},{7,5},{8,10},{9,11},{10,... | collective-permute-start | bytes 3145736 | tf_op jit(solution)/shard_map/ppermute | solution.py:519
  547.4 74.5 %collective-permute-start.56 = (bf16[1024,512]{1,0:T(8,128)(2,1)S(1)}, bf16[1024,512]{1,0:T(8,128)(2,1)S(1)}, u32[]{:S(2)}, u32[]{:S(2)}) collective-permute-start(bf16[1024,512]{1,0:T(8,128)(2,1)S(1)} %add_convert_fusion.4), channel_id=1, source_target_pairs={{0,4},{1,5},{2,6},{3,7},{4,0},{5,1},{6,2},{7,3},{8,12},{9,13},{10,... | collective-permute-start | bytes 3145736 | tf_op jit(solution)/shard_map/ppermute | solution.py:519
  548.1 79.6 %collective-permute-start.49 = (bf16[256,2048]{1,0:T(8,128)(2,1)}, bf16[256,2048]{1,0:T(8,128)(2,1)}, u32[]{:S(2)}, u32[]{:S(2)}) collective-permute-start(bf16[256,2048]{1,0:T(8,128)(2,1)} %get-tuple-element.231), channel_id=1, source_target_pairs={{0,1},{1,0},{2,3},{3,2},{4,5},{5,4},{6,7},{7,6},{8,9},{9,8},{10,11... | collective-permute-start | bytes 3145736 | tf_op jit(solution)/shard_map/ppermute | solution.py:519
  635.7 157.5 %collective-permute-start.47 = (bf16[256,2048]{1,0:T(8,128)(2,1)}, bf16[256,2048]{1,0:T(8,128)(2,1)}, u32[]{:S(2)}, u32[]{:S(2)}) collective-permute-start(bf16[256,2048]{1,0:T(8,128)(2,1)} %get-tuple-element.223), channel_id=1, source_target_pairs={{0,1},{1,0},{2,3},{3,2},{4,5},{5,4},{6,7},{7,6},{8,9},{9,8},{10,11... | collective-permute-start | bytes 3145736 | tf_op jit(solution)/shard_map/ppermute | solution.py:519
  703.6 89.6 %collective-permute-start.57 = (bf16[256,2048]{1,0:T(8,128)(2,1)}, bf16[256,2048]{1,0:T(8,128)(2,1)}, u32[]{:S(2)}, u32[]{:S(2)}) collective-permute-start(bf16[256,2048]{1,0:T(8,128)(2,1)} %add_convert_fusion.5), channel_id=1, source_target_pairs={{0,2},{1,3},{2,0},{3,1},{4,6},{5,7},{6,4},{7,5},{8,10},{9,11},{10,... | collective-permute-start | bytes 3145736 | tf_op jit(solution)/shard_map/ppermute | solution.py:519
  (133 other events, 1842.4 us)
Sparse Core Ops, SparseCore 0:
  30.1 86.8 all-gather.3
  119.2 79.2 all-gather.5
  200.6 148.1 all-gather.7
  351.1 148.5 reduce-scatter.3
  527.5 80.2 reduce-scatter.5
  627.8 80.7 reduce-scatter.7
